TPU v7x, 128 devices: a whole 4x4x4 slice. The times are simulated.
128 devices in a mesh: ctx: 8 (over x, z_lo), fsdp: 16 (over z_hi, y, core).
Axes of the slice: x: 4, y: 4, z: 4 (z_hi: 2, z_lo: 2; z = z_hi * 2 + z_lo), core: 2. Of those that a mesh axis runs over, the one named last changes fastest.
Arguments:
- tokens: bfloat16 [16, 2048, 768], P('fsdp', 'ctx'), may hold values from -6 to 6
- prev_logits: float32 [16, 2048, 12], P('fsdp', 'ctx'), may hold values from -4 to 4
- routes: int32 [16, 2048, 2], P('fsdp', 'ctx'), may hold values from 0 to 11, all different within a row; in each aligned block of 256 rows (0 to 255, 256 to 511, ..., all dimensions but the last counted through in order) at most 81 rows name the same one
- segments: int32 [16, 2048], P('fsdp', 'ctx'), may hold values from 0 to 5, as said below
- rank_order: int32 [16, 8, 256], P('fsdp', 'ctx'), may hold values from 0 to 255, each once within a row
- norm_first: bfloat16 [768], P(('ctx', 'fsdp')), may hold values from 0.5 to 1.5
- w_query: bfloat16 [768, 768], P(('ctx', 'fsdp')), may hold values from -0.21875 to 0.21875
- w_key: bfloat16 [768, 768], P(('ctx', 'fsdp')), may hold values from -0.21875 to 0.21875
- w_value: bfloat16 [768, 768], P(('ctx', 'fsdp')), may hold values from -0.21875 to 0.21875
- w_output: bfloat16 [768, 768], P(('ctx', 'fsdp')), may hold values from -1.25 to 1.25
- norm_second: bfloat16 [768], P(('ctx', 'fsdp')), may hold values from 0.5 to 1.5
- w_router: bfloat16 [768, 12], P(('ctx', 'fsdp')), may hold values from -0.21875 to 0.21875
- w_residual: float32 [12, 12], replicated, may hold values from -1.75 to 1.75
- w_constant: bfloat16 [768, 4], P(('ctx', 'fsdp')), may hold values from -0.21875 to 0.21875
- v_constant: bfloat16 [768, 2], P(('ctx', 'fsdp')), may hold values from -6 to 6
- w_gate: bfloat16 [16, 768, 1024], P('fsdp', 'ctx'), may hold values from -0.21875 to 0.21875
- w_up: bfloat16 [16, 768, 1024], P('fsdp', 'ctx'), may hold values from -0.21875 to 0.21875
- w_down: bfloat16 [16, 1024, 768], P('fsdp', 'ctx'), may hold values from -0.125 to 0.125
- cotangent: bfloat16 [16, 2048, 768], P('fsdp', 'ctx'), may hold values from -6 to 6
Outputs:
- block_out: bfloat16 [16, 2048, 768], P('fsdp', 'ctx')
- grad_tokens: float32 [16, 2048, 768], P('fsdp', 'ctx')
- grad_prev: float32 [16, 2048, 12], P('fsdp', 'ctx')
- grad_norm_first: float32 [768], P(('ctx', 'fsdp'))
- grad_query: float32 [768, 768], P(('ctx', 'fsdp'))
- grad_key: float32 [768, 768], P(('ctx', 'fsdp'))
- grad_value: float32 [768, 768], P(('ctx', 'fsdp'))
- grad_output: float32 [768, 768], P(('ctx', 'fsdp'))
- grad_norm_second: float32 [768], P(('ctx', 'fsdp'))
- grad_router: float32 [768, 12], P(('ctx', 'fsdp'))
- grad_residual: float32 [12, 12], replicated
- grad_constant: float32 [768, 4], P(('ctx', 'fsdp'))
- grad_vectors: float32 [768, 2], P(('ctx', 'fsdp'))
- grad_gate: float32 [16, 768, 1024], P('fsdp', 'ctx')
- grad_up: float32 [16, 768, 1024], P('fsdp', 'ctx')
- grad_down: float32 [16, 1024, 768], P('fsdp', 'ctx')
Inputs may be any that keep to these rules, and one draw needn't show every extreme that they name: `routes`: each token names two different experts. In each aligned block of 256 rows no expert is named by more than 81 rows, and one is named by exactly that many in some blocks. `segments`: one sequence, which one drawn from the seed, is a single document: all its numbers are 0. In every other sequence the numbers start at 0, never fall, rise by one at each document start and end at 5; each of its documents holds between two thirds and four thirds of 341 positions, the last up to 5 more. `rank_order`: each device's 256 ranks are a permutation.
All inputs are finite; a program needn't handle non-finite values.
Results may differ from a plain program's by a relative error of at most 0.025.
Values may be sent and summed in bfloat16 or wider, within the bound.
A program may use at most 128 MiB of HBM per device.

v0:
```python
import jax
import jax.numpy as jnp
from jax import lax
from jax.sharding import PartitionSpec as P

HEADS = 12
HDIM = 64
EXPERTS = 8
NALL = 12
CAP = 54


highest = lax.Precision.HIGHEST
masked_score = -1e30
epsilon = 1e-06


def rms_forward(values, gain_vec):
    scaling = lax.rsqrt(jnp.mean(values * values, axis=-1, keepdims=True) + epsilon)
    return (values * scaling * gain_vec, scaling)


def rms_backward(values, scaling, gain_vec, gradient):
    weighted = gradient * gain_vec
    inner_mean = jnp.mean(weighted * values, axis=-1, keepdims=True)
    return (
        scaling * weighted - values * scaling**3 * inner_mean,
        jnp.sum(gradient * values * scaling, axis=0),
    )


def rotary_tables(positions, head_dim):
    half_dim = head_dim // 2
    frequency = jnp.exp(
        -jnp.log(10000.0) * jnp.arange(half_dim, dtype=jnp.float32) * 2.0 / head_dim
    )
    phases = positions.astype(jnp.float32)[:, None] * frequency[None, :]
    return (jnp.cos(phases)[:, None, :], jnp.sin(phases)[:, None, :])


def rotate(values, cosine, sine_table):
    half_dim = values.shape[-1] // 2
    lower_half = values[..., :half_dim]
    upper_half = values[..., half_dim:]
    return jnp.concatenate(
        [
            lower_half * cosine - upper_half * sine_table,
            upper_half * cosine + lower_half * sine_table,
        ],
        axis=-1,
    )


def block_scores(queries, keys_blk, query_pos, key_pos, query_seg, key_seg, scaling):
    scores = (
        jnp.einsum("qhd,khd->hqk", queries, keys_blk, preferred_element_type=jnp.float32) * scaling
    )
    allowed = (key_pos[None, :] <= query_pos[:, None]) & (key_seg[None, :] == query_seg[:, None])
    return jnp.where(allowed[None], scores, masked_score)


def on_device(
    tokens,
    prev_logits,
    routes,
    segments,
    rank_order,
    norm_first,
    w_query,
    w_key,
    w_value,
    w_output,
    norm_second,
    w_router,
    w_residual,
    w_constant,
    v_constant,
    w_gate,
    w_up,
    w_down,
    cotangent,
):
    gain_one, gain_two, query_w, key_w, value_w, output_w, router_w, constant_w, constant_v = (
        lax.all_gather(norm_first, ("ctx", "fsdp"), axis=0, tiled=True),
        lax.all_gather(norm_second, ("ctx", "fsdp"), axis=0, tiled=True),
        lax.all_gather(w_query, ("ctx", "fsdp"), axis=0, tiled=True),
        lax.all_gather(w_key, ("ctx", "fsdp"), axis=0, tiled=True),
        lax.all_gather(w_value, ("ctx", "fsdp"), axis=0, tiled=True),
        lax.all_gather(w_output, ("ctx", "fsdp"), axis=0, tiled=True),
        lax.all_gather(w_router, ("ctx", "fsdp"), axis=0, tiled=True),
        lax.all_gather(w_constant, ("ctx", "fsdp"), axis=0, tiled=True),
        lax.all_gather(v_constant, ("ctx", "fsdp"), axis=0, tiled=True),
    )
    gate_full, up_full, down_full = (
        lax.all_gather(w_gate, "ctx", axis=1, tiled=True),
        lax.all_gather(w_up, "ctx", axis=1, tiled=True),
        lax.all_gather(w_down, "ctx", axis=1, tiled=True),
    )
    gate_w = gate_full[0]
    up_w = up_full[0]
    down_w = down_full[0]
    ctx_count = lax.axis_size("ctx")
    halves = lax.axis_size("fsdp") // EXPERTS
    block_len = tokens.shape[1]
    width = HEADS * HDIM
    length = block_len * ctx_count
    scaling = HDIM ** (-0.5)
    first_position = lax.axis_index("ctx") * block_len
    positions = first_position + jnp.arange(block_len, dtype=jnp.int32)
    cosine, sine_table = rotary_tables(positions, HDIM)
    inputs_wide = tokens[0].astype(jnp.float32)
    normed_one, scale_one = rms_forward(inputs_wide, gain_one.astype(jnp.float32))
    normed_one = normed_one.astype(jnp.bfloat16)

    def project(weight):
        return jnp.dot(normed_one, weight, preferred_element_type=jnp.float32).reshape(
            block_len, HEADS, HDIM
        )

    queries = rotate(project(query_w), cosine, sine_table).astype(jnp.bfloat16)
    keys_own = rotate(project(key_w), cosine, sine_table).astype(jnp.bfloat16)
    values_own = project(value_w).astype(jnp.bfloat16)
    query_seg = segments[0]
    keys_all, values_all, seg_all = (
        lax.all_gather(keys_own.reshape(block_len, width), "ctx", axis=0, tiled=True),
        lax.all_gather(values_own.reshape(block_len, width), "ctx", axis=0, tiled=True),
        lax.all_gather(query_seg.astype(jnp.bfloat16), "ctx", axis=0, tiled=True),
    )
    key_block = min(512, length)
    block_count = length // key_block
    key_blocks = keys_all.reshape(block_count, key_block, HEADS, HDIM)
    value_blocks = values_all.reshape(block_count, key_block, HEADS, HDIM)
    seg_blocks = seg_all.astype(jnp.int32).reshape(block_count, key_block)
    key_offsets = jnp.arange(key_block, dtype=jnp.int32)
    needed = (first_position + block_len - 1) // key_block + 1

    def own_scores(index):
        return block_scores(
            queries,
            key_blocks[index],
            positions,
            index * key_block + key_offsets,
            query_seg,
            seg_blocks[index],
            scaling,
        )

    def stats_body(index, running):
        maxima, totals = running
        scores = own_scores(index)
        new_max = jnp.maximum(maxima, jnp.max(scores, axis=-1))
        totals = totals * jnp.exp(maxima - new_max) + jnp.sum(
            jnp.exp(scores - new_max[..., None]), axis=-1
        )
        return (new_max, totals)

    start_stats = (
        jnp.full((HEADS, block_len), masked_score, jnp.float32),
        jnp.zeros((HEADS, block_len), jnp.float32),
    )
    maxima, totals = lax.fori_loop(0, needed, stats_body, start_stats)
    log_total = maxima + jnp.log(totals)

    def output_body(index, running):
        weights = jnp.exp(own_scores(index) - log_total[..., None]).astype(jnp.bfloat16)
        return running + jnp.einsum(
            "hqk,khd->qhd", weights, value_blocks[index], preferred_element_type=jnp.float32
        )

    attended_sum = lax.fori_loop(
        0, needed, output_body, jnp.zeros((block_len, HEADS, HDIM), jnp.float32)
    )
    attended = attended_sum.reshape(block_len, width).astype(jnp.bfloat16)
    residual_state = inputs_wide + jnp.dot(attended, output_w, preferred_element_type=jnp.float32)
    normed_two, scale_two = rms_forward(residual_state, gain_two.astype(jnp.float32))
    normed_two = normed_two.astype(jnp.bfloat16)
    normed_wide = normed_two.astype(jnp.float32)
    prev_rows = prev_logits[0]
    logits = jnp.dot(normed_two, router_w, preferred_element_type=jnp.float32) + jnp.dot(
        prev_rows, w_residual, precision=highest
    )
    route_rows = routes[0]
    onehot = (route_rows[:, :, None] == jnp.arange(NALL, dtype=jnp.int32)[None, None, :]).astype(
        jnp.float32
    )
    chosen = jnp.sum(onehot * logits[:, None, :], axis=-1)
    chosen = jnp.exp(chosen - jnp.max(chosen, axis=1, keepdims=True))
    gate_values = chosen / jnp.sum(chosen, axis=1, keepdims=True)
    rank_rows = rank_order[0, 0]
    earlier = (rank_rows[None, :] < rank_rows[:, None]).astype(jnp.float32)
    slot_table = jnp.dot(earlier, jnp.sum(onehot, axis=1), precision=highest).astype(jnp.int32)
    pair_slot = jnp.sum(slot_table[:, None, :] * onehot.astype(jnp.int32), axis=-1)
    kept_pairs = (route_rows < EXPERTS) & (pair_slot < CAP)
    target = jnp.where(kept_pairs, route_rows * CAP + pair_slot, -1)
    tables = (jnp.arange(EXPERTS * CAP, dtype=jnp.int32)[:, None, None] == target[None]).astype(
        jnp.bfloat16
    )
    tables_split = tables.reshape(EXPERTS, CAP, block_len, 2)
    dispatched = jnp.einsum(
        "jtk,td->jd", tables, normed_two, preferred_element_type=jnp.float32
    ).astype(jnp.bfloat16)
    outgoing = jnp.repeat(dispatched.reshape(EXPERTS, CAP, width), halves, axis=0)
    received = lax.all_to_all(outgoing, "fsdp", split_axis=0, concat_axis=0, tiled=True)
    flat_rows = received.reshape(-1, received.shape[-1])
    gate_proj = jnp.dot(flat_rows, gate_w, preferred_element_type=jnp.float32)
    up_proj = jnp.dot(flat_rows, up_w, preferred_element_type=jnp.float32)
    hidden = (gate_proj * jax.nn.sigmoid(gate_proj) * up_proj).astype(jnp.bfloat16)
    piece_out = (
        jnp.dot(hidden, down_w, preferred_element_type=jnp.float32)
        .astype(jnp.bfloat16)
        .reshape(received.shape)
    )
    returned = lax.all_to_all(piece_out, "fsdp", split_axis=0, concat_axis=0, tiled=True)
    returned, arrived = (returned, received)
    ffn_pairs = jnp.einsum(
        "ectk,ehcd->tkd",
        tables_split,
        returned.reshape(EXPERTS, halves, CAP, width),
        preferred_element_type=jnp.float32,
    )
    mix_weights = jnp.dot(normed_two, constant_w, preferred_element_type=jnp.float32).reshape(
        block_len, 2, 2
    )
    mix_weights = jnp.exp(mix_weights - jnp.max(mix_weights, axis=2, keepdims=True))
    mix_weights = mix_weights / jnp.sum(mix_weights, axis=2, keepdims=True)
    constant_rows = constant_v.astype(jnp.float32).T
    constant_out = (
        mix_weights[:, :, 0:1] * normed_wide[:, None, :]
        + mix_weights[:, :, 1:2] * constant_rows[None]
    )
    is_copy = (route_rows == EXPERTS + 1).astype(jnp.float32)[:, :, None]
    is_first = (route_rows == EXPERTS + 2).astype(jnp.float32)[:, :, None]
    is_second = (route_rows == EXPERTS + 3).astype(jnp.float32)[:, :, None]
    pairs = (
        ffn_pairs
        + is_copy * normed_wide[:, None, :]
        + is_first * constant_out[:, 0:1, :]
        + is_second * constant_out[:, 1:2, :]
    )
    block_output = residual_state + jnp.sum(gate_values[:, :, None] * pairs, axis=1)
    upstream = cotangent[0].astype(jnp.float32)
    gate_grad = jnp.sum(pairs * upstream[:, None, :], axis=-1)
    pair_grad = gate_values[:, :, None] * upstream[:, None, :]
    chosen_grad = gate_values * (
        gate_grad - jnp.sum(gate_values * gate_grad, axis=1, keepdims=True)
    )
    logit_grad = jnp.sum(chosen_grad[:, :, None] * onehot, axis=1)
    normed_grad = jnp.dot(logit_grad, router_w.astype(jnp.float32).T, precision=highest)
    router_grad = jnp.dot(normed_wide.T, logit_grad, precision=highest)
    prev_grad = jnp.dot(logit_grad, w_residual.T, precision=highest)
    residual_grad = jnp.dot(prev_rows.T, logit_grad, precision=highest)
    normed_grad = normed_grad + jnp.sum(is_copy * pair_grad, axis=1)
    const_grad = jnp.stack(
        [jnp.sum(is_first * pair_grad, axis=1), jnp.sum(is_second * pair_grad, axis=1)], axis=1
    )
    mix_grad = jnp.stack(
        [
            jnp.sum(const_grad * normed_wide[:, None, :], axis=-1),
            jnp.sum(const_grad * constant_rows[None], axis=-1),
        ],
        axis=-1,
    )
    mix_grad = mix_weights * (mix_grad - jnp.sum(mix_weights * mix_grad, axis=2, keepdims=True))
    normed_grad = normed_grad + jnp.sum(mix_weights[:, :, 0:1] * const_grad, axis=1)
    vector_grad = jnp.sum(mix_weights[:, :, 1:2] * const_grad, axis=0).T
    mix_flat = mix_grad.reshape(block_len, 4)
    normed_grad = normed_grad + jnp.dot(
        mix_flat, constant_w.astype(jnp.float32).T, precision=highest
    )
    constant_grad = jnp.dot(normed_wide.T, mix_flat, precision=highest)
    slot_grad = jnp.einsum(
        "jtk,tkd->jd", tables, pair_grad.astype(jnp.bfloat16), preferred_element_type=jnp.float32
    ).astype(jnp.bfloat16)
    slot_outgoing = jnp.repeat(slot_grad.reshape(EXPERTS, CAP, width), halves, axis=0)
    arrived_grad = lax.all_to_all(slot_outgoing, "fsdp", split_axis=0, concat_axis=0, tiled=True)
    flat_rows = arrived.reshape(-1, width)
    flat_grad = arrived_grad.reshape(-1, width)
    gate_proj = jnp.dot(flat_rows, gate_w, preferred_element_type=jnp.float32)
    up_proj = jnp.dot(flat_rows, up_w, preferred_element_type=jnp.float32)
    sigmoid_gate = jax.nn.sigmoid(gate_proj)
    activated = gate_proj * sigmoid_gate
    hidden = (activated * up_proj).astype(jnp.bfloat16)
    hidden_grad = jnp.dot(flat_grad, down_w.T, preferred_element_type=jnp.float32)
    down_grad = jnp.dot(hidden.T, flat_grad, preferred_element_type=jnp.float32)
    gate_proj_grad = (
        hidden_grad * up_proj * sigmoid_gate * (1.0 + gate_proj * (1.0 - sigmoid_gate))
    ).astype(jnp.bfloat16)
    up_proj_grad = (hidden_grad * activated).astype(jnp.bfloat16)
    gate_grad_w = jnp.dot(flat_rows.T, gate_proj_grad, preferred_element_type=jnp.float32)
    up_grad_w = jnp.dot(flat_rows.T, up_proj_grad, preferred_element_type=jnp.float32)
    piece_input_grad = (
        (
            jnp.dot(gate_proj_grad, gate_w.T, preferred_element_type=jnp.float32)
            + jnp.dot(up_proj_grad, up_w.T, preferred_element_type=jnp.float32)
        )
        .astype(jnp.bfloat16)
        .reshape(arrived.shape)
    )
    returned_grad = lax.all_to_all(
        piece_input_grad, "fsdp", split_axis=0, concat_axis=0, tiled=True
    )
    normed_grad = normed_grad + jnp.einsum(
        "ectk,ehcd->td",
        tables_split,
        returned_grad.reshape(EXPERTS, halves, CAP, width),
        preferred_element_type=jnp.float32,
    )
    expert_gate_grad, expert_up_grad, expert_down_grad = (
        lax.psum_scatter(
            gate_grad_w[None].astype(jnp.bfloat16), "ctx", scatter_dimension=1, tiled=True
        ).astype(jnp.float32),
        lax.psum_scatter(
            up_grad_w[None].astype(jnp.bfloat16), "ctx", scatter_dimension=1, tiled=True
        ).astype(jnp.float32),
        lax.psum_scatter(
            down_grad[None].astype(jnp.bfloat16), "ctx", scatter_dimension=1, tiled=True
        ).astype(jnp.float32),
    )
    state_grad, gain_two_grad = rms_backward(
        residual_state, scale_two, gain_two.astype(jnp.float32), normed_grad
    )
    state_grad = state_grad + upstream
    state_low = state_grad.astype(jnp.bfloat16)
    output_grad_w = jnp.dot(attended.T, state_low, preferred_element_type=jnp.float32)
    attended_grad = (
        jnp.dot(state_low, output_w.T, preferred_element_type=jnp.float32)
        .reshape(block_len, HEADS, HDIM)
        .astype(jnp.bfloat16)
    )
    row_inner = jnp.sum(attended_sum * attended_grad.astype(jnp.float32), axis=-1).T

    def grad_body(index, running):
        query_acc, key_store, value_store = running
        key_rows = key_blocks[index]
        weights = jnp.exp(own_scores(index) - log_total[..., None])
        weight_grad = jnp.einsum(
            "qhd,khd->hqk", attended_grad, value_blocks[index], preferred_element_type=jnp.float32
        )
        score_grad = (weights * (weight_grad - row_inner[..., None])).astype(jnp.bfloat16)
        query_acc = (
            query_acc
            + jnp.einsum("hqk,khd->qhd", score_grad, key_rows, preferred_element_type=jnp.float32)
            * scaling
        )
        key_part = (
            jnp.einsum("hqk,qhd->khd", score_grad, queries, preferred_element_type=jnp.float32)
            * scaling
        )
        value_part = jnp.einsum(
            "hqk,qhd->khd",
            weights.astype(jnp.bfloat16),
            attended_grad,
            preferred_element_type=jnp.float32,
        )
        key_store = lax.dynamic_update_slice_in_dim(
            key_store, key_part.reshape(key_block, width), index * key_block, 0
        )
        value_store = lax.dynamic_update_slice_in_dim(
            value_store, value_part.reshape(key_block, width), index * key_block, 0
        )
        return (query_acc, key_store, value_store)

    start_grads = (
        jnp.zeros((block_len, HEADS, HDIM), jnp.float32),
        jnp.zeros((length, width), jnp.float32),
        jnp.zeros((length, width), jnp.float32),
    )
    query_grad, key_parts, value_parts = lax.fori_loop(0, needed, grad_body, start_grads)
    key_grad, value_grad = (
        lax.psum_scatter(
            key_parts.astype(jnp.bfloat16), "ctx", scatter_dimension=0, tiled=True
        ).astype(jnp.float32),
        lax.psum_scatter(
            value_parts.astype(jnp.bfloat16), "ctx", scatter_dimension=0, tiled=True
        ).astype(jnp.float32),
    )
    query_low = (
        rotate(query_grad, cosine, -sine_table).reshape(block_len, width).astype(jnp.bfloat16)
    )
    key_low = (
        rotate(key_grad.reshape(block_len, HEADS, HDIM), cosine, -sine_table)
        .reshape(block_len, width)
        .astype(jnp.bfloat16)
    )
    value_low = value_grad.astype(jnp.bfloat16)
    query_grad_w = jnp.dot(normed_one.T, query_low, preferred_element_type=jnp.float32)
    key_grad_w = jnp.dot(normed_one.T, key_low, preferred_element_type=jnp.float32)
    value_grad_w = jnp.dot(normed_one.T, value_low, preferred_element_type=jnp.float32)
    first_grad = (
        jnp.dot(query_low, query_w.T, preferred_element_type=jnp.float32)
        + jnp.dot(key_low, key_w.T, preferred_element_type=jnp.float32)
        + jnp.dot(value_low, value_w.T, preferred_element_type=jnp.float32)
    )
    tokens_grad, gain_one_grad = rms_backward(
        inputs_wide, scale_one, gain_one.astype(jnp.float32), first_grad
    )
    tokens_grad = tokens_grad + state_grad
    (
        sum_gain_one,
        sum_query,
        sum_key,
        sum_value,
        sum_output,
        sum_gain_two,
        sum_router,
        sum_constant,
        sum_vectors,
    ) = (
        lax.psum_scatter(gain_one_grad, ("ctx", "fsdp"), scatter_dimension=0, tiled=True),
        lax.psum_scatter(query_grad_w, ("ctx", "fsdp"), scatter_dimension=0, tiled=True),
        lax.psum_scatter(key_grad_w, ("ctx", "fsdp"), scatter_dimension=0, tiled=True),
        lax.psum_scatter(value_grad_w, ("ctx", "fsdp"), scatter_dimension=0, tiled=True),
        lax.psum_scatter(output_grad_w, ("ctx", "fsdp"), scatter_dimension=0, tiled=True),
        lax.psum_scatter(gain_two_grad, ("ctx", "fsdp"), scatter_dimension=0, tiled=True),
        lax.psum_scatter(router_grad, ("ctx", "fsdp"), scatter_dimension=0, tiled=True),
        lax.psum_scatter(constant_grad, ("ctx", "fsdp"), scatter_dimension=0, tiled=True),
        lax.psum_scatter(vector_grad, ("ctx", "fsdp"), scatter_dimension=0, tiled=True),
    )
    residual_total = lax.psum(residual_grad, ("ctx", "fsdp"))
    return (
        block_output.astype(jnp.bfloat16)[None],
        tokens_grad[None],
        prev_grad[None],
        sum_gain_one,
        sum_query,
        sum_key,
        sum_value,
        sum_output,
        sum_gain_two,
        sum_router,
        residual_total,
        sum_constant,
        sum_vectors,
        expert_gate_grad,
        expert_up_grad,
        expert_down_grad,
    )


def solution(mesh):
    in_specs = (
        P("fsdp", "ctx", None),
        P("fsdp", "ctx", None),
        P("fsdp", "ctx", None),
        P("fsdp", "ctx"),
        P("fsdp", "ctx", None),
        P(("ctx", "fsdp")),
        P(("ctx", "fsdp"), None),
        P(("ctx", "fsdp"), None),
        P(("ctx", "fsdp"), None),
        P(("ctx", "fsdp"), None),
        P(("ctx", "fsdp")),
        P(("ctx", "fsdp"), None),
        P(),
        P(("ctx", "fsdp"), None),
        P(("ctx", "fsdp"), None),
        P("fsdp", "ctx", None),
        P("fsdp", "ctx", None),
        P("fsdp", "ctx", None),
        P("fsdp", "ctx", None),
    )
    out_specs = (
        P("fsdp", "ctx", None),
        P("fsdp", "ctx", None),
        P("fsdp", "ctx", None),
        P(("ctx", "fsdp")),
        P(("ctx", "fsdp"), None),
        P(("ctx", "fsdp"), None),
        P(("ctx", "fsdp"), None),
        P(("ctx", "fsdp"), None),
        P(("ctx", "fsdp")),
        P(("ctx", "fsdp"), None),
        P(),
        P(("ctx", "fsdp"), None),
        P(("ctx", "fsdp"), None),
        P("fsdp", "ctx", None),
        P("fsdp", "ctx", None),
        P("fsdp", "ctx", None),
    )
    return jax.shard_map(
        on_device, mesh=mesh, in_specs=in_specs, out_specs=out_specs, check_vma=False
    )
```

profile of v0, /device:TPU:4, one launch (start us, length us, event | category | flops | bytes accessed | tf_op | source)
XLA Modules:
  0.0 2598.0 jit_solution(2627843766774746024)
XLA Ops:
  11.7 66.6 %all-reduce.16 = (bf16[768]{0:T(1024)(128)(2,1)S(1)}, bf16[768]{0:T(1024)(128)(2,1)S(1)}) all-reduce(bf16[768]{0:T(1024)(128)(2,1)S(1)} %dynamic-update-slice, bf16[768]{0:T(1024)(128)(2,1)S(1)} %dynamic-update-slice.1), channel_id=1, replica_groups=mesh['ctx'=8,'fsdp'=16] {'ctx','fsdp'}, use_global_device_ids=true, to_apply=%add | all-reduce | flops 1536 | bytes 6144
  80.1 124.7 %all-gather.28.cloned.1.call-done = bf16[128,6,768]{2,1,0:T(8,128)(2,1)} async-done(((bf16[1,6,768]{2,1,0:T(8,128)(2,1)}), bf16[128,6,768]{2,1,0:T(8,128)(2,1)}) %all-gather.28.cloned.1.call-update) | async-done | bytes 1179664 | tf_op jit(solution)/shard_map/all_gather | solution.py:88
  210.7 187.8 %all-gather.32.cloned.1.call-done = bf16[128,6,768]{2,1,0:T(8,128)(2,1)} async-done(((bf16[1,6,768]{2,1,0:T(8,128)(2,1)}), bf16[128,6,768]{2,1,0:T(8,128)(2,1)}) %all-gather.32.cloned.1.call-update) | async-done | bytes 1179664 | tf_op jit(solution)/shard_map/all_gather | solution.py:86
  401.9 190.4 %all-gather.30.cloned.1.call-done = bf16[128,6,768]{2,1,0:T(8,128)(2,1)} async-done(((bf16[1,6,768]{2,1,0:T(8,128)(2,1)}), bf16[128,6,768]{2,1,0:T(8,128)(2,1)}) %all-gather.30.cloned.1.call-update) | async-done | bytes 1179664 | tf_op jit(solution)/shard_map/all_gather | solution.py:87
  600.5 14.1 all-gather
  615.9 154.7 %all-gather.5 = bf16[128,6,12]{2,1,0:T(8,128)(2,1)S(1)} all-gather(bf16[1,6,12]{2,1,0:T(8,128)(2,1)S(1)} %bitcast.417), channel_id=1, replica_groups=mesh['ctx'=8,'fsdp'=16] {'ctx','fsdp'}, dimensions={0}, use_global_device_ids=true | all-gather | bytes 18576 | tf_op jit(solution)/shard_map/all_gather | solution.py:90
  771.4 14.4 all-gather.34.cloned.1.call-done
  785.8 3.2 reshape.671
  789.0 73.6 %all-gather.18.cloned.1.call-done = bf16[2048,768]{0,1:T(8,128)(2,1)} async-done(((bf16[256,768]{0,1:T(8,128)(2,1)}), bf16[2048,768]{0,1:T(8,128)(2,1)}) %all-gather.18.cloned.1.call-update) | async-done | bytes 3145744 | tf_op jit(solution)/shard_map/all_gather | solution.py:126
  862.7 4.8 reshape.633
  870.0 71.9 %all-gather.20.cloned.1.call-done = bf16[2048,768]{0,1:T(8,128)(2,1)} async-done(((bf16[256,768]{0,1:T(8,128)(2,1)}), bf16[2048,768]{0,1:T(8,128)(2,1)}) %all-gather.20.cloned.1.call-update) | async-done | bytes 3145744 | tf_op jit(solution)/shard_map/all_gather | solution.py:125
  941.8 6.2 reshape.636
  951.8 16.3 while.39
  970.4 21.7 while.40
  973.2 4.4 fusion.245
  980.5 4.4 fusion.245
  987.7 4.4 fusion.245
  1004.8 7.2 all-to-all-start
  1022.6 12.7 all-to-all-done
  1037.6 5.7 all-to-all-start.2
  1043.9 164.0 %all-gather.6 = bf16[128,6,4]{1,2,0:T(4,128)(2,1)S(1)} all-gather(bf16[1,6,4]{1,2,0:T(4,128)(2,1)} %bitcast.418), channel_id=1, replica_groups=mesh['ctx'=8,'fsdp'=16] {'ctx','fsdp'}, dimensions={0}, use_global_device_ids=true | all-gather | bytes 6192 | tf_op jit(solution)/shard_map/all_gather | solution.py:91
  1210.2 157.0 %all-gather.7 = bf16[128,6,2]{1,2,0:T(2,128)(2,1)} all-gather(bf16[1,6,2]{1,2,0:T(2,128)(2,1)} %bitcast.419), channel_id=1, replica_groups=mesh['ctx'=8,'fsdp'=16] {'ctx','fsdp'}, dimensions={0}, use_global_device_ids=true | all-gather | bytes 3096 | tf_op jit(solution)/shard_map/all_gather | solution.py:92
  1384.2 5.1 fusion.83
  1389.3 5.1 fusion.79
  1394.4 8.6 multiply_convert_fusion.1
  1409.2 4.4 all-to-all-start.1
  1423.1 3.2 fusion.81
  1431.3 3.8 all-to-all-done.1
  1435.1 4.4 all-to-all-start.3
  1441.5 4.6 multiply_reduce_fusion.4
  1451.7 9.3 all-to-all-done.3
  1478.4 56.7 %while.41 = (s32[]{:T(128)}, f32[256,12,64]{0,2,1:T(8,128)}, bf16[2048,768]{0,1:T(8,128)(2,1)}, bf16[2048,768]{0,1:T(8,128)(2,1)}, s32[]{:T(128)}, /*index=5*/bf...) while((s32[]{:T(128)}, f32[256,12,64]{0,2,1:T(8,128)}, ...), condition=%wide.region_33.34_spmd.clone, body=%wide.region_32.33_spmd.clone.sunk | while | flops 1023935232 | bytes 94086600 | solution.py:368
  1478.4 3.6 fusion.256
  1482.9 5.3 fusion.257
  1497.3 3.7 fusion.256
  1501.9 5.3 fusion.257
  1516.2 3.7 fusion.256
  1520.8 5.3 fusion.257
  1536.4 4.5 fusion.85
  1541.0 4.6 fusion.86
  1545.7 4.6 fusion.87
  1553.4 116.2 %reduce-scatter.16.cloned.1.call-done = bf16[256,768]{0,1:T(8,128)(2,1)} async-done(((bf16[2048,768]{0,1:T(8,128)(2,1)}), bf16[256,768]{0,1:T(8,128)(2,1)}) %reduce-scatter.16.cloned.1.call-update) | async-done | bytes 393232 | tf_op jit(solution)/shard_map/reduce_scatter | solution.py:370
  1676.3 67.3 %reduce-scatter.18.cloned.1.call-done = bf16[256,768]{0,1:T(8,128)(2,1)} async-done(((bf16[2048,768]{0,1:T(8,128)(2,1)}), bf16[256,768]{0,1:T(8,128)(2,1)}) %reduce-scatter.18.cloned.1.call-update) | async-done | bytes 393232 | tf_op jit(solution)/shard_map/reduce_scatter | solution.py:373
  1746.7 339.8 %fusion.153 = (f32[8,768]{1,0:T(8,128)S(1)}, f32[8,768]{1,0:T(8,128)S(1)}, f32[8,768]{1,0:T(8,128)}, f32[8,768]{1,0:T(8,128)S(1)}) fusion(f32[768,768]{1,0:T(8,128)} %fusion.126, f32[768,768]{1,0:T(8,128)} %fusion.124, f32[768,768]{1,0:T(8,128)} %fusion.117, f32[768,768]{1,0:T(8,128)} %fusion.131), kind=kCustom, calls=%all-reduce-scatter.4 | all-reduce-scatter fusion | flops 3145729 | bytes 9535488
  2088.8 37.3 %collective-permute-start.63 = (f32[6,768]{1,0:T(8,128)S(1)}, f32[6,768]{1,0:T(8,128)S(1)}, u32[]{:S(2)}, u32[]{:S(2)}) collective-permute-start(f32[6,768]{1,0:T(8,128)S(1)} %slice.61), channel_id=1, source_target_pairs={{0,32},{1,33},{2,34},{3,35},{4,36},{5,37},{6,38},{7,39},{8,40},{9,... | collective-permute-start | bytes 55304
  2126.8 10.2 collective-permute-start.95
  2137.0 7.3 collective-permute-start.30
  2152.9 5.4 collective-permute-done.127
  2176.1 3.1 collective-permute-start.17
  2184.1 3.6 collective-permute-start.14
  2202.6 3.7 collective-permute-start.6
  2211.4 3.7 collective-permute-start.3
  2276.4 3.4 collective-permute-start.38
  2284.9 3.7 collective-permute-start.35
  2365.7 3.7 collective-permute-start.67
  2380.1 80.9 %all-reduce.15 = (f32[768]{0:T(1024)S(1)}, f32[768]{0:T(1024)S(1)}, f32[768,12]{1,0:T(8,128)S(1)}, f32[12,12]{0,1:T(8,128)S(1)}, f32[768,4]{0,1:T(4,128)S(1)}, /*index=5*/f32[768,2]{0,1:T(2,128)S(1)}) all-reduce(f32[768]{0:T(1024)S(1)} %get-tuple-element.539, ...), channel_id=5, replica_groups=mesh['ctx'=8,'fsdp'=16] {'ctx','fsdp'}, use_global_device_ids=true, to_apply=%region_38.39.clone | all-reduce | flops 15504 | bytes 124032
  2461.0 3.8 collective-permute-start.125
  2464.9 5.2 collective-permute-start.124
  2500.4 4.9 concatenate.18
  2505.3 5.3 collective-permute-start.110
  2519.5 24.2 concatenate.19
  2555.7 11.6 concatenate.20
  2569.8 3.7 collective-permute-start.99
  2587.3 3.4 concatenate.21
  (879 shorter events, 466.3 us)
Async XLA Ops:
  7.2 197.7 %all-gather.28.cloned.1.call-start = ((), (), s32[]{:S(2)}) async-start(), calls=%async_computation.19 | async-start | bytes 1585152 | tf_op jit(solution)/shard_map/all_gather | solution.py:88
  7.9 390.6 %all-gather.32.cloned.1.call-start = ((), (), s32[]{:S(2)}) async-start(), calls=%async_computation.21 | async-start | bytes 1585152 | tf_op jit(solution)/shard_map/all_gather | solution.py:86
  8.7 583.6 %all-gather.30.cloned.1.call-start = ((), (), s32[]{:S(2)}) async-start(), calls=%async_computation.20 | async-start | bytes 1585152 | tf_op jit(solution)/shard_map/all_gather | solution.py:87
  9.4 776.4 %all-gather.34.cloned.1.call-start = ((), (), s32[]{:S(2)}) async-start(), calls=%async_computation.22 | async-start | bytes 1585152 | tf_op jit(solution)/shard_map/all_gather | solution.py:89
  10.0 852.7 %all-gather.18.cloned.1.call-start = ((), (), s32[]{:S(2)}) async-start(), calls=%async_computation.9 | async-start | bytes 3538944 | tf_op jit(solution)/shard_map/all_gather | solution.py:126
  209.8 732.0 %all-gather.20.cloned.1.call-start = ((), (), s32[]{:S(2)}) async-start(), calls=%async_computation.10 | async-start | bytes 3538944 | tf_op jit(solution)/shard_map/all_gather | solution.py:125
  599.0 785.2 %all-gather.22.cloned.1.call-start = ((), (), s32[]{:S(2)}) async-start(), calls=%async_computation.11 | async-start | bytes 1769472 | tf_op jit(solution)/shard_map/all_gather | solution.py:95
  599.8 789.5 %all-gather.24.cloned.1.call-start = ((), (), s32[]{:S(2)}) async-start(), calls=%async_computation.12 | async-start | bytes 1769472 | tf_op jit(solution)/shard_map/all_gather | solution.py:96
  1004.8 30.5 %all-to-all-start = ((bf16[16,54,768]{2,1,0:T(8,128)(2,1)}), bf16[16,54,768]{2,1,0:T(8,128)(2,1)}, u32[]{:S(2)}, u32[]{:S(2)}) async-start(bf16[16,54,768]{2,1,0:T(8,128)(2,1)} %bitcast.381), calls=%async_computation | async-start | bytes 2752512 | tf_op jit(solution)/shard_map/all_to_all | solution.py:203
  1012.0 382.4 %all-gather.26.cloned.1.call-start = ((), (), s32[]{:S(2)}) async-start(), calls=%async_computation.13 | async-start | bytes 1769472 | tf_op jit(solution)/shard_map/all_gather | solution.py:97
  1037.6 344.2 %all-to-all-start.2 = ((bf16[16,54,768]{2,1,0:T(8,128)(2,1)}), bf16[16,54,768]{2,1,0:T(8,128)(2,1)}, u32[]{:S(2)}, u32[]{:S(2)}) async-start(bf16[16,54,768]{2,1,0:T(8,128)(2,1)} %bitcast.380), calls=%async_computation.2 | async-start | bytes 2752512 | tf_op jit(solution)/shard_map/all_to_all | solution.py:275
  1409.2 25.9 all-to-all-start.1
  1435.1 25.9 all-to-all-start.3
  1439.5 230.1 %reduce-scatter.16.cloned.1.call-start = ((), (), s32[]{:S(2)}) async-start(), calls=%async_computation.14 | async-start | bytes 3538944 | tf_op jit(solution)/shard_map/reduce_scatter | solution.py:370
  1535.1 208.5 %reduce-scatter.18.cloned.1.call-start = ((), (), s32[]{:S(2)}) async-start(), calls=%async_computation.15 | async-start | bytes 3538944 | tf_op jit(solution)/shard_map/reduce_scatter | solution.py:373
  1535.8 777.5 %reduce-scatter.20.cloned.1.call-start = ((), (), s32[]{:S(2)}) async-start(), calls=%async_computation.16 | async-start | bytes 1769472 | tf_op jit(solution)/shard_map/reduce_scatter | solution.py:309
  1541.0 774.4 %reduce-scatter.22.cloned.1.call-start = ((), (), s32[]{:S(2)}) async-start(), calls=%async_computation.17 | async-start | bytes 1769472 | tf_op jit(solution)/shard_map/reduce_scatter | solution.py:312
  1545.6 771.6 %reduce-scatter.24.cloned.1.call-start = ((), (), s32[]{:S(2)}) async-start(), calls=%async_computation.18 | async-start | bytes 1769472 | tf_op jit(solution)/shard_map/reduce_scatter | solution.py:315
  2086.5 60.5 %collective-permute-start.31 = (f32[6,768]{1,0:T(8,128)S(1)}, f32[6,768]{1,0:T(8,128)S(1)}, u32[]{:S(2)}, u32[]{:S(2)}) collective-permute-start(f32[6,768]{1,0:T(8,128)S(1)} %slice.60), channel_id=1, source_target_pairs={{0,32},{1,33},{2,34},{3,35},{4,36},{5,37},{6,38},{7,39},{8,40},{9,... | collective-permute-start | bytes 55304
  2088.8 60.2 %collective-permute-start.63 = (f32[6,768]{1,0:T(8,128)S(1)}, f32[6,768]{1,0:T(8,128)S(1)}, u32[]{:S(2)}, u32[]{:S(2)}) collective-permute-start(f32[6,768]{1,0:T(8,128)S(1)} %slice.61), channel_id=1, source_target_pairs={{0,32},{1,33},{2,34},{3,35},{4,36},{5,37},{6,38},{7,39},{8,40},{9,... | collective-permute-start | bytes 55304
  2126.8 24.1 collective-permute-start.95
  2137.0 23.2 collective-permute-start.30
  2144.4 17.8 collective-permute-start.29
  2147.1 17.1 collective-permute-start.28
  2149.0 17.1 collective-permute-start.27
  2174.2 13.5 collective-permute-start.18
  2176.1 13.8 collective-permute-start.17
  2200.7 14.5 collective-permute-start.7
  2202.6 14.5 collective-permute-start.6
  2266.4 13.5 collective-permute-start.42
  2268.3 14.0 collective-permute-start.41
  2270.8 14.1 collective-permute-start.40
  2274.5 15.0 collective-permute-start.39
  2276.4 15.0 collective-permute-start.38
  2279.8 13.8 collective-permute-start.37
  2282.3 13.9 collective-permute-start.36
  2300.9 18.0 collective-permute-start.92
  2302.8 18.0 collective-permute-start.91
  2304.7 18.0 collective-permute-start.90
  2308.7 16.1 collective-permute-start.89
  2310.6 16.0 collective-permute-start.88
  2365.7 95.2 %collective-permute-start.67 = (f32[8,768]{1,0:T(8,128)}, f32[8,768]{1,0:T(8,128)S(1)}, u32[]{:S(2)}, u32[]{:S(2)}) collective-permute-start(f32[8,768]{1,0:T(8,128)} %get-tuple-element.626), channel_id=1, source_target_pairs={{0,4},{1,5},{2,6},{3,7},{4,8},{5,9},{6,10},{7,11},{8,12},{9,13},{1... | collective-permute-start | bytes 73736
  2369.5 95.4 %collective-permute-start.66 = (f32[8,768]{1,0:T(8,128)}, f32[8,768]{1,0:T(8,128)S(1)}, u32[]{:S(2)}, u32[]{:S(2)}) collective-permute-start(f32[8,768]{1,0:T(8,128)} %get-tuple-element.626), channel_id=1, source_target_pairs={{0,3},{1,4},{2,5},{3,6},{4,7},{5,8},{6,9},{7,10},{8,11},{9,12},{10... | collective-permute-start | bytes 73736
  2371.4 98.7 %collective-permute-start.65 = (f32[8,768]{1,0:T(8,128)}, f32[8,768]{1,0:T(8,128)S(1)}, u32[]{:S(2)}, u32[]{:S(2)}) collective-permute-start(f32[8,768]{1,0:T(8,128)} %get-tuple-element.626), channel_id=1, source_target_pairs={{0,2},{1,3},{2,4},{3,5},{4,6},{5,7},{6,8},{7,9},{8,10},{9,11},{10,... | collective-permute-start | bytes 73736
  2373.6 98.5 %collective-permute-start.64 = (f32[8,768]{1,0:T(8,128)}, f32[8,768]{1,0:T(8,128)S(1)}, u32[]{:S(2)}, u32[]{:S(2)}) collective-permute-start(f32[8,768]{1,0:T(8,128)} %get-tuple-element.626), channel_id=1, source_target_pairs={{0,1},{1,2},{2,3},{3,4},{4,5},{5,6},{6,7},{7,8},{8,9},{9,10},{10,1... | collective-permute-start | bytes 73736
  2376.2 97.8 %collective-permute-start.126 = (f32[8,768]{1,0:T(8,128)S(1)}, f32[8,768]{1,0:T(8,128)S(1)}, u32[]{:S(2)}, u32[]{:S(2)}) collective-permute-start(f32[8,768]{1,0:T(8,128)S(1)} %copy-done.47), channel_id=1, source_target_pairs={{0,31},{1,32},{2,33},{3,34},{4,35},{5,36},{6,37},{7,38},{8,39},{9,... | collective-permute-start | bytes 73736
  2461.0 16.0 collective-permute-start.125
  2464.9 14.1 collective-permute-start.124
  2487.4 17.9 collective-permute-start.115
  2489.3 21.2 collective-permute-start.114
  2491.3 21.5 collective-permute-start.113
  2493.2 21.5 collective-permute-start.112
  2495.2 21.8 collective-permute-start.111
  2505.3 38.5 %collective-permute-start.110 = (f32[8,768]{1,0:T(8,128)S(1)}, f32[8,768]{1,0:T(8,128)S(1)}, u32[]{:S(2)}, u32[]{:S(2)}) collective-permute-start(f32[8,768]{1,0:T(8,128)S(1)} %copy-done.47), channel_id=1, source_target_pairs={{0,15},{1,16},{2,17},{3,18},{4,19},{5,20},{6,21},{7,22},{8,23},{9,... | collective-permute-start | bytes 73736
  2510.6 35.1 %collective-permute-start.109 = (f32[8,768]{1,0:T(8,128)S(1)}, f32[8,768]{1,0:T(8,128)S(1)}, u32[]{:S(2)}, u32[]{:S(2)}) collective-permute-start(f32[8,768]{1,0:T(8,128)S(1)} %copy-done.47), channel_id=1, source_target_pairs={{0,14},{1,15},{2,16},{3,17},{4,18},{5,19},{6,20},{7,21},{8,22},{9,... | collective-permute-start | bytes 73736
  2512.8 35.1 %collective-permute-start.108 = (f32[8,768]{1,0:T(8,128)S(1)}, f32[8,768]{1,0:T(8,128)S(1)}, u32[]{:S(2)}, u32[]{:S(2)}) collective-permute-start(f32[8,768]{1,0:T(8,128)S(1)} %copy-done.47), channel_id=1, source_target_pairs={{0,13},{1,14},{2,15},{3,16},{4,17},{5,18},{6,19},{7,20},{8,21},{9,... | collective-permute-start | bytes 73736
  2514.7 35.4 %collective-permute-start.107 = (f32[8,768]{1,0:T(8,128)S(1)}, f32[8,768]{1,0:T(8,128)S(1)}, u32[]{:S(2)}, u32[]{:S(2)}) collective-permute-start(f32[8,768]{1,0:T(8,128)S(1)} %copy-done.47), channel_id=1, source_target_pairs={{0,12},{1,13},{2,14},{3,15},{4,16},{5,17},{6,18},{7,19},{8,20},{9,... | collective-permute-start | bytes 73736
  2517.0 35.4 %collective-permute-start.106 = (f32[8,768]{1,0:T(8,128)S(1)}, f32[8,768]{1,0:T(8,128)S(1)}, u32[]{:S(2)}, u32[]{:S(2)}) collective-permute-start(f32[8,768]{1,0:T(8,128)S(1)} %copy-done.47), channel_id=1, source_target_pairs={{0,11},{1,12},{2,13},{3,14},{4,15},{5,16},{6,17},{7,18},{8,19},{9,... | collective-permute-start | bytes 73736
  2543.8 23.5 collective-permute-start.105
  2545.7 24.1 collective-permute-start.104
  2547.9 25.6 collective-permute-start.103
  2550.1 25.3 collective-permute-start.102
  2552.3 25.3 collective-permute-start.101
  2567.3 13.6 collective-permute-start.100
  (284 other events, 16789.3 us)
Sparse Core Ops, SparseCore 0:
  9.8 195.0 all-gather.27
  206.6 191.9 all-gather.31
  400.3 191.9 all-gather.29
  593.8 191.9 all-gather.33
  787.8 74.8 all-gather.17
  864.7 77.0 all-gather.19
  943.5 43.7 all-gather.21
  988.9 79.8 all-gather.23
  1070.4 44.5 all-gather.25
  1535.2 134.3 reduce-scatter.15
  1672.0 71.5 reduce-scatter.17
  1745.9 49.7 reduce-scatter.19
  1798.1 51.1 reduce-scatter.21
  1851.6 50.4 reduce-scatter.23
where the time goes:
time: 2630 us; the launch traced here: 2600 us
  blocking collectives  977 us (37%)
  waiting for transfers between devices  896 us (34%)
  starting transfers between devices  359 us (14%)
  local copies, waits for them, and re-layouts  153 us (6%)
  matrix products  138 us (5%)
  other arithmetic  55.4 us (2%)
    unnamed x3, blocking collectives  487 us
    unnamed x128, starting transfers between devices  336 us
    all_gather x1, waiting for transfers between devices, on_device(): lax.all_gather(w_key, ('ctx', 'fsdp'), axis=0, tiled=True)  190 us
    all_gather x1, waiting for transfers between devices, on_device(): lax.all_gather(w_query, ('ctx', 'fsdp'), axis=0, tiled=True)  188 us
    all_gather x1, blocking collectives, on_device(): lax.all_gather(w_constant, ('ctx', 'fsdp'), axis=0, tiled=True)  164 us
    all_gather x1, blocking collectives, on_device(): lax.all_gather(v_constant, ('ctx', 'fsdp'), axis=0, tiled=True)  157 us
    all_gather x1, blocking collectives, on_device(): lax.all_gather(w_router, ('ctx', 'fsdp'), axis=0, tiled=True)  155 us
    all_gather x1, waiting for transfers between devices, on_device(): lax.all_gather(w_value, ('ctx', 'fsdp'), axis=0, tiled=True)  125 us
  transfers between devices with their start and end apart: 146, of which 21 were waited for; matrix products, arithmetic and copies ran while one was open for 23% of the time, Pallas kernels for 0%

commit v1 on v0

--- a/solution.py
+++ b/solution.py
@@ -1,6 +1,11 @@
+import functools
+
 import jax
 import jax.numpy as jnp
+import numpy as np
 from jax import lax
+from jax.experimental import pallas as pl
+from jax.experimental.pallas import tpu as pltpu
 from jax.sharding import PartitionSpec as P
 
 HEADS = 12
@@ -8,6 +13,446 @@
 EXPERTS = 8
 NALL = 12
 CAP = 54
+WIDTH = HEADS * HDIM
+
+MESH = pl.DeviceIdType.MESH
+PART_LANES = (512, 384, 384)
+PART_START = (0, 512, 896)
+PART_ORDER = ((0, 1, 2), (1, 2, 0), (2, 0, 1))
+
+
+def place():
+    ctx = lax.axis_index("ctx")
+    fsdp = lax.axis_index("fsdp")
+    return ctx // 2, (ctx % 2) * 2 + fsdp // 8, (fsdp // 2) % 4, fsdp % 2
+
+
+def device_at(x, z, y, core):
+    return {"ctx": x * 2 + z // 2, "fsdp": (z % 2) * 8 + y * 2 + core}
+
+
+def shifted(spot, axis, by):
+    moved = list(spot)
+    moved[axis] = (moved[axis] + by) % 4
+    return tuple(moved)
+
+
+def greet(devices):
+    barrier = pltpu.get_barrier_semaphore()
+    for device in devices:
+        pl.semaphore_signal(barrier, inc=1, device_id=device, device_id_type=MESH)
+    pl.semaphore_wait(barrier, len(devices))
+
+
+def torus_peers(spot, core):
+    peers = [device_at(*shifted(spot, axis, by), core) for axis in range(3) for by in (1, 2, 3)]
+    return peers + [device_at(*spot, 1 - core)]
+
+
+def region(ref, spot, core, whole):
+    return ref.at[
+        tuple(slice(None) if axis in whole else spot[axis] for axis in range(3)) + (core,)
+    ]
+
+
+def gather_kernel(own_ref, *refs):
+    parts = refs[:3]
+    net_send, net_recv, twin_send, twin_recv, own_sem = refs[3:]
+    *spot, core = place()
+    spot = tuple(spot)
+    twin = device_at(*spot, 1 - core)
+    greet(torus_peers(spot, core))
+
+    def net(part, step, by, source, target):
+        axis = PART_ORDER[part][step]
+        return pltpu.make_async_remote_copy(
+            src_ref=source,
+            dst_ref=target,
+            send_sem=net_send.at[part, step, by - 1],
+            recv_sem=net_recv.at[part, step, by - 1],
+            device_id=device_at(*shifted(spot, axis, by), core),
+            device_id_type=MESH,
+        )
+
+    def share(part, slot, source, target):
+        return pltpu.make_async_remote_copy(
+            src_ref=source,
+            dst_ref=target,
+            send_sem=twin_send.at[part, slot],
+            recv_sem=twin_recv.at[part, slot],
+            device_id=twin,
+            device_id_type=MESH,
+        )
+
+    started = []
+    kept = []
+    for part in range(3):
+        own = own_ref.at[:, pl.ds(PART_START[part], PART_LANES[part])]
+        mine = region(parts[part], spot, core, ())
+        for by in (1, 2, 3):
+            copy = net(part, 0, by, own, mine)
+            copy.start()
+            started.append(copy)
+    for part in range(3):
+        own = own_ref.at[:, pl.ds(PART_START[part], PART_LANES[part])]
+        mine = region(parts[part], spot, core, ())
+        copy = pltpu.make_async_copy(own, mine, own_sem.at[part])
+        copy.start()
+        kept.append(copy)
+        copy = share(part, 0, own, mine)
+        copy.start()
+        started.append(copy)
+    for copy in kept:
+        copy.wait()
+    for step in range(3):
+        for part in range(3):
+            order = PART_ORDER[part]
+            axis = order[step]
+            whole = order[:step]
+            for by in (1, 2, 3):
+                came = region(parts[part], shifted(spot, axis, -by), core, whole)
+                net(part, step, by, came, came).wait_recv()
+                copy = share(part, 1 + step * 3 + by - 1, came, came)
+                copy.start()
+                started.append(copy)
+            if step < 2:
+                held = region(parts[part], spot, core, order[: step + 1])
+                for by in (1, 2, 3):
+                    copy = net(part, step + 1, by, held, held)
+                    copy.start()
+                    started.append(copy)
+    for part in range(3):
+        order = PART_ORDER[part]
+        first = region(parts[part], spot, 1 - core, ())
+        share(part, 0, first, first).wait_recv()
+        for step in range(3):
+            for by in (1, 2, 3):
+                came = region(
+                    parts[part], shifted(spot, order[step], -by), 1 - core, order[:step]
+                )
+                share(part, 1 + step * 3 + by - 1, came, came).wait_recv()
+    for copy in started:
+        copy.wait_send()
+
+
+def gather_shards(own):
+    return pl.pallas_call(
+        gather_kernel,
+        out_shape=[
+            jax.ShapeDtypeStruct((4, 4, 4, 2, 16, lanes), jnp.bfloat16) for lanes in PART_LANES
+        ],
+        in_specs=[pl.BlockSpec(memory_space=pltpu.VMEM)],
+        out_specs=[pl.BlockSpec(memory_space=pl.ANY)] * 3,
+        scratch_shapes=[
+            pltpu.SemaphoreType.DMA((3, 3, 3)),
+            pltpu.SemaphoreType.DMA((3, 3, 3)),
+            pltpu.SemaphoreType.DMA((3, 10)),
+            pltpu.SemaphoreType.DMA((3, 10)),
+            pltpu.SemaphoreType.DMA((3,)),
+        ],
+        name="gather_shards",
+        compiler_params=pltpu.CompilerParams(collective_id=1, has_side_effects=True),
+    )(own)
+
+
+def scatter_kernel(grads_ref, small_ref, out_ref, total_ref, *refs):
+    twin_in, held = refs[0:3], refs[3:6]
+    in_one, in_two, in_three = refs[6:9], refs[9:12], refs[12:15]
+    sum_one, sum_two = refs[15:18], refs[18:21]
+    small_in, small_sum, net_send, net_recv, twin_send, twin_recv, small_send, small_recv = refs[21:]
+    *spot, core = place()
+    spot = tuple(spot)
+    twin = device_at(*spot, 1 - core)
+    greet(torus_peers(spot, core))
+    started = []
+
+    def net(part, step, by, source, target):
+        axis = PART_ORDER[part][2 - step]
+        return pltpu.make_async_remote_copy(
+            src_ref=source,
+            dst_ref=target,
+            send_sem=net_send.at[part, step, by - 1],
+            recv_sem=net_recv.at[part, step, by - 1],
+            device_id=device_at(*shifted(spot, axis, by), core),
+            device_id_type=MESH,
+        )
+
+    def share(part):
+        lanes = pl.ds(PART_START[part], PART_LANES[part])
+        return pltpu.make_async_remote_copy(
+            src_ref=grads_ref.at[:, :, :, 1 - core, :, lanes],
+            dst_ref=twin_in[part],
+            send_sem=twin_send.at[part],
+            recv_sem=twin_recv.at[part],
+            device_id=twin,
+            device_id_type=MESH,
+        )
+
+    def small(axis, by, source, slot):
+        device = twin if axis == 3 else device_at(*shifted(spot, axis, by), core)
+        return pltpu.make_async_remote_copy(
+            src_ref=source,
+            dst_ref=small_in.at[axis, slot],
+            send_sem=small_send.at[axis, by - 1],
+            recv_sem=small_recv.at[axis, by - 1],
+            device_id=device,
+            device_id_type=MESH,
+        )
+
+    for part in range(3):
+        copy = share(part)
+        copy.start()
+        started.append(copy)
+    copy = small(3, 1, small_ref, core)
+    copy.start()
+    started.append(copy)
+
+    def add_pairs(part):
+        start, lanes = PART_START[part], PART_LANES[part]
+
+        def step(index, carry):
+            x, z, y = index // 16, (index // 4) % 4, index % 4
+            held[part][x, z, y] = (
+                grads_ref[x, z, y, core, :, start : start + lanes].astype(jnp.float32)
+                + twin_in[part][x, z, y].astype(jnp.float32)
+            ).astype(jnp.bfloat16)
+            return carry
+
+        lax.fori_loop(0, 64, step, 0, unroll=2)
+
+    def cut(spots, axis, at):
+        return tuple(at if a == axis else slice(None) for a in spots)
+
+    for part in range(3):
+        share(part).wait_recv()
+        add_pairs(part)
+        axis = PART_ORDER[part][2]
+        for by in (1, 2, 3):
+            index = cut((0, 1, 2), axis, shifted(spot, axis, by)[axis])
+            copy = net(part, 0, by, held[part].at[index], in_one[part].at[by - 1])
+            copy.start()
+            started.append(copy)
+
+    small(3, 1, small_ref, 1 - core).wait_recv()
+    small_in[3, core] = small_ref[...]
+    small_sum[0] = small_in[3, 0] + small_in[3, 1]
+    for by in (1, 2, 3):
+        copy = small(0, by, small_sum.at[0], spot[0])
+        copy.start()
+        started.append(copy)
+
+    def small_step(axis):
+        for by in (1, 2, 3):
+            small(axis, by, small_sum.at[axis], shifted(spot, axis, -by)[axis]).wait_recv()
+        small_in[axis, spot[axis]] = small_sum[axis]
+        total = small_in[axis, 0] + small_in[axis, 1] + small_in[axis, 2] + small_in[axis, 3]
+        if axis == 2:
+            total_ref[...] = total
+            return
+        small_sum[axis + 1] = total
+        for by in (1, 2, 3):
+            copy = small(axis + 1, by, small_sum.at[axis + 1], spot[axis + 1])
+            copy.start()
+            started.append(copy)
+
+    for part in range(3):
+        first, second, third = PART_ORDER[part]
+        for by in (1, 2, 3):
+            net(part, 0, by, in_one[part].at[by - 1], in_one[part].at[by - 1]).wait_recv()
+        rest = tuple(a for a in (0, 1, 2) if a != third)
+
+        def add_four(index, carry, part=part, third=third, rest=rest):
+            at = {rest[0]: index // 4, rest[1]: index % 4, third: spot[third]}
+            total = held[part][at[0], at[1], at[2]].astype(jnp.float32)
+            for by in range(3):
+                total = total + in_one[part][by, index // 4, index % 4].astype(jnp.float32)
+            sum_one[part][index // 4, index % 4] = total.astype(jnp.bfloat16)
+            return carry
+
+        lax.fori_loop(0, 16, add_four, 0, unroll=2)
+        for by in (1, 2, 3):
+            at = shifted(spot, second, by)[second]
+            source = sum_one[part].at[at] if second == rest[0] else sum_one[part].at[:, at]
+            copy = net(part, 1, by, source, in_two[part].at[by - 1])
+            copy.start()
+            started.append(copy)
+    small_step(0)
+    for part in range(3):
+        first, second, third = PART_ORDER[part]
+        for by in (1, 2, 3):
+            net(part, 1, by, in_two[part].at[by - 1], in_two[part].at[by - 1]).wait_recv()
+        rest = tuple(a for a in (0, 1, 2) if a != third)
+        for index in range(4):
+            if second == rest[0]:
+                total = sum_one[part][spot[second], index].astype(jnp.float32)
+            else:
+                total = sum_one[part][index, spot[second]].astype(jnp.float32)
+            for by in range(3):
+                total = total + in_two[part][by, index].astype(jnp.float32)
+            sum_two[part][index] = total.astype(jnp.bfloat16)
+        for by in (1, 2, 3):
+            at = shifted(spot, first, by)[first]
+            copy = net(part, 2, by, sum_two[part].at[at], in_three[part].at[by - 1])
+            copy.start()
+            started.append(copy)
+    small_step(1)
+    for part in range(3):
+        first = PART_ORDER[part][0]
+        for by in (1, 2, 3):
+            net(part, 2, by, in_three[part].at[by - 1], in_three[part].at[by - 1]).wait_recv()
+        total = sum_two[part][spot[first]].astype(jnp.float32)
+        for by in range(3):
+            total = total + in_three[part][by].astype(jnp.float32)
+        out_ref[:, PART_START[part] : PART_START[part] + PART_LANES[part]] = total
+    small_step(2)
+    for copy in started:
+        copy.wait_send()
+
+
+def scatter_shards(grads, small):
+    by_part = lambda *lead: [pltpu.VMEM((*lead, 16, lanes), jnp.bfloat16) for lanes in PART_LANES]
+    return pl.pallas_call(
+        scatter_kernel,
+        out_shape=[
+            jax.ShapeDtypeStruct((16, 1280), jnp.float32),
+            jax.ShapeDtypeStruct((16, 128), jnp.float32),
+        ],
+        in_specs=[pl.BlockSpec(memory_space=pltpu.VMEM)] * 2,
+        out_specs=[pl.BlockSpec(memory_space=pltpu.VMEM)] * 2,
+        scratch_shapes=[
+            *by_part(4, 4, 4),
+            *by_part(4, 4, 4),
+            *by_part(3, 4, 4),
+            *by_part(3, 4),
+            *by_part(3),
+            *by_part(4, 4),
+            *by_part(4),
+            pltpu.VMEM((4, 4, 16, 128), jnp.float32),
+            pltpu.VMEM((3, 16, 128), jnp.float32),
+            pltpu.SemaphoreType.DMA((3, 3, 3)),
+            pltpu.SemaphoreType.DMA((3, 3, 3)),
+            pltpu.SemaphoreType.DMA((3,)),
+            pltpu.SemaphoreType.DMA((3,)),
+            pltpu.SemaphoreType.DMA((4, 3)),
+            pltpu.SemaphoreType.DMA((4, 3)),
+        ],
+        name="scatter_shards",
+        compiler_params=pltpu.CompilerParams(
+            collective_id=2, has_side_effects=True, vmem_limit_bytes=40 * 2**20
+        ),
+    )(grads, small)
+
+
+def placing_tables():
+    left = np.zeros((192, 256), np.float32)
+    right = np.zeros((192, 256), np.float32)
+    small = np.zeros((48, 128), np.float32)
+    for device in range(8):
+        for weight in range(4):
+            for row in range(6):
+                at, line = weight * 48 + device * 6 + row, weight * 6 + row
+                if line < 16:
+                    left[at, device * 16 + line] = right[at, device * 16 + line] = 1
+                else:
+                    left[at, 128 + device * 16 + line - 16] = 1
+                    right[at, 128 + device * 16 + line - 8] = 1
+        for row in range(6):
+            small[device * 6 + row, device * 16 + row] = 1
+    return left, right, small
+
+
+def unpack_kernel(a_ref, b_ref, c_ref, left_ref, right_ref, small_ref, weights_ref, smalls_ref):
+    a, b, c = a_ref[0], b_ref[0], c_ref[0]
+    tail = jnp.concatenate([b[:, 256:], c[:, :256]], axis=1)
+    left = jnp.dot(
+        left_ref[...],
+        jnp.concatenate([a[:, :384], tail], axis=0),
+        preferred_element_type=jnp.float32,
+    )
+    right = jnp.dot(
+        right_ref[...],
+        jnp.concatenate([jnp.concatenate([a[:, 384:], b[:, :256]], axis=1), tail], axis=0),
+        preferred_element_type=jnp.float32,
+    )
+    for weight in range(4):
+        rows = slice(weight * 48, weight * 48 + 48)
+        weights_ref[weight, :, :384] = left[rows].astype(jnp.bfloat16)
+        weights_ref[weight, :, 384:] = right[rows].astype(jnp.bfloat16)
+    smalls_ref[...] = jnp.dot(
+        small_ref[...], c[:, 256:], preferred_element_type=jnp.float32
+    ).astype(jnp.bfloat16)
+
+
+def unpack_shards(parts):
+    left, right, small = (jnp.asarray(t, jnp.bfloat16) for t in placing_tables())
+    whole = lambda t: pl.BlockSpec(t.shape, lambda g: (0, 0))
+    return pl.pallas_call(
+        unpack_kernel,
+        grid=(16,),
+        out_shape=[
+            jax.ShapeDtypeStruct((4, WIDTH, WIDTH), jnp.bfloat16),
+            jax.ShapeDtypeStruct((WIDTH, 128), jnp.bfloat16),
+        ],
+        in_specs=[
+            *(pl.BlockSpec((1, 128, lanes), lambda g: (g, 0, 0)) for lanes in PART_LANES),
+            whole(left),
+            whole(right),
+            whole(small),
+        ],
+        out_specs=[
+            pl.BlockSpec((4, 48, WIDTH), lambda g: (0, g, 0)),
+            pl.BlockSpec((48, 128), lambda g: (g, 0)),
+        ],
+        name="unpack_shards",
+        compiler_params=pltpu.CompilerParams(vmem_limit_bytes=24 * 2**20),
+    )(*(part.reshape(16, 128, -1) for part in parts), left, right, small)
+
+
+def pack_kernel(weights_ref, smalls_ref, left_ref, right_ref, small_ref, out_ref):
+    left = jnp.concatenate([weights_ref[w, :, :384] for w in range(4)], axis=0).astype(jnp.bfloat16)
+    right = jnp.concatenate([weights_ref[w, :, 384:] for w in range(4)], axis=0).astype(jnp.bfloat16)
+    from_left = jnp.dot(left_ref[...], left, preferred_element_type=jnp.float32)
+    from_right = jnp.dot(right_ref[...], right, preferred_element_type=jnp.float32)
+    out_ref[0, :, :384] = from_left[:128].astype(jnp.bfloat16)
+    out_ref[0, :, 384:768] = from_right[:128].astype(jnp.bfloat16)
+    out_ref[0, :, 768:1152] = (from_left[128:] + from_right[128:]).astype(jnp.bfloat16)
+    out_ref[0, :, 1152:] = jnp.dot(
+        small_ref[...], smalls_ref[...].astype(jnp.bfloat16), preferred_element_type=jnp.float32
+    ).astype(jnp.bfloat16)
+
+
+def pack_shards(weights, smalls):
+    left, right, small = (jnp.asarray(t.T, jnp.bfloat16) for t in placing_tables())
+    whole = lambda t: pl.BlockSpec(t.shape, lambda g: (0, 0))
+    return pl.pallas_call(
+        pack_kernel,
+        grid=(16,),
+        out_shape=jax.ShapeDtypeStruct((16, 128, 1280), jnp.bfloat16),
+        in_specs=[
+            pl.BlockSpec((4, 48, WIDTH), lambda g: (0, g, 0)),
+            pl.BlockSpec((48, 128), lambda g: (g, 0)),
+            whole(left),
+            whole(right),
+            whole(small),
+        ],
+        out_specs=pl.BlockSpec((1, 128, 1280), lambda g: (g, 0, 0)),
+        name="pack_shards",
+        compiler_params=pltpu.CompilerParams(vmem_limit_bytes=24 * 2**20),
+    )(weights, smalls, left, right, small).reshape(4, 4, 4, 2, 16, 1280)
+
+
+def pack_own(weights, smalls):
+    rows = jnp.concatenate(weights, axis=0)
+    tail = jnp.concatenate([rows[16:, :384], rows[16:, 384:]], axis=0)
+    small = jnp.pad(jnp.concatenate(smalls, axis=1), ((0, 10), (0, 108)))
+    return jnp.concatenate([rows[:16], tail, small], axis=1)
+
+
+def unpack_own(packed):
+    tail = jnp.concatenate([packed[:8, 768:1152], packed[8:, 768:1152]], axis=1)
+    rows = jnp.concatenate([packed[:16, :768], tail], axis=0)
+    small = packed[:6, 1152:]
+    return [rows[i * 6 : i * 6 + 6] for i in range(4)], small
 
 
 highest = lax.Precision.HIGHEST
@@ -80,25 +525,24 @@
     w_down,
     cotangent,
 ):
-    gain_one, gain_two, query_w, key_w, value_w, output_w, router_w, constant_w, constant_v = (
-        lax.all_gather(norm_first, ("ctx", "fsdp"), axis=0, tiled=True),
-        lax.all_gather(norm_second, ("ctx", "fsdp"), axis=0, tiled=True),
-        lax.all_gather(w_query, ("ctx", "fsdp"), axis=0, tiled=True),
-        lax.all_gather(w_key, ("ctx", "fsdp"), axis=0, tiled=True),
-        lax.all_gather(w_value, ("ctx", "fsdp"), axis=0, tiled=True),
-        lax.all_gather(w_output, ("ctx", "fsdp"), axis=0, tiled=True),
-        lax.all_gather(w_router, ("ctx", "fsdp"), axis=0, tiled=True),
-        lax.all_gather(w_constant, ("ctx", "fsdp"), axis=0, tiled=True),
-        lax.all_gather(v_constant, ("ctx", "fsdp"), axis=0, tiled=True),
-    )
-    gate_full, up_full, down_full = (
-        lax.all_gather(w_gate, "ctx", axis=1, tiled=True),
-        lax.all_gather(w_up, "ctx", axis=1, tiled=True),
-        lax.all_gather(w_down, "ctx", axis=1, tiled=True),
-    )
-    gate_w = gate_full[0]
-    up_w = up_full[0]
-    down_w = down_full[0]
+    def over_ctx(array):
+        return lax.all_to_all(
+            jnp.broadcast_to(array[None], (8, *array.shape)), "ctx", 0, 0, tiled=True
+        )
+
+    experts = over_ctx(
+        jnp.concatenate([w_gate[0], w_up[0], w_down[0].reshape(96, 1024)], axis=0)
+    ).reshape(8, 3, 96, 1024)
+    own = pack_own(
+        [w_query, w_key, w_value, w_output],
+        [w_router, w_constant, v_constant, norm_first[:, None], norm_second[:, None]],
+    )
+    (query_w, key_w, value_w, output_w), smalls = unpack_shards(gather_shards(own))
+    router_w, constant_w, constant_v = smalls[:, :12], smalls[:, 12:16], smalls[:, 16:18]
+    gain_one, gain_two = smalls[:, 18], smalls[:, 19]
+    gate_w = experts[:, 0].reshape(768, 1024)
+    up_w = experts[:, 1].reshape(768, 1024)
+    down_w = experts[:, 2].reshape(1024, 768)
     ctx_count = lax.axis_size("ctx")
     halves = lax.axis_size("fsdp") // EXPERTS
     block_len = tokens.shape[1]
@@ -121,11 +565,12 @@
     keys_own = rotate(project(key_w), cosine, sine_table).astype(jnp.bfloat16)
     values_own = project(value_w).astype(jnp.bfloat16)
     query_seg = segments[0]
-    keys_all, values_all, seg_all = (
-        lax.all_gather(keys_own.reshape(block_len, width), "ctx", axis=0, tiled=True),
-        lax.all_gather(values_own.reshape(block_len, width), "ctx", axis=0, tiled=True),
-        lax.all_gather(query_seg.astype(jnp.bfloat16), "ctx", axis=0, tiled=True),
-    )
+    keys_values = over_ctx(
+        jnp.concatenate([keys_own.reshape(block_len, width), values_own.reshape(block_len, width)], axis=0)
+    )
+    keys_all = keys_values[:, :block_len].reshape(length, width)
+    values_all = keys_values[:, block_len:].reshape(length, width)
+    seg_all = over_ctx(query_seg.astype(jnp.bfloat16)).reshape(length)
     key_block = min(512, length)
     block_count = length // key_block
     key_blocks = keys_all.reshape(block_count, key_block, HEADS, HDIM)
@@ -305,17 +750,20 @@
         returned_grad.reshape(EXPERTS, halves, CAP, width),
         preferred_element_type=jnp.float32,
     )
-    expert_gate_grad, expert_up_grad, expert_down_grad = (
-        lax.psum_scatter(
-            gate_grad_w[None].astype(jnp.bfloat16), "ctx", scatter_dimension=1, tiled=True
-        ).astype(jnp.float32),
-        lax.psum_scatter(
-            up_grad_w[None].astype(jnp.bfloat16), "ctx", scatter_dimension=1, tiled=True
-        ).astype(jnp.float32),
-        lax.psum_scatter(
-            down_grad[None].astype(jnp.bfloat16), "ctx", scatter_dimension=1, tiled=True
-        ).astype(jnp.float32),
-    )
+    expert_grads = jnp.concatenate(
+        [
+            gate_grad_w.astype(jnp.bfloat16).reshape(8, 96, 1024),
+            up_grad_w.astype(jnp.bfloat16).reshape(8, 96, 1024),
+            down_grad.astype(jnp.bfloat16).reshape(8, 96, 1024),
+        ],
+        axis=1,
+    )
+    expert_sum = jnp.sum(
+        lax.all_to_all(expert_grads, "ctx", 0, 0, tiled=True).astype(jnp.float32), axis=0
+    )
+    expert_gate_grad = expert_sum[None, :96]
+    expert_up_grad = expert_sum[None, 96:192]
+    expert_down_grad = expert_sum[192:].reshape(1, 128, 768)
     state_grad, gain_two_grad = rms_backward(
         residual_state, scale_two, gain_two.astype(jnp.float32), normed_grad
     )
@@ -366,14 +814,14 @@
         jnp.zeros((length, width), jnp.float32),
     )
     query_grad, key_parts, value_parts = lax.fori_loop(0, needed, grad_body, start_grads)
-    key_grad, value_grad = (
-        lax.psum_scatter(
-            key_parts.astype(jnp.bfloat16), "ctx", scatter_dimension=0, tiled=True
-        ).astype(jnp.float32),
-        lax.psum_scatter(
-            value_parts.astype(jnp.bfloat16), "ctx", scatter_dimension=0, tiled=True
-        ).astype(jnp.float32),
-    )
+    both_parts = jnp.concatenate(
+        [key_parts.astype(jnp.bfloat16).reshape(8, block_len, width), value_parts.astype(jnp.bfloat16).reshape(8, block_len, width)],
+        axis=1,
+    )
+    both_sum = jnp.sum(
+        lax.all_to_all(both_parts, "ctx", 0, 0, tiled=True).astype(jnp.float32), axis=0
+    )
+    key_grad, value_grad = both_sum[:block_len], both_sum[block_len:]
     query_low = (
         rotate(query_grad, cosine, -sine_table).reshape(block_len, width).astype(jnp.bfloat16)
     )
@@ -395,28 +843,20 @@
         inputs_wide, scale_one, gain_one.astype(jnp.float32), first_grad
     )
     tokens_grad = tokens_grad + state_grad
-    (
-        sum_gain_one,
-        sum_query,
-        sum_key,
-        sum_value,
-        sum_output,
-        sum_gain_two,
-        sum_router,
-        sum_constant,
-        sum_vectors,
-    ) = (
-        lax.psum_scatter(gain_one_grad, ("ctx", "fsdp"), scatter_dimension=0, tiled=True),
-        lax.psum_scatter(query_grad_w, ("ctx", "fsdp"), scatter_dimension=0, tiled=True),
-        lax.psum_scatter(key_grad_w, ("ctx", "fsdp"), scatter_dimension=0, tiled=True),
-        lax.psum_scatter(value_grad_w, ("ctx", "fsdp"), scatter_dimension=0, tiled=True),
-        lax.psum_scatter(output_grad_w, ("ctx", "fsdp"), scatter_dimension=0, tiled=True),
-        lax.psum_scatter(gain_two_grad, ("ctx", "fsdp"), scatter_dimension=0, tiled=True),
-        lax.psum_scatter(router_grad, ("ctx", "fsdp"), scatter_dimension=0, tiled=True),
-        lax.psum_scatter(constant_grad, ("ctx", "fsdp"), scatter_dimension=0, tiled=True),
-        lax.psum_scatter(vector_grad, ("ctx", "fsdp"), scatter_dimension=0, tiled=True),
-    )
-    residual_total = lax.psum(residual_grad, ("ctx", "fsdp"))
+    small_grads = jnp.pad(
+        jnp.concatenate(
+            [router_grad, constant_grad, vector_grad, gain_one_grad[:, None], gain_two_grad[:, None]], axis=1
+        ),
+        ((0, 0), (0, 108)),
+    )
+    packed = pack_shards(
+        jnp.stack([query_grad_w, key_grad_w, value_grad_w, output_grad_w]), small_grads
+    )
+    summed, residual_total = scatter_shards(packed, jnp.pad(residual_grad, ((0, 4), (0, 116))))
+    (sum_query, sum_key, sum_value, sum_output), small_sum = unpack_own(summed)
+    sum_router, sum_constant, sum_vectors = small_sum[:, :12], small_sum[:, 12:16], small_sum[:, 16:18]
+    sum_gain_one, sum_gain_two = small_sum[:, 18], small_sum[:, 19]
+    residual_total = residual_total[:12, :12]
     return (
         block_output.astype(jnp.bfloat16)[None],
         tokens_grad[None],

time: 2630 us -> 732 us (0.28)
  blocking collectives: 977 us -> 0 us
  waiting for transfers between devices: 896 us -> 189 us
  starting transfers between devices: 359 us -> 90.1 us
  Pallas kernels: 0 us -> 126 us
    all_gather x9 -> x0, waiting for transfers between devices: 663 us -> none  [the longest x1 190 us: on_device(): lax.all_gather(w_key, ('ctx', 'fsdp'), axis=0, tiled=True)]
    all_gather x4 -> x0, blocking collectives: 490 us -> none  [the longest x1 164 us: on_device(): lax.all_gather(w_constant, ('ctx', 'fsdp'), axis=0, tiled=True)]
    unnamed x3 -> x0, blocking collectives: 487 us -> none
    unnamed x128 -> x0, starting transfers between devices: 336 us -> none
    reduce_scatter x5 -> x0, waiting for transfers between devices: 184 us -> none  [the longest x1 116 us: on_device(): lax.psum_scatter(key_parts.astype(jnp.bfloat16), 'ctx', scatter_dimension...]
    all_to_all x0 -> x5, waiting for transfers between devices: none -> 153 us  [the longest x3 78.3 us: over_ctx(): lax.all_to_all(jnp.broadcast_to(array[None], (8, *array.shape)), 'ctx', 0...]
    pallas_call x0 -> x4, Pallas kernels: none -> 126 us  [the longest x1 85 us: gather_shards(): pl.pallas_call(gather_kernel, out_shape=[jax.ShapeDtypeStruct((4, 4, 4, 2...]
    all_to_all x0 -> x5, starting transfers between devices: none -> 69 us  [the longest x1 30.7 us: on_device(): lax.all_to_all(both_parts, 'ctx', 0, 0, tiled=True).astype(jnp.float32)]
  transfers between devices with their start and end apart: 146 -> 9, of which waited for: 21 -> 6; matrix products, arithmetic and copies ran while one was open for 23% -> 25% of each run, Pallas kernels for 0% -> 12%
where the time goes in v1:
time: 732 us; the launch traced here: 718 us
  waiting for transfers between devices  189 us (26%)
  local copies, waits for them, and re-layouts  134 us (18%)
  matrix products  133 us (18%)
  Pallas kernels  126 us (17%)
  starting transfers between devices  90.1 us (12%)
  other arithmetic  44.3 us (6%)
    pallas_call x1, Pallas kernels, gather_shards(): pl.pallas_call(gather_kernel, out_shape=[jax.ShapeDtypeStruct((4, 4, 4, 2...  85 us
    all_to_all x3, waiting for transfers between devices, over_ctx(): lax.all_to_all(jnp.broadcast_to(array[None], (8, *array.shape)), 'ctx', 0...  78.3 us
    all_to_all x1, waiting for transfers between devices, on_device(): lax.all_to_all(both_parts, 'ctx', 0, 0, tiled=True).astype(jnp.float32)  74.2 us
    all_to_all x1, starting transfers between devices, on_device(): lax.all_to_all(both_parts, 'ctx', 0, 0, tiled=True).astype(jnp.float32)  30.7 us
    pallas_call x1, Pallas kernels, scatter_shards(): pl.pallas_call(scatter_kernel, out_shape=[jax.ShapeDtypeStruct((16, 1280)...  30.4 us
    all_to_all x3, starting transfers between devices, over_ctx(): lax.all_to_all(jnp.broadcast_to(array[None], (8, *array.shape)), 'ctx', 0...  22.6 us
    unnamed x132, local copies, waits for them, and re-layouts  21.9 us
    all_to_all x1, waiting for transfers between devices, on_device(): lax.all_to_all(outgoing, 'fsdp', split_axis=0, concat_axis=0, tiled=True)  16.3 us
  transfers between devices with their start and end apart: 9, of which 6 were waited for; matrix products, arithmetic and copies ran while one was open for 25% of the time, Pallas kernels for 12%

profile of v1, /device:TPU:4, one launch (start us, length us, event | category | flops | bytes accessed | tf_op | source)
XLA Modules:
  0.0 718.5 jit_solution(15949669093425761090)
XLA Ops:
  3.2 6.2 all-to-all-start.1
  13.1 2.7 broadcast_in_dim.80
  15.9 7.0 all-to-all-start.3
  24.0 85.0 %gather_shards.1 = (bf16[4,4,4,2,16,512]{5,4,3,2,1,0:T(8,128)(2,1)}, bf16[4,4,4,2,16,384]{5,4,3,2,1,0:T(8,128)(2,1)}, bf16[4,4,4,2,16,384]{5,4,3,2,1,0:T(8,128)(2,1)}) custom-call(bf16[16,1280]{1,0:T(8,128)(2,1)} %fusion.139.own_ref), custom_call_target="tpu_custom_call" | custom-call | tf_op jit(solution)/shard_map/gather_shards/pallas_call | solution.py:139
  113.5 4.4 unpack_shards.1
  130.9 3.2 broadcast_in_dim.74
  134.1 9.5 %all-to-all-start = ((bf16[8,512,768]{1,2,0:T(8,128)(2,1)}), bf16[8,512,768]{1,2,0:T(8,128)(2,1)}, u32[]{:S(2)}, u32[]{:S(2)}) async-start(bf16[8,512,768]{1,2,0:T(8,128)(2,1)} %broadcast_in_dim.74), calls=%async_computation | async-start | bytes 12582912 | tf_op jit(solution)/shard_map/all_to_all | solution.py:529
  144.8 4.8 fusion.169
  151.7 76.7 %all-to-all-done = bf16[8,512,768]{1,2,0:T(8,128)(2,1)} async-done(((bf16[8,512,768]{1,2,0:T(8,128)(2,1)}), bf16[8,512,768]{1,2,0:T(8,128)(2,1)}, u32[]{:S(2)}, u32[]{:S(2)}) %all-to-all-start) | async-done | bytes 6291488 | tf_op jit(solution)/shard_map/all_to_all | solution.py:529
  228.5 5.1 fusion.167
  233.6 3.5 copy.176
  237.0 6.0 reshape_reshape.7
  243.0 4.3 copy.180
  247.3 12.2 %while.39 = (s32[]{:T(128)}, f32[12,256]{1,0:T(8,128)S(1)}, f32[12,256]{1,0:T(8,128)S(1)}, s32[]{:T(128)}, s32[4,512]{1,0:T(4,128)S(1)}, /*index=5*/s32[1,256]{1...) while((s32[]{:T(128)}, f32[12,256]{1,0:T(8,128)S(1)}, ...), condition=%wide.region_4.5_spmd.clone, body=%wide.region_1.4_spmd.clone.sunk | while | flops 212736768 | bytes 14329019 | solution.py:606
  259.5 5.3 copy.175
  264.8 6.0 reshape_reshape.6
  270.8 4.4 copy.179
  275.3 11.8 %while.40 = (s32[]{:T(128)}, f32[256,12,64]{0,2,1:T(8,128)S(1)}, s32[]{:T(128)}, bf16[4,512,12,64]{1,3,2,0:T(8,128)(2,1)}, s32[4,512]{1,0:T(4,128)S(1)}, /*index...) while((s32[]{:T(128)}, f32[256,12,64]{0,2,1:T(8,128)S(1)}, ...), condition=%wide.region_6.7_spmd.clone, body=%wide.region_5.6_spmd.clone.sunk | while | flops 409535232 | bytes 3827903 | solution.py:615
  275.6 3.7 fusion.259
  279.5 3.7 fusion.259
  283.4 3.7 fusion.259
  296.3 4.4 all-to-all-start.2
  305.9 16.3 %all-to-all-done.2 = bf16[16,54,768]{2,1,0:T(8,128)(2,1)} async-done(((bf16[16,54,768]{2,1,0:T(8,128)(2,1)}), bf16[16,54,768]{2,1,0:T(8,128)(2,1)}, u32[]{:S(2)}, u32[]{:S(2)}) %all-to-all-start.2) | async-done | bytes 1327136 | tf_op jit(solution)/shard_map/all_to_all | solution.py:648
  324.5 4.8 all-to-all-start.5
  336.0 5.4 fusion.173
  341.4 3.3 fusion.174
  344.6 6.2 all-to-all-done.5
  353.2 8.6 %multiply_convert_fusion.1 = (bf16[864,1024]{1,0:T(8,128)(2,1)}, bf16[864,1024]{1,0:T(8,128)(2,1)}, bf16[864,1024]{1,0:T(8,128)(2,1)S(1)}) fusion(f32[864,1024]{1,0:T(8,128)} %fusion.173, f32[864,1024]{1,0:T(8,128)} %fusion.174, bf16[864,768]{1,0:T(8,128)(2,1)} %reshape.696, bf16[1024,768]{1,0:T(8,128)(2,1)} %reshape_squeeze.15), kind=kOutput, calls=%fused_computation.80 | convolution fusion | flops 1372225536 | bytes 15286272 | tf_op jit(solution)/shard_map/dot_general | solution.py:728
  363.1 2.6 convolution_convert_fusion.3
  368.2 4.6 all-to-all-start.4
  372.8 3.7 fusion.175
  376.5 2.7 add_convert_fusion
  379.2 3.0 convolution_convert_fusion
  382.2 3.9 reshape.704
  388.4 3.8 convolution_convert_fusion.2
  396.5 7.3 %all-to-all-start.6 = ((bf16[16,54,768]{2,1,0:T(8,128)(2,1)}), bf16[16,54,768]{2,1,0:T(8,128)(2,1)}, u32[]{:S(2)}, u32[]{:S(2)}) async-start(bf16[16,54,768]{2,1,0:T(8,128)(2,1)} %reshape.697), calls=%async_computation.6 | async-start | bytes 2752512 | tf_op jit(solution)/shard_map/all_to_all | solution.py:744
  405.6 4.3 multiply_reduce_fusion.4
  411.5 13.9 %all-to-all-done.6 = bf16[16,54,768]{2,1,0:T(8,128)(2,1)} async-done(((bf16[16,54,768]{2,1,0:T(8,128)(2,1)}), bf16[16,54,768]{2,1,0:T(8,128)(2,1)}, u32[]{:S(2)}, u32[]{:S(2)}) %all-to-all-start.6) | async-done | bytes 1327136 | tf_op jit(solution)/shard_map/all_to_all | solution.py:744
  425.3 15.8 %all-to-all-start.8 = ((bf16[8,288,1024]{2,1,0:T(8,128)(2,1)}), bf16[8,288,1024]{2,1,0:T(8,128)(2,1)}, u32[]{:S(2)}, u32[]{:S(2)}) async-start(bf16[8,288,1024]{2,1,0:T(8,128)(2,1)} %pad_maximum_fusion.2), calls=%async_computation.8 | async-start | bytes 9437184 | tf_op jit(solution)/shard_map/all_to_all | solution.py:762
  453.7 74.5 %while.41 = (s32[]{:T(128)}, f32[256,12,64]{0,2,1:T(8,128)}, bf16[2048,768]{1,0:T(8,128)(2,1)}, bf16[2048,768]{1,0:T(8,128)(2,1)}, s32[]{:T(128)}, /*index=5*/bf...) while((s32[]{:T(128)}, f32[256,12,64]{0,2,1:T(8,128)}, ...), condition=%wide.region_33.34_spmd.clone, body=%wide.region_32.33_spmd.clone.sunk | while | flops 1023935232 | bytes 68863312 | solution.py:816
  456.3 3.8 fusion.271
  460.1 3.0 convolution_multiply_fusion.3
  465.4 5.3 fusion.273
  473.0 2.6 constant_dynamic-update-slice_fusion.3
  475.6 2.9 fusion.272
  481.1 3.8 fusion.271
  484.9 3.0 convolution_multiply_fusion.3
  490.2 5.3 fusion.273
  497.8 2.6 constant_dynamic-update-slice_fusion.3
  500.4 2.9 fusion.272
  505.9 3.8 fusion.271
  509.8 3.0 convolution_multiply_fusion.3
  515.0 5.3 fusion.273
  522.6 2.6 constant_dynamic-update-slice_fusion.3
  525.3 2.9 fusion.272
  528.2 5.9 pad_maximum_fusion.1
  534.0 8.7 %copy.190 = bf16[8,512,768]{1,2,0:T(8,128)(2,1)} copy(bf16[8,512,768]{2,1,0:T(8,128)(2,1)} %pad_maximum_fusion.1) | data formatting | bytes 12582912 | tf_op jit(solution)/shard_map/concatenate | solution.py:817
  542.8 30.7 %all-to-all-start.7 = ((bf16[8,512,768]{1,2,0:T(8,128)(2,1)}), bf16[8,512,768]{1,2,0:T(8,128)(2,1)}, u32[]{:S(2)}, u32[]{:S(2)}) async-start(bf16[8,512,768]{1,2,0:T(8,128)(2,1)} %copy.190), calls=%async_computation.7 | async-start | bytes 12582912 | tf_op jit(solution)/shard_map/all_to_all | solution.py:822
  576.9 3.5 convert_reduce_fusion.1
  582.3 74.2 %all-to-all-done.7 = bf16[8,512,768]{1,2,0:T(8,128)(2,1)} async-done(((bf16[8,512,768]{1,2,0:T(8,128)(2,1)}), bf16[8,512,768]{1,2,0:T(8,128)(2,1)}, u32[]{:S(2)}, u32[]{:S(2)}) %all-to-all-start.7) | async-done | bytes 6291488 | tf_op jit(solution)/shard_map/all_to_all | solution.py:822
  656.5 3.9 convert_reduce_fusion
  671.8 4.3 pad_maximum_fusion.weights_ref
  676.1 5.7 pack_shards.1
  681.8 30.4 %scatter_shards.1 = (f32[16,1280]{1,0:T(8,128)S(1)}, f32[16,128]{1,0:T(8,128)S(1)}) custom-call(bf16[4,4,4,2,16,1280]{5,4,3,2,1,0:T(8,128)(2,1)S(1)} %bitcast.388, f32[16,128]{1,0:T(8,128)S(1)} %pad.14.small_ref), custom_call_target="tpu_custom_call" | custom-call | tf_op jit(solution)/shard_map/scatter_shards/pallas_call | solution.py:314
  (337 shorter events, 135.9 us)
Async XLA Ops:
  0.6 288.9 %copy-start = (f32[12,12]{1,0:T(8,128)S(1)}, f32[12,12]{1,0:T(8,128)}, u32[]{:S(2)}) copy-start(f32[12,12]{1,0:T(8,128)} %param.43) | copy-start | bytes 1732
  3.2 9.9 %all-to-all-start.1 = ((bf16[8,2,128]{2,1,0:T(2,128)(2,1)}), bf16[8,2,128]{2,1,0:T(2,128)(2,1)S(1)}, u32[]{:S(2)}, u32[]{:S(2)}) async-start(bf16[8,2,128]{2,1,0:T(2,128)(2,1)} %reshape.727), calls=%async_computation.1 | async-start | bytes 8192 | tf_op jit(solution)/shard_map/all_to_all | solution.py:529
  15.7 7.1 copy-start.52
  15.7 7.2 %copy-start.53 = (bf16[6,2]{0,1:T(2,128)(2,1)S(1)}, bf16[6,2]{0,1:T(2,128)(2,1)}, u32[]{:S(2)}) copy-start(bf16[6,2]{0,1:T(2,128)(2,1)} %param.45) | copy-start | bytes 76
  15.7 7.3 %copy-start.54 = (bf16[6]{0:T(256)(128)(2,1)S(1)}, bf16[6]{0:T(256)(128)(2,1)}, u32[]{:S(2)}) copy-start(bf16[6]{0:T(256)(128)(2,1)} %param.36) | copy-start | bytes 40
  15.7 7.4 %copy-start.55 = (bf16[6]{0:T(256)(128)(2,1)S(1)}, bf16[6]{0:T(256)(128)(2,1)}, u32[]{:S(2)}) copy-start(bf16[6]{0:T(256)(128)(2,1)} %param.41) | copy-start | bytes 40
  15.8 7.5 %copy-start.51 = (bf16[6,12]{1,0:T(8,128)(2,1)S(1)}, bf16[6,12]{1,0:T(8,128)(2,1)}, u32[]{:S(2)}) copy-start(bf16[6,12]{1,0:T(8,128)(2,1)} %param.42) | copy-start | bytes 436
  15.8 7.6 %copy-start.46 = (bf16[6,768]{1,0:T(8,128)(2,1)S(1)}, bf16[6,768]{1,0:T(8,128)(2,1)}, u32[]{:S(2)}) copy-start(bf16[6,768]{1,0:T(8,128)(2,1)} %param.40) | copy-start | bytes 27652
  15.8 7.6 %copy-start.47 = (bf16[6,768]{1,0:T(8,128)(2,1)S(1)}, bf16[6,768]{1,0:T(8,128)(2,1)}, u32[]{:S(2)}) copy-start(bf16[6,768]{1,0:T(8,128)(2,1)} %param.39) | copy-start | bytes 27652
  15.8 7.6 %copy-start.48 = (bf16[6,768]{1,0:T(8,128)(2,1)S(1)}, bf16[6,768]{1,0:T(8,128)(2,1)}, u32[]{:S(2)}) copy-start(bf16[6,768]{1,0:T(8,128)(2,1)} %param.38) | copy-start | bytes 27652
  15.8 7.6 %copy-start.49 = (bf16[6,768]{1,0:T(8,128)(2,1)S(1)}, bf16[6,768]{1,0:T(8,128)(2,1)}, u32[]{:S(2)}) copy-start(bf16[6,768]{1,0:T(8,128)(2,1)} %param.37) | copy-start | bytes 27652
  15.8 93.2 %copy-start.7 = (bf16[192,256]{1,0:T(8,128)(2,1)S(1)}, bf16[192,256]{1,0:T(8,128)(2,1)}, u32[]{:S(2)}) copy-start(bf16[192,256]{1,0:T(8,128)(2,1)} %constant.128.clone.left_ref) | copy-start | bytes 294916
  15.8 93.2 %copy-start.8 = (bf16[192,256]{1,0:T(8,128)(2,1)S(1)}, bf16[192,256]{1,0:T(8,128)(2,1)}, u32[]{:S(2)}) copy-start(bf16[192,256]{1,0:T(8,128)(2,1)} %constant.129.clone.right_ref) | copy-start | bytes 294916
  15.8 93.2 %copy-start.10 = (bf16[48,128]{1,0:T(8,128)(2,1)S(1)}, bf16[48,128]{1,0:T(8,128)(2,1)}, u32[]{:S(2)}) copy-start(bf16[48,128]{1,0:T(8,128)(2,1)} %constant.130.clone.small_ref) | copy-start | bytes 36868
  15.9 115.0 %all-to-all-start.3 = ((bf16[8,288,1024]{2,1,0:T(8,128)(2,1)}), bf16[8,288,1024]{2,1,0:T(8,128)(2,1)}, u32[]{:S(2)}, u32[]{:S(2)}) async-start(bf16[8,288,1024]{2,1,0:T(8,128)(2,1)} %broadcast_in_dim.80), calls=%async_computation.3 | async-start | bytes 9437184 | tf_op jit(solution)/shard_map/all_to_all | solution.py:529
  117.9 3.3 copy-start.1
  123.4 2.8 copy-start.12
  126.2 3.8 copy-start.38
  127.0 3.1 copy-start.42
  134.1 9.7 %copy-start.44 = (s32[1,256,2]{1,2,0:T(2,128)S(1)}, s32[1,256,2]{1,2,0:T(2,128)}, u32[]{:S(2)}) copy-start(s32[1,256,2]{1,2,0:T(2,128)} %param.33) | copy-start | bytes 6148
  134.1 9.8 %copy-start.24 = (bf16[1,256,768]{2,1,0:T(8,128)(2,1)S(1)}, bf16[1,256,768]{2,1,0:T(8,128)(2,1)}, u32[]{:S(2)}) copy-start(bf16[1,256,768]{2,1,0:T(8,128)(2,1)} %param.49) | copy-start | bytes 1179652
  134.1 94.4 %all-to-all-start = ((bf16[8,512,768]{1,2,0:T(8,128)(2,1)}), bf16[8,512,768]{1,2,0:T(8,128)(2,1)}, u32[]{:S(2)}, u32[]{:S(2)}) async-start(bf16[8,512,768]{1,2,0:T(8,128)(2,1)} %broadcast_in_dim.74), calls=%async_computation | async-start | bytes 12582912 | tf_op jit(solution)/shard_map/all_to_all | solution.py:529
  243.0 4.3 copy-start.40
  287.2 2.1 copy-start.25
  289.4 16.1 %copy-start.14 = (bf16[256,768]{1,0:T(8,128)(2,1)}, bf16[256,768]{1,0:T(8,128)(2,1)S(1)}, u32[]{:S(2)}) copy-start(bf16[256,768]{1,0:T(8,128)(2,1)S(1)} %get-tuple-element.617) | copy-start | bytes 1179652
  296.3 25.9 %all-to-all-start.2 = ((bf16[16,54,768]{2,1,0:T(8,128)(2,1)}), bf16[16,54,768]{2,1,0:T(8,128)(2,1)}, u32[]{:S(2)}, u32[]{:S(2)}) async-start(bf16[16,54,768]{2,1,0:T(8,128)(2,1)} %bitcast.402), calls=%async_computation.2 | async-start | bytes 2752512 | tf_op jit(solution)/shard_map/all_to_all | solution.py:648
  324.5 26.3 %all-to-all-start.5 = ((bf16[16,54,768]{2,1,0:T(8,128)(2,1)}), bf16[16,54,768]{2,1,0:T(8,128)(2,1)}, u32[]{:S(2)}, u32[]{:S(2)}) async-start(bf16[16,54,768]{2,1,0:T(8,128)(2,1)} %bitcast.401), calls=%async_computation.5 | async-start | bytes 2752512 | tf_op jit(solution)/shard_map/all_to_all | solution.py:720
  336.0 5.4 copy-start.21
  336.0 5.4 copy-start.27
  353.2 9.9 %copy-start.23 = (bf16[1024,768]{1,0:T(8,128)(2,1)S(1)}, bf16[1024,768]{1,0:T(8,128)(2,1)}, u32[]{:S(2)}) copy-start(bf16[1024,768]{1,0:T(8,128)(2,1)} %reshape_squeeze.15) | copy-start | bytes 4718596
  368.2 28.3 %all-to-all-start.4 = ((bf16[16,54,768]{2,1,0:T(8,128)(2,1)}), bf16[16,54,768]{2,1,0:T(8,128)(2,1)}, u32[]{:S(2)}, u32[]{:S(2)}) async-start(bf16[16,54,768]{2,1,0:T(8,128)(2,1)} %reshape.692), calls=%async_computation.4 | async-start | bytes 2752512 | tf_op jit(solution)/shard_map/all_to_all | solution.py:658
  372.7 3.7 copy-start.22
  372.8 3.7 copy-start.57
  376.5 2.7 copy-start.29
  376.5 2.7 copy-start.60
  388.4 3.9 copy-start.28
  388.4 3.9 copy-start.58
  392.3 1.9 copy-start.18
  396.5 28.9 %all-to-all-start.6 = ((bf16[16,54,768]{2,1,0:T(8,128)(2,1)}), bf16[16,54,768]{2,1,0:T(8,128)(2,1)}, u32[]{:S(2)}, u32[]{:S(2)}) async-start(bf16[16,54,768]{2,1,0:T(8,128)(2,1)} %reshape.697), calls=%async_computation.6 | async-start | bytes 2752512 | tf_op jit(solution)/shard_map/all_to_all | solution.py:744
  403.8 1.7 copy-start.31
  403.8 1.8 copy-start.33
  425.3 117.4 %all-to-all-start.8 = ((bf16[8,288,1024]{2,1,0:T(8,128)(2,1)}), bf16[8,288,1024]{2,1,0:T(8,128)(2,1)}, u32[]{:S(2)}, u32[]{:S(2)}) async-start(bf16[8,288,1024]{2,1,0:T(8,128)(2,1)} %pad_maximum_fusion.2), calls=%async_computation.8 | async-start | bytes 9437184 | tf_op jit(solution)/shard_map/all_to_all | solution.py:762
  445.7 1.9 copy-start.19
  453.9 2.3 copy-start.35
  456.3 3.8 copy-start.11
  478.8 2.3 copy-start.35
  481.1 3.8 copy-start.11
  503.6 2.3 copy-start.35
  505.9 3.8 copy-start.11
  542.8 31.6 %copy-start.17 = (f32[256,768]{1,0:T(8,128)S(1)}, f32[256,768]{1,0:T(8,128)}, u32[]{:S(2)}) copy-start(f32[256,768]{1,0:T(8,128)} %copy-done.16) | copy-start | bytes 2359300
  542.8 31.6 %copy-start.26 = (bf16[256,12,64]{0,2,1:T(8,128)(2,1)S(1)}, bf16[256,12,64]{0,2,1:T(8,128)(2,1)}, u32[]{:S(2)}) copy-start(bf16[256,12,64]{0,2,1:T(8,128)(2,1)} %copy-done.25) | copy-start | bytes 1179652
  542.8 113.7 %all-to-all-start.7 = ((bf16[8,512,768]{1,2,0:T(8,128)(2,1)}), bf16[8,512,768]{1,2,0:T(8,128)(2,1)}, u32[]{:S(2)}, u32[]{:S(2)}) async-start(bf16[8,512,768]{1,2,0:T(8,128)(2,1)} %copy.190), calls=%async_computation.7 | async-start | bytes 12582912 | tf_op jit(solution)/shard_map/all_to_all | solution.py:822
  574.4 1.9 copy-start.15
  582.3 78.2 %copy-start.37 = (f32[256,32]{0,1:T(8,128)S(1)}, f32[256,32]{0,1:T(8,128)}, u32[]{:S(2)}) copy-start(f32[256,32]{0,1:T(8,128)} %copy-done.36) | copy-start | bytes 98308
  582.3 78.2 %copy-start.41 = (f32[256,32]{0,1:T(8,128)S(1)}, f32[256,32]{0,1:T(8,128)}, u32[]{:S(2)}) copy-start(f32[256,32]{0,1:T(8,128)} %get-tuple-element.664) | copy-start | bytes 98308
  660.4 9.7 %slice-start = ((s8[4718592]{0:T(1024)(128)(4,1)}), s8[4194304]{0:T(1024)(128)(4,1)S(1)}, s32[]{:S(2)}) async-start(s8[4718592]{0:T(1024)(128)(4,1)} %bitcast.389), calls=%async_computation.9 | async-start | bytes 8388608
  662.0 1.9 copy-start.13
  662.0 1.9 copy-start.39
  662.0 1.9 copy-start.43
  664.0 6.2 slice-start.1
  671.7 4.3 copy-start.5
  671.7 4.3 copy-start.6
  671.8 4.3 copy-start.9
  681.8 34.5 %copy-start.50 = (f32[256]{0:T(256)S(1)}, f32[256]{0:T(256)}, u32[]{:S(2)}) copy-start(f32[256]{0:T(256)} %get-tuple-element.667) | copy-start | bytes 3076
  (12 other events, 14.3 us)

commit v2 on v1

v2 whole, which is shorter than its diff:
```python
import functools

import jax
import jax.numpy as jnp
import numpy as np
from jax import lax
from jax.experimental import pallas as pl
from jax.experimental.pallas import tpu as pltpu
from jax.sharding import PartitionSpec as P

HEADS = 12
HDIM = 64
EXPERTS = 8
NALL = 12
CAP = 54
WIDTH = HEADS * HDIM
PAIRS = HEADS // 2
BLK = 256
SLOTS = 64

highest = lax.Precision.HIGHEST
masked_score = -1e30
epsilon = 1e-06

MESH = pl.DeviceIdType.MESH
PART_LANES = (512, 384, 384)
PART_START = (0, 512, 896)
PART_ORDER = ((0, 1, 2), (1, 2, 0), (2, 0, 1))


def place():
    ctx = lax.axis_index("ctx")
    fsdp = lax.axis_index("fsdp")
    return ctx // 2, (ctx % 2) * 2 + fsdp // 8, (fsdp // 2) % 4, fsdp % 2


def device_at(x, z, y, core):
    return {"ctx": x * 2 + z // 2, "fsdp": (z % 2) * 8 + y * 2 + core}


def shifted(spot, axis, by):
    moved = list(spot)
    moved[axis] = (moved[axis] + by) % 4
    return tuple(moved)


def greet(devices):
    barrier = pltpu.get_barrier_semaphore()
    for device in devices:
        pl.semaphore_signal(barrier, inc=1, device_id=device, device_id_type=MESH)
    pl.semaphore_wait(barrier, len(devices))


def torus_peers(spot, core):
    peers = [device_at(*shifted(spot, axis, by), core) for axis in range(3) for by in (1, 2, 3)]
    return peers + [device_at(*spot, 1 - core)]


def sequence_peers(spot, core):
    x, z, y = spot
    return [device_at((x + by) % 4, (z + 2) % 4, y, core) for by in (1, 2, 3)]


def region(ref, spot, core, whole):
    return ref.at[
        tuple(slice(None) if axis in whole else spot[axis] for axis in range(3)) + (core,)
    ]


def gather_kernel(own_ref, tokens_ref, *refs):
    parts, blocks_ref = refs[:3], refs[3]
    net_send, net_recv, twin_send, twin_recv, own_sem, block_send, block_recv = refs[4:]
    ctx = lax.axis_index("ctx")
    *spot, core = place()
    spot = tuple(spot)
    twin = device_at(*spot, 1 - core)
    greet(torus_peers(spot, core) + sequence_peers(spot, core))

    def net(part, step, by, source, target):
        axis = PART_ORDER[part][step]
        return pltpu.make_async_remote_copy(
            src_ref=source,
            dst_ref=target,
            send_sem=net_send.at[part, step, by - 1],
            recv_sem=net_recv.at[part, step, by - 1],
            device_id=device_at(*shifted(spot, axis, by), core),
            device_id_type=MESH,
        )

    def share(part, slot, source, target):
        return pltpu.make_async_remote_copy(
            src_ref=source,
            dst_ref=target,
            send_sem=twin_send.at[part, slot],
            recv_sem=twin_recv.at[part, slot],
            device_id=twin,
            device_id_type=MESH,
        )

    def block(by, owner, target):
        return pltpu.make_async_remote_copy(
            src_ref=tokens_ref,
            dst_ref=blocks_ref.at[owner],
            send_sem=block_send.at[by - 1],
            recv_sem=block_recv.at[by - 1],
            device_id={"ctx": target, "fsdp": lax.axis_index("fsdp")},
            device_id_type=MESH,
        )

    started = []
    kept = []
    for part in range(3):
        own = own_ref.at[:, pl.ds(PART_START[part], PART_LANES[part])]
        mine = region(parts[part], spot, core, ())
        for by in (1, 2, 3):
            copy = net(part, 0, by, own, mine)
            copy.start()
            started.append(copy)
    for part in range(3):
        own = own_ref.at[:, pl.ds(PART_START[part], PART_LANES[part])]
        mine = region(parts[part], spot, core, ())
        copy = pltpu.make_async_copy(own, mine, own_sem.at[part])
        copy.start()
        kept.append(copy)
        copy = share(part, 0, own, mine)
        copy.start()
        started.append(copy)
    copy = pltpu.make_async_copy(tokens_ref, blocks_ref.at[ctx], own_sem.at[3])
    copy.start()
    kept.append(copy)
    for by in range(1, 8):

        @pl.when(ctx + by < 8)
        def _(by=by):
            block(by, ctx, ctx + by).start()

    for copy in kept:
        copy.wait()
    for step in range(3):
        for part in range(3):
            order = PART_ORDER[part]
            axis = order[step]
            whole = order[:step]
            for by in (1, 2, 3):
                came = region(parts[part], shifted(spot, axis, -by), core, whole)
                net(part, step, by, came, came).wait_recv()
                copy = share(part, 1 + step * 3 + by - 1, came, came)
                copy.start()
                started.append(copy)
            if step < 2:
                held = region(parts[part], spot, core, order[: step + 1])
                for by in (1, 2, 3):
                    copy = net(part, step + 1, by, held, held)
                    copy.start()
                    started.append(copy)
    for part in range(3):
        order = PART_ORDER[part]
        first = region(parts[part], spot, 1 - core, ())
        share(part, 0, first, first).wait_recv()
        for step in range(3):
            for by in (1, 2, 3):
                came = region(
                    parts[part], shifted(spot, order[step], -by), 1 - core, order[:step]
                )
                share(part, 1 + step * 3 + by - 1, came, came).wait_recv()
    for by in range(1, 8):

        @pl.when(ctx - by >= 0)
        def _(by=by):
            block(by, ctx - by, ctx).wait_recv()

        @pl.when(ctx + by < 8)
        def _(by=by):
            block(by, ctx, ctx + by).wait_send()

    for copy in started:
        copy.wait_send()


def gather_shards(own, tokens):
    return pl.pallas_call(
        gather_kernel,
        out_shape=[
            jax.ShapeDtypeStruct((4, 4, 4, 2, 16, lanes), jnp.bfloat16) for lanes in PART_LANES
        ]
        + [jax.ShapeDtypeStruct((8, BLK + 16, WIDTH), jnp.bfloat16)],
        in_specs=[pl.BlockSpec(memory_space=pltpu.VMEM)] * 2,
        out_specs=[pl.BlockSpec(memory_space=pl.ANY)] * 4,
        scratch_shapes=[
            pltpu.SemaphoreType.DMA((3, 3, 3)),
            pltpu.SemaphoreType.DMA((3, 3, 3)),
            pltpu.SemaphoreType.DMA((3, 10)),
            pltpu.SemaphoreType.DMA((3, 10)),
            pltpu.SemaphoreType.DMA((4,)),
            pltpu.SemaphoreType.DMA((7,)),
            pltpu.SemaphoreType.DMA((7,)),
        ],
        name="gather_shards",
        compiler_params=pltpu.CompilerParams(collective_id=1, has_side_effects=True),
    )(own, tokens)


def scatter_kernel(
    grads_ref, small_ref, others_ref, first_ref, state_grad_ref, tokens_ref, gain_ref,
    out_ref, total_ref, tokens_grad_ref, *refs
):
    *refs, total_first, block_in, block_send, block_recv = refs
    ctx = lax.axis_index("ctx")
    twin_in, held = refs[0:3], refs[3:6]
    in_one, in_two, in_three = refs[6:9], refs[9:12], refs[12:15]
    sum_one, sum_two = refs[15:18], refs[18:21]
    small_in, small_sum, net_send, net_recv, twin_send, twin_recv, small_send, small_recv = refs[21:]
    *spot, core = place()
    spot = tuple(spot)
    twin = device_at(*spot, 1 - core)
    greet(torus_peers(spot, core) + sequence_peers(spot, core))
    started = []

    def block(by, target):
        return pltpu.make_async_remote_copy(
            src_ref=others_ref.at[target],
            dst_ref=block_in.at[by - 1],
            send_sem=block_send.at[by - 1],
            recv_sem=block_recv.at[by - 1],
            device_id={"ctx": target, "fsdp": lax.axis_index("fsdp")},
            device_id_type=MESH,
        )

    for by in range(1, 8):

        @pl.when(ctx - by >= 0)
        def _(by=by):
            block(by, ctx - by).start()

    def net(part, step, by, source, target):
        axis = PART_ORDER[part][2 - step]
        return pltpu.make_async_remote_copy(
            src_ref=source,
            dst_ref=target,
            send_sem=net_send.at[part, step, by - 1],
            recv_sem=net_recv.at[part, step, by - 1],
            device_id=device_at(*shifted(spot, axis, by), core),
            device_id_type=MESH,
        )

    def share(part):
        lanes = pl.ds(PART_START[part], PART_LANES[part])
        return pltpu.make_async_remote_copy(
            src_ref=grads_ref.at[:, :, :, 1 - core, :, lanes],
            dst_ref=twin_in[part],
            send_sem=twin_send.at[part],
            recv_sem=twin_recv.at[part],
            device_id=twin,
            device_id_type=MESH,
        )

    def small(axis, by, source, slot):
        device = twin if axis == 3 else device_at(*shifted(spot, axis, by), core)
        return pltpu.make_async_remote_copy(
            src_ref=source,
            dst_ref=small_in.at[axis, slot],
            send_sem=small_send.at[axis, by - 1],
            recv_sem=small_recv.at[axis, by - 1],
            device_id=device,
            device_id_type=MESH,
        )

    for part in range(3):
        copy = share(part)
        copy.start()
        started.append(copy)
    copy = small(3, 1, small_ref, core)
    copy.start()
    started.append(copy)

    def add_pairs(part):
        start, lanes = PART_START[part], PART_LANES[part]

        def step(index, carry):
            x, z, y = index // 16, (index // 4) % 4, index % 4
            held[part][x, z, y] = (
                grads_ref[x, z, y, core, :, start : start + lanes].astype(jnp.float32)
                + twin_in[part][x, z, y].astype(jnp.float32)
            ).astype(jnp.bfloat16)
            return carry

        lax.fori_loop(0, 64, step, 0, unroll=2)

    def cut(spots, axis, at):
        return tuple(at if a == axis else slice(None) for a in spots)

    for part in range(3):
        share(part).wait_recv()
        add_pairs(part)
        axis = PART_ORDER[part][2]
        for by in (1, 2, 3):
            index = cut((0, 1, 2), axis, shifted(spot, axis, by)[axis])
            copy = net(part, 0, by, held[part].at[index], in_one[part].at[by - 1])
            copy.start()
            started.append(copy)

    small(3, 1, small_ref, 1 - core).wait_recv()
    small_in[3, core] = small_ref[...]
    small_sum[0] = small_in[3, 0] + small_in[3, 1]
    for by in (1, 2, 3):
        copy = small(0, by, small_sum.at[0], spot[0])
        copy.start()
        started.append(copy)

    def small_step(axis):
        for by in (1, 2, 3):
            small(axis, by, small_sum.at[axis], shifted(spot, axis, -by)[axis]).wait_recv()
        small_in[axis, spot[axis]] = small_sum[axis]
        total = small_in[axis, 0] + small_in[axis, 1] + small_in[axis, 2] + small_in[axis, 3]
        if axis == 2:
            total_ref[...] = total
            return
        small_sum[axis + 1] = total
        for by in (1, 2, 3):
            copy = small(axis + 1, by, small_sum.at[axis + 1], spot[axis + 1])
            copy.start()
            started.append(copy)

    for part in range(3):
        first, second, third = PART_ORDER[part]
        for by in (1, 2, 3):
            net(part, 0, by, in_one[part].at[by - 1], in_one[part].at[by - 1]).wait_recv()
        rest = tuple(a for a in (0, 1, 2) if a != third)

        def add_four(index, carry, part=part, third=third, rest=rest):
            at = {rest[0]: index // 4, rest[1]: index % 4, third: spot[third]}
            total = held[part][at[0], at[1], at[2]].astype(jnp.float32)
            for by in range(3):
                total = total + in_one[part][by, index // 4, index % 4].astype(jnp.float32)
            sum_one[part][index // 4, index % 4] = total.astype(jnp.bfloat16)
            return carry

        lax.fori_loop(0, 16, add_four, 0, unroll=2)
        for by in (1, 2, 3):
            at = shifted(spot, second, by)[second]
            source = sum_one[part].at[at] if second == rest[0] else sum_one[part].at[:, at]
            copy = net(part, 1, by, source, in_two[part].at[by - 1])
            copy.start()
            started.append(copy)
    small_step(0)
    for part in range(3):
        first, second, third = PART_ORDER[part]
        for by in (1, 2, 3):
            net(part, 1, by, in_two[part].at[by - 1], in_two[part].at[by - 1]).wait_recv()
        rest = tuple(a for a in (0, 1, 2) if a != third)
        for index in range(4):
            if second == rest[0]:
                total = sum_one[part][spot[second], index].astype(jnp.float32)
            else:
                total = sum_one[part][index, spot[second]].astype(jnp.float32)
            for by in range(3):
                total = total + in_two[part][by, index].astype(jnp.float32)
            sum_two[part][index] = total.astype(jnp.bfloat16)
        for by in (1, 2, 3):
            at = shifted(spot, first, by)[first]
            copy = net(part, 2, by, sum_two[part].at[at], in_three[part].at[by - 1])
            copy.start()
            started.append(copy)
    small_step(1)
    for part in range(3):
        first = PART_ORDER[part][0]
        for by in (1, 2, 3):
            net(part, 2, by, in_three[part].at[by - 1], in_three[part].at[by - 1]).wait_recv()
        total = sum_two[part][spot[first]].astype(jnp.float32)
        for by in range(3):
            total = total + in_three[part][by].astype(jnp.float32)
        out_ref[:, PART_START[part] : PART_START[part] + PART_LANES[part]] = total
    small_step(2)
    total_first[...] = first_ref[...]
    for by in range(1, 8):

        @pl.when(ctx + by < 8)
        def _(by=by):
            block(by, ctx).wait_recv()
            total_first[...] += block_in[by - 1].astype(jnp.float32)

        @pl.when(ctx - by >= 0)
        def _(by=by):
            block(by, ctx - by).wait_send()

    wide = tokens_ref[...].astype(jnp.float32)
    scale = rms_rows(wide)
    weighted = total_first[...] * gain_ref[...]
    tokens_grad_ref[...] = (
        state_grad_ref[...]
        + scale * weighted
        - wide * (scale**3 * jnp.mean(weighted * wide, axis=-1, keepdims=True))
    )
    for copy in started:
        copy.wait_send()


def scatter_shards(grads, small, others, first, state_grad, tokens, gain):
    by_part = lambda *lead: [pltpu.VMEM((*lead, 16, lanes), jnp.bfloat16) for lanes in PART_LANES]
    return pl.pallas_call(
        scatter_kernel,
        out_shape=[
            jax.ShapeDtypeStruct((16, 1280), jnp.float32),
            jax.ShapeDtypeStruct((16, 128), jnp.float32),
            jax.ShapeDtypeStruct((BLK, WIDTH), jnp.float32),
        ],
        in_specs=[pl.BlockSpec(memory_space=pltpu.VMEM)] * 2
        + [pl.BlockSpec(memory_space=pl.ANY)]
        + [pl.BlockSpec(memory_space=pltpu.VMEM)] * 4,
        out_specs=[pl.BlockSpec(memory_space=pltpu.VMEM)] * 3,
        scratch_shapes=[
            *by_part(4, 4, 4),
            *by_part(4, 4, 4),
            *by_part(3, 4, 4),
            *by_part(3, 4),
            *by_part(3),
            *by_part(4, 4),
            *by_part(4),
            pltpu.VMEM((4, 4, 16, 128), jnp.float32),
            pltpu.VMEM((3, 16, 128), jnp.float32),
            pltpu.SemaphoreType.DMA((3, 3, 3)),
            pltpu.SemaphoreType.DMA((3, 3, 3)),
            pltpu.SemaphoreType.DMA((3,)),
            pltpu.SemaphoreType.DMA((3,)),
            pltpu.SemaphoreType.DMA((4, 3)),
            pltpu.SemaphoreType.DMA((4, 3)),
            pltpu.VMEM((BLK, WIDTH), jnp.float32),
            pltpu.VMEM((7, BLK, WIDTH), jnp.bfloat16),
            pltpu.SemaphoreType.DMA((7,)),
            pltpu.SemaphoreType.DMA((7,)),
        ],
        name="scatter_shards",
        compiler_params=pltpu.CompilerParams(
            collective_id=2, has_side_effects=True, vmem_limit_bytes=40 * 2**20
        ),
    )(grads, small, others, first, state_grad, tokens, gain)


def placing_tables():
    left = np.zeros((192, 256), np.float32)
    right = np.zeros((192, 256), np.float32)
    small = np.zeros((48, 128), np.float32)
    for device in range(8):
        for weight in range(4):
            for row in range(6):
                at, line = weight * 48 + device * 6 + row, weight * 6 + row
                if line < 16:
                    left[at, device * 16 + line] = right[at, device * 16 + line] = 1
                else:
                    left[at, 128 + device * 16 + line - 16] = 1
                    right[at, 128 + device * 16 + line - 8] = 1
        for row in range(6):
            small[device * 6 + row, device * 16 + row] = 1
    return left, right, small


def unpack_kernel(a_ref, b_ref, c_ref, left_ref, right_ref, small_ref, weights_ref, smalls_ref):
    a, b, c = a_ref[0], b_ref[0], c_ref[0]
    tail = jnp.concatenate([b[:, 256:], c[:, :256]], axis=1)
    left = jnp.dot(
        left_ref[...],
        jnp.concatenate([a[:, :384], tail], axis=0),
        preferred_element_type=jnp.float32,
    )
    right = jnp.dot(
        right_ref[...],
        jnp.concatenate([jnp.concatenate([a[:, 384:], b[:, :256]], axis=1), tail], axis=0),
        preferred_element_type=jnp.float32,
    )
    for weight in range(4):
        rows = slice(weight * 48, weight * 48 + 48)
        weights_ref[weight, :, :384] = left[rows].astype(jnp.bfloat16)
        weights_ref[weight, :, 384:] = right[rows].astype(jnp.bfloat16)
    smalls_ref[...] = jnp.dot(
        small_ref[...], c[:, 256:], preferred_element_type=jnp.float32
    ).astype(jnp.bfloat16)


def unpack_shards(parts):
    left, right, small = (jnp.asarray(t, jnp.bfloat16) for t in placing_tables())
    whole = lambda t: pl.BlockSpec(t.shape, lambda g: (0, 0))
    return pl.pallas_call(
        unpack_kernel,
        grid=(16,),
        out_shape=[
            jax.ShapeDtypeStruct((4, WIDTH, WIDTH), jnp.bfloat16),
            jax.ShapeDtypeStruct((WIDTH, 128), jnp.bfloat16),
        ],
        in_specs=[
            *(pl.BlockSpec((1, 128, lanes), lambda g: (g, 0, 0)) for lanes in PART_LANES),
            whole(left),
            whole(right),
            whole(small),
        ],
        out_specs=[
            pl.BlockSpec((4, 48, WIDTH), lambda g: (0, g, 0)),
            pl.BlockSpec((48, 128), lambda g: (g, 0)),
        ],
        name="unpack_shards",
        compiler_params=pltpu.CompilerParams(vmem_limit_bytes=24 * 2**20),
    )(*(part.reshape(16, 128, -1) for part in parts), left, right, small)


def pack_kernel(weights_ref, smalls_ref, left_ref, right_ref, small_ref, out_ref):
    left = jnp.concatenate([weights_ref[w, :, :384] for w in range(4)], axis=0).astype(jnp.bfloat16)
    right = jnp.concatenate([weights_ref[w, :, 384:] for w in range(4)], axis=0).astype(jnp.bfloat16)
    from_left = jnp.dot(left_ref[...], left, preferred_element_type=jnp.float32)
    from_right = jnp.dot(right_ref[...], right, preferred_element_type=jnp.float32)
    out_ref[0, :, :384] = from_left[:128].astype(jnp.bfloat16)
    out_ref[0, :, 384:768] = from_right[:128].astype(jnp.bfloat16)
    out_ref[0, :, 768:1152] = (from_left[128:] + from_right[128:]).astype(jnp.bfloat16)
    out_ref[0, :, 1152:] = jnp.dot(
        small_ref[...], smalls_ref[...].astype(jnp.bfloat16), preferred_element_type=jnp.float32
    ).astype(jnp.bfloat16)


def pack_shards(weights, smalls):
    left, right, small = (jnp.asarray(t.T, jnp.bfloat16) for t in placing_tables())
    whole = lambda t: pl.BlockSpec(t.shape, lambda g: (0, 0))
    return pl.pallas_call(
        pack_kernel,
        grid=(16,),
        out_shape=jax.ShapeDtypeStruct((16, 128, 1280), jnp.bfloat16),
        in_specs=[
            pl.BlockSpec((4, 48, WIDTH), lambda g: (0, g, 0)),
            pl.BlockSpec((48, 128), lambda g: (g, 0)),
            whole(left),
            whole(right),
            whole(small),
        ],
        out_specs=pl.BlockSpec((1, 128, 1280), lambda g: (g, 0, 0)),
        name="pack_shards",
        compiler_params=pltpu.CompilerParams(vmem_limit_bytes=24 * 2**20),
    )(weights, smalls, left, right, small).reshape(4, 4, 4, 2, 16, 1280)


def pack_own(weights, smalls):
    rows = jnp.concatenate(weights, axis=0)
    tail = jnp.concatenate([rows[16:, :384], rows[16:, 384:]], axis=0)
    small = jnp.pad(jnp.concatenate(smalls, axis=1), ((0, 10), (0, 108)))
    return jnp.concatenate([rows[:16], tail, small], axis=1)


def unpack_own(packed):
    tail = jnp.concatenate([packed[:8, 768:1152], packed[8:, 768:1152]], axis=1)
    rows = jnp.concatenate([packed[:16, :768], tail], axis=0)
    small = packed[:6, 1152:]
    return [rows[i * 6 : i * 6 + 6] for i in range(4)], small


def rope_tables():
    frequency = 10000.0 ** (-2.0 * (np.arange(128) % 32) / HDIM)
    inner = np.arange(BLK)[:, None] * frequency
    outer = (np.arange(8) * BLK)[:, None] * frequency
    return [jnp.asarray(t, jnp.float32) for t in (np.cos(inner), np.sin(inner), np.cos(outer), np.sin(outer))]


def turning(index, tables):
    cos_in, sin_in, cos_out, sin_out = tables
    ca, sa = cos_out[pl.ds(index, 1), :], sin_out[pl.ds(index, 1), :]
    cb, sb = cos_in[...], sin_in[...]
    lower = lax.broadcasted_iota(jnp.int32, (BLK, 128), 1) % HDIM < HDIM // 2
    sine = sa * cb + ca * sb
    return ca * cb - sa * sb, jnp.where(lower, -sine, sine)


def swapped(values):
    lower = lax.broadcasted_iota(jnp.int32, values.shape, 1) % HDIM < HDIM // 2
    return jnp.where(lower, pltpu.roll(values, 96, 1), pltpu.roll(values, 32, 1))


def dot(left, right):
    return jnp.dot(left, right, preferred_element_type=jnp.float32)


def dot_nt(left, right):
    return lax.dot_general(left, right, (((1,), (1,)), ((), ())), preferred_element_type=jnp.float32)


def column(row):
    return jnp.broadcast_to(row, (128, row.shape[1])).T[:, 0:1]


def blocks_back(segs_ref, ctx):
    first = segs_ref[ctx, 0]
    count = jnp.int32(0)
    for index in range(8):
        count = count + jnp.where((index < ctx) & (segs_ref[index, BLK - 1] == first), 1, 0)
    return count


def mask_bias(segments_ref, bias_ref, ctx, index):
    key_seg = column(segments_ref[pl.ds(index, 1), :])
    query_seg = segments_ref[pl.ds(ctx, 1), :]
    key_pos = lax.broadcasted_iota(jnp.int32, (BLK, BLK), 0)
    query_pos = lax.broadcasted_iota(jnp.int32, (BLK, BLK), 1)
    reach = jnp.where(index == ctx, 0, BLK)
    allowed = (key_seg == query_seg) & (key_pos <= query_pos + reach)
    bias_ref[...] = jnp.where(allowed, 0.0, masked_score)


def rms_rows(values):
    return lax.rsqrt(jnp.mean(values * values, axis=-1, keepdims=True) + epsilon)


def pick(onehot, values):
    return jnp.sum(jnp.where(onehot, values, 0.0), axis=1, keepdims=True)


def lane_is(lanes):
    return lax.broadcasted_iota(jnp.int32, (BLK, 128), 1) == lanes


def forward_kernel(
    segs_ref, segments_ref, tok_ref, w_ref, small_ref, cos_in, sin_in, cos_out, sin_out,
    prev_ref, wres_ref, routes_ref, rank_ref, cot_ref,
    state_ref, normed_ref, att_ref, lse_ref, q_ref, keys_ref, values_ref, rows_ref, grads_ref,
    info_ref, proj_ref,
    qt_ref, vt_ref, bias_ref, max_ref, sum_ref, acc_ref,
):
    tables = (cos_in, sin_in, cos_out, sin_out)
    ctx = lax.axis_index("ctx")
    back = blocks_back(segs_ref, ctx)
    across = small_ref[...].astype(jnp.float32).T
    gain_one, gain_two = across[18:19], across[19:20]

    def normed_block(index):
        wide = tok_ref[index, :BLK].astype(jnp.float32)
        return (wide * rms_rows(wide) * gain_one).astype(jnp.bfloat16)

    query = dot(normed_block(ctx), w_ref[0])
    cosine, sine = turning(ctx, tables)
    for pair in range(PAIRS):
        part = query[:, pair * 128 : pair * 128 + 128]
        turned = (part * cosine + swapped(part) * sine) * (HDIM**-0.5)
        q_ref[pair] = turned.astype(jnp.bfloat16)
        across_q = turned.T.astype(jnp.bfloat16)
        blank = jnp.zeros((HDIM, BLK), jnp.bfloat16)
        qt_ref[2 * pair] = jnp.concatenate([across_q[:HDIM], blank], axis=0)
        qt_ref[2 * pair + 1] = jnp.concatenate([blank, across_q[HDIM:]], axis=0)
    max_ref[...] = jnp.full(max_ref.shape, masked_score, jnp.float32)
    sum_ref[...] = jnp.zeros_like(sum_ref)
    acc_ref[...] = jnp.zeros_like(acc_ref)

    def block(step, carry):
        index = ctx - step
        normed = normed_block(index)
        key = dot(normed, w_ref[1])
        value = dot(normed, w_ref[2])
        cosine, sine = turning(index, tables)
        for pair in range(PAIRS):
            lanes = slice(pair * 128, pair * 128 + 128)
            part = key[:, lanes]
            keys_ref[index, pair] = (part * cosine + swapped(part) * sine).astype(jnp.bfloat16)
            values_ref[index, pair] = value[:, lanes].astype(jnp.bfloat16)
            vt_ref[lanes, :] = value[:, lanes].T.astype(jnp.bfloat16)
        mask_bias(segments_ref, bias_ref, ctx, index)
        for head in range(HEADS):
            rows = slice(head * HDIM, head * HDIM + HDIM)
            scores = dot(keys_ref[index, head // 2], qt_ref[head]) + bias_ref[...]
            before = max_ref[head : head + 1]
            top = jnp.maximum(before, jnp.max(scores, axis=0, keepdims=True))
            weights = jnp.exp(scores - top)
            shrink = jnp.exp(before - top)
            sum_ref[head : head + 1] = sum_ref[head : head + 1] * shrink + jnp.sum(
                weights, axis=0, keepdims=True
            )
            max_ref[head : head + 1] = top
            acc_ref[rows] = acc_ref[rows] * shrink + dot(vt_ref[rows, :], weights.astype(jnp.bfloat16))
        return carry

    lax.fori_loop(0, back + 1, block, 0)
    for head in range(HEADS):
        rows = slice(head * HDIM, head * HDIM + HDIM)
        att_ref[rows] = acc_ref[rows] / sum_ref[head : head + 1]
    lse_ref[...] = max_ref[...] + jnp.log(jnp.maximum(sum_ref[...], 1e-30))
    attended = att_ref[...].T.astype(jnp.bfloat16)
    state = tok_ref[ctx, :BLK].astype(jnp.float32) + dot(attended, w_ref[3])
    state_ref[...] = state
    normed_two = (state * rms_rows(state) * gain_two).astype(jnp.bfloat16)
    normed_ref[...] = normed_two

    proj = dot(normed_two, small_ref[...])
    proj_ref[...] = proj
    logits = proj + jnp.dot(
        prev_ref[...], wres_ref[...], precision=highest, preferred_element_type=jnp.float32
    )
    lanes = lax.broadcasted_iota(jnp.int32, (BLK, 128), 1)
    route_0, route_1 = routes_ref[:, 0:1], routes_ref[:, 1:2]
    hot_0, hot_1 = lanes == route_0, lanes == route_1
    chosen_0, chosen_1 = pick(hot_0, logits), pick(hot_1, logits)
    top = jnp.maximum(chosen_0, chosen_1)
    chosen_0, chosen_1 = jnp.exp(chosen_0 - top), jnp.exp(chosen_1 - top)
    gate_0, gate_1 = chosen_0 / (chosen_0 + chosen_1), chosen_1 / (chosen_0 + chosen_1)
    rank = rank_ref[...]
    earlier = (rank < column(rank)).astype(jnp.float32).astype(jnp.bfloat16)
    slots = dot(earlier, (hot_0 | hot_1).astype(jnp.float32).astype(jnp.bfloat16))

    def target(route, hot):
        slot = pick(hot, slots)
        return jnp.where(
            (route < EXPERTS) & (slot < CAP), route.astype(jnp.float32) * SLOTS + slot, -1.0
        )

    target_0, target_1 = target(route_0, hot_0), target(route_1, hot_1)
    info = jnp.where(lanes == 0, gate_0, 0.0) + jnp.where(lanes == 1, gate_1, 0.0)
    info = info + jnp.where(lanes == 2, target_0, 0.0) + jnp.where(lanes == 3, target_1, 0.0)
    info_ref[...] = info
    targets = info.T
    rows = lax.broadcasted_iota(jnp.int32, (EXPERTS * SLOTS, BLK), 0).astype(jnp.float32)
    table_0 = (rows == targets[2:3]).astype(jnp.float32).astype(jnp.bfloat16)
    table_1 = (rows == targets[3:4]).astype(jnp.float32).astype(jnp.bfloat16)
    rows_ref[...] = dot(table_0 + table_1, normed_two).astype(jnp.bfloat16)
    upstream = cot_ref[...].astype(jnp.float32)
    grads_ref[...] = dot(
        jnp.concatenate([table_0, table_1], axis=1),
        jnp.concatenate([gate_0 * upstream, gate_1 * upstream], axis=0).astype(jnp.bfloat16),
    ).astype(jnp.bfloat16)


def attend(segs, segments, tok, weights, smalls, prev, wres, routes, rank, cot):
    vmem = pl.BlockSpec(memory_space=pltpu.VMEM)
    shape = jax.ShapeDtypeStruct
    low, wide = jnp.bfloat16, jnp.float32
    return pl.pallas_call(
        forward_kernel,
        out_shape=[
            shape((BLK, WIDTH), wide),
            shape((BLK, WIDTH), low),
            shape((WIDTH, BLK), wide),
            shape((16, BLK), wide),
            shape((PAIRS, BLK, 128), low),
            shape((8, PAIRS, BLK, 128), low),
            shape((8, PAIRS, BLK, 128), low),
            shape((EXPERTS * SLOTS, WIDTH), low),
            shape((EXPERTS * SLOTS, WIDTH), low),
            shape((BLK, 128), wide),
            shape((BLK, 128), wide),
        ],
        in_specs=[pl.BlockSpec(memory_space=pltpu.SMEM)] + [vmem] * 13,
        out_specs=[vmem] * 11,
        scratch_shapes=[
            pltpu.VMEM((HEADS, 128, BLK), low),
            pltpu.VMEM((WIDTH, BLK), low),
            pltpu.VMEM((BLK, BLK), wide),
            pltpu.VMEM((16, BLK), wide),
            pltpu.VMEM((16, BLK), wide),
            pltpu.VMEM((WIDTH, BLK), wide),
        ],
        name="attend",
        compiler_params=pltpu.CompilerParams(vmem_limit_bytes=48 * 2**20),
        cost_estimate=pl.CostEstimate(flops=3 * 10**10, bytes_accessed=10**7, transcendentals=10**6),
    )(segs, segments, tok, weights, smalls, *rope_tables(), prev, wres, routes, rank, cot)


def split(values):
    high = values.astype(jnp.bfloat16)
    low = (values - high.astype(jnp.float32)).astype(jnp.bfloat16)
    return jnp.concatenate([high, low], axis=1)


def backward_kernel(
    segs_ref, segments_ref, tok_ref, w_ref, small_ref, cos_in, sin_in, cos_out, sin_out,
    prev_ref, wres_ref, routes_ref, cot_ref,
    state_ref, normed_ref, att_ref, lse_ref, q_ref, keys_ref, values_ref, info_ref, proj_ref,
    back_rows_ref, back_grads_ref,
    out_ref, prev_grad_ref, res_grad_ref, dw_ref, dsmall_ref, others_ref, own_ref, state_grad_ref,
    qt_ref, ot_ref, o_ref, qm_ref, bias_ref, inner_ref, dqt_ref, gain_ref, dk_ref, dv_ref,
):
    tables = (cos_in, sin_in, cos_out, sin_out)
    ctx = lax.axis_index("ctx")
    back = blocks_back(segs_ref, ctx)
    across = small_ref[...].astype(jnp.float32).T
    gain_one, gain_two = across[18:19], across[19:20]
    value_rows = across[16:18]

    lanes = lax.broadcasted_iota(jnp.int32, (BLK, 128), 1)
    info = info_ref[...]
    gates = (info[:, 0:1], info[:, 1:2])
    slots = lax.broadcasted_iota(jnp.int32, (BLK, EXPERTS * SLOTS), 1).astype(jnp.float32)
    tables_of = [
        (slots == info[:, 2 + k : 3 + k]).astype(jnp.float32).astype(jnp.bfloat16) for k in (0, 1)
    ]
    routes = (routes_ref[:, 0:1], routes_ref[:, 1:2])
    hots = [lanes == routes[k] for k in (0, 1)]
    named = [
        [(routes[k] == EXPERTS + 1 + kind).astype(jnp.float32) for kind in range(3)] for k in (0, 1)
    ]
    proj = proj_ref[...]
    mixes = []
    for c in (0, 1):
        first, second = proj[:, 12 + 2 * c : 13 + 2 * c], proj[:, 13 + 2 * c : 14 + 2 * c]
        top = jnp.maximum(first, second)
        first, second = jnp.exp(first - top), jnp.exp(second - top)
        mixes.append((first / (first + second), second / (first + second)))
    normed_low = normed_ref[...]
    normed_two = normed_low.astype(jnp.float32)
    upstream_low = cot_ref[...]
    upstream = upstream_low.astype(jnp.float32)
    state = state_ref[...]
    back_rows = back_rows_ref[...]
    result = state
    gate_grads = []
    for k in (0, 1):
        copy, one, two = named[k]
        pair = dot(tables_of[k], back_rows)
        pair = pair + (copy + one * mixes[0][0] + two * mixes[1][0]) * normed_two
        pair = pair + (one * mixes[0][1]) * value_rows[0:1] + (two * mixes[1][1]) * value_rows[1:2]
        result = result + gates[k] * pair
        gate_grads.append(jnp.sum(pair * upstream, axis=1, keepdims=True))
    out_ref[...] = result.astype(jnp.bfloat16)
    inner = gates[0] * gate_grads[0] + gates[1] * gate_grads[1]
    logit_grad = jnp.zeros((BLK, 128), jnp.float32)
    for k in (0, 1):
        logit_grad = logit_grad + jnp.where(hots[k], gates[k] * (gate_grads[k] - inner), 0.0)
    prev_grad_ref[...] = lax.dot_general(
        logit_grad, wres_ref[...], (((1,), (1,)), ((), ())),
        precision=highest, preferred_element_type=jnp.float32,
    )
    res_grad_ref[...] = jnp.dot(
        prev_ref[...].T, logit_grad, precision=highest, preferred_element_type=jnp.float32
    )[:16]
    on_normed = jnp.sum(normed_two * upstream, axis=1, keepdims=True)
    on_vectors = dot(upstream_low, small_ref[...])
    flat = logit_grad
    weight_up = gates[0] * named[0][0] + gates[1] * named[1][0]
    vector_weights = jnp.zeros((BLK, 128), jnp.float32)
    for c in (0, 1):
        scale = gates[0] * named[0][1 + c] + gates[1] * named[1][1 + c]
        mix_0, mix_1 = mixes[c]
        m_0, m_1 = scale * on_normed, scale * on_vectors[:, 16 + c : 17 + c]
        mean = mix_0 * m_0 + mix_1 * m_1
        flat = flat + jnp.where(lanes == 12 + 2 * c, mix_0 * (m_0 - mean), 0.0)
        flat = flat + jnp.where(lanes == 13 + 2 * c, mix_1 * (m_1 - mean), 0.0)
        weight_up = weight_up + mix_0 * scale
        vector_weights = vector_weights + jnp.where(lanes == 16 + c, mix_1 * scale, 0.0)
    flat_split = split(flat)
    normed_grad = dot_nt(flat_split, jnp.concatenate([small_ref[...]] * 2, axis=1))
    normed_grad = normed_grad + weight_up * upstream
    normed_grad = normed_grad + dot(tables_of[0] + tables_of[1], back_grads_ref[...])
    normed_across = normed_two.T.astype(jnp.bfloat16)
    upstream_across = upstream.T.astype(jnp.bfloat16)
    small_grad = dot(normed_across, flat_split)
    small_vector = dot(upstream_across, split(vector_weights))
    small_grad = small_grad[:, :128] + small_grad[:, 128:] + small_vector[:, :128] + small_vector[:, 128:]
    scale_two = rms_rows(state)
    weighted = normed_grad * gain_two
    state_grad = (
        upstream
        + scale_two * weighted
        - state * (scale_two**3 * jnp.mean(weighted * state, axis=-1, keepdims=True))
    )
    state_grad_ref[...] = state_grad
    gain_two_row = jnp.sum(normed_grad * state * scale_two, axis=0, keepdims=True)
    state_low = state_grad.astype(jnp.bfloat16)
    attended = att_ref[...]
    dw_ref[3] = dot(attended.astype(jnp.bfloat16), state_low)
    att_grad = dot_nt(state_low, w_ref[3])
    blank = jnp.zeros((HDIM, BLK), jnp.bfloat16)
    low_half = lax.broadcasted_iota(jnp.int32, (BLK, 128), 1) < HDIM
    none = jnp.zeros((BLK, 128), jnp.bfloat16)
    inner_ref[...] = jnp.zeros_like(inner_ref)
    for pair in range(PAIRS):
        part = att_grad[:, pair * 128 : pair * 128 + 128].astype(jnp.bfloat16)
        across_o = part.astype(jnp.float32).T
        products = across_o * attended[pair * 128 : pair * 128 + 128]
        across_o = across_o.astype(jnp.bfloat16)
        across_q = q_ref[pair].astype(jnp.float32).T.astype(jnp.bfloat16)
        for half in (0, 1):
            head = 2 * pair + half
            rows = slice(half * HDIM, half * HDIM + HDIM)
            inner_ref[head : head + 1] = jnp.sum(products[rows], axis=0, keepdims=True)
            order = (lambda a, b: [a, b]) if half == 0 else (lambda a, b: [b, a])
            ot_ref[head] = jnp.concatenate(order(across_o[rows], blank), axis=0)
            qt_ref[head] = jnp.concatenate(order(across_q[rows], blank), axis=0)
        o_ref[pair, :BLK] = jnp.where(low_half, part, none)
        o_ref[pair, BLK:] = jnp.where(low_half, none, part)
        qm_ref[pair, :BLK] = jnp.where(low_half, q_ref[pair], none)
        qm_ref[pair, BLK:] = jnp.where(low_half, none, q_ref[pair])
    dqt_ref[...] = jnp.zeros_like(dqt_ref)
    dw_ref[1] = jnp.zeros((WIDTH, WIDTH), jnp.float32)
    dw_ref[2] = jnp.zeros((WIDTH, WIDTH), jnp.float32)
    gain_ref[...] = jnp.zeros_like(gain_ref)

    def normed_block(index):
        wide = tok_ref[index, :BLK].astype(jnp.float32)
        scaled = wide * rms_rows(wide)
        return scaled, (scaled * gain_one).T.astype(jnp.bfloat16)

    def block(step, carry):
        index = ctx - step
        mask_bias(segments_ref, bias_ref, ctx, index)
        cosine, sine = turning(index, tables)
        for pair in range(PAIRS):
            key, value = keys_ref[index, pair], values_ref[index, pair]
            key_across = key.astype(jnp.float32).T.astype(jnp.bfloat16)
            weights, score_grads = [], []
            for half in (0, 1):
                head = 2 * pair + half
                scores = dot(key, qt_ref[head]) + bias_ref[...]
                weight = jnp.exp(scores - lse_ref[head : head + 1])
                weight_grad = dot(value, ot_ref[head])
                score_grad = (weight * (weight_grad - inner_ref[head : head + 1])).astype(jnp.bfloat16)
                weights.append(weight.astype(jnp.bfloat16))
                score_grads.append(score_grad)
                rows = slice(head * HDIM, head * HDIM + HDIM)
                dqt_ref[rows] += dot(key_across[half * HDIM : half * HDIM + HDIM], score_grad)
            lanes = slice(pair * 128, pair * 128 + 128)
            dv_ref[:, lanes] = dot(jnp.concatenate(weights, axis=1), o_ref[pair]).astype(jnp.bfloat16)
            dk = dot(jnp.concatenate(score_grads, axis=1), qm_ref[pair])
            dk_ref[:, lanes] = (dk * cosine - swapped(dk) * sine).astype(jnp.bfloat16)
        scaled, normed_across = normed_block(index)
        dw_ref[1] += dot(normed_across, dk_ref[...])
        dw_ref[2] += dot(normed_across, dv_ref[...])
        first = dot_nt(dk_ref[...], w_ref[1]) + dot_nt(dv_ref[...], w_ref[2])
        gain_ref[...] += jnp.sum(first * scaled, axis=0, keepdims=True)
        others_ref[index] = first.astype(jnp.bfloat16)

        @pl.when(step == 0)
        def _():
            own_ref[...] = first

        return carry

    lax.fori_loop(0, back + 1, block, 0)

    def clear(index, carry):
        others_ref[index] = jnp.zeros((BLK, WIDTH), jnp.bfloat16)
        return carry

    lax.fori_loop(0, ctx - back, clear, 0)
    cosine, sine = turning(ctx, tables)
    for pair in range(PAIRS):
        lanes = slice(pair * 128, pair * 128 + 128)
        dq = dqt_ref[lanes, :].T * (HDIM**-0.5)
        dk_ref[:, lanes] = (dq * cosine - swapped(dq) * sine).astype(jnp.bfloat16)
    scaled, normed_across = normed_block(ctx)
    dw_ref[0] = dot(normed_across, dk_ref[...])
    first = dot_nt(dk_ref[...], w_ref[0])
    own_ref[...] += first
    gain_one_row = gain_ref[...] + jnp.sum(first * scaled, axis=0, keepdims=True)
    lanes = lax.broadcasted_iota(jnp.int32, (WIDTH, 128), 1)
    ones = jnp.broadcast_to(gain_one_row, (128, WIDTH)).T
    twos = jnp.broadcast_to(gain_two_row, (128, WIDTH)).T
    dsmall_ref[...] = jnp.where(lanes == 18, ones, jnp.where(lanes == 19, twos, small_grad))


def unattend(segs, segments, tok, weights, smalls, prev, wres, routes, cot, kept, back_rows, back_grads):
    vmem = pl.BlockSpec(memory_space=pltpu.VMEM)
    shape = jax.ShapeDtypeStruct
    low, wide = jnp.bfloat16, jnp.float32
    state, normed, att, lse, q, keys, values, info, proj = kept
    return pl.pallas_call(
        backward_kernel,
        out_shape=[
            shape((BLK, WIDTH), low),
            shape((BLK, 128), wide),
            shape((16, 128), wide),
            shape((4, WIDTH, WIDTH), wide),
            shape((WIDTH, 128), wide),
            shape((8, BLK, WIDTH), low),
            shape((BLK, WIDTH), wide),
            shape((BLK, WIDTH), wide),
        ],
        in_specs=[pl.BlockSpec(memory_space=pltpu.SMEM)] + [vmem] * 23,
        out_specs=[vmem] * 8,
        scratch_shapes=[
            pltpu.VMEM((HEADS, 128, BLK), low),
            pltpu.VMEM((HEADS, 128, BLK), low),
            pltpu.VMEM((PAIRS, 2 * BLK, 128), low),
            pltpu.VMEM((PAIRS, 2 * BLK, 128), low),
            pltpu.VMEM((BLK, BLK), wide),
            pltpu.VMEM((16, BLK), wide),
            pltpu.VMEM((WIDTH, BLK), wide),
            pltpu.VMEM((1, WIDTH), wide),
            pltpu.VMEM((BLK, WIDTH), low),
            pltpu.VMEM((BLK, WIDTH), low),
        ],
        name="unattend",
        compiler_params=pltpu.CompilerParams(vmem_limit_bytes=56 * 2**20),
        cost_estimate=pl.CostEstimate(flops=4 * 10**10, bytes_accessed=10**7, transcendentals=10**6),
    )(
        segs, segments, tok, weights, smalls, *rope_tables(), prev, wres, routes, cot,
        state, normed, att, lse, q, keys, values, info, proj, back_rows, back_grads,
    )


def dot_tn(left, right):
    return lax.dot_general(left, right, (((0,), (0,)), ((), ())), preferred_element_type=jnp.float32)


def experts_kernel(
    rows_ref, grads_ref, gate_up_ref, down_ref,
    back_rows_ref, back_grads_ref, d_gate_up_ref, d_down_ref,
    gate_w, up_w, down_w, x_ref, g_ref, gate_ref, up_ref, hidden_ref, d_gate, d_up,
    mine_ref, twin_out, twin_in, sums_ref,
    load_sem, send_sem, recv_sem, share_send, share_recv, half_send, half_recv, ret_send, ret_recv,
    own_sem,
):
    ctx, fsdp = lax.axis_index("ctx"), lax.axis_index("fsdp")
    chip, core = fsdp // 2, fsdp % 2
    other = 1 - core
    half = EXPERTS * SLOTS

    def at(where, on):
        return {"ctx": ctx, "fsdp": where * 2 + on}

    greet([at((chip + by) % EXPERTS, core) for by in range(1, EXPERTS)] + [at(chip, other)])
    loads = []
    for index in range(8):
        for source, target, size in (
            (gate_up_ref.at[index, :96], gate_w, 96),
            (gate_up_ref.at[index, 96:], up_w, 96),
            (down_ref.at[index], down_w, 128),
        ):
            copy = pltpu.make_async_copy(
                source, target.at[pl.ds(index * size, size)], load_sem.at[len(loads)]
            )
            loads.append(copy)

    def slots(index, on):
        return pl.ds(pl.multiple_of((on * EXPERTS + index) * SLOTS, SLOTS), SLOTS)

    def chunk(index):
        return pl.ds(pl.multiple_of(index * SLOTS, SLOTS), SLOTS)

    buffers = ((rows_ref, x_ref), (grads_ref, g_ref))

    def dispatch(kind, by):
        source, target = buffers[kind]
        where = (chip + by) % EXPERTS
        return pltpu.make_async_remote_copy(
            src_ref=source.at[chunk(where)],
            dst_ref=target.at[slots(chip, core)],
            send_sem=send_sem.at[kind, by - 1],
            recv_sem=recv_sem.at[kind, by - 1],
            device_id=at(where, core),
            device_id_type=MESH,
        )

    def share(kind, by, on):
        source, target = buffers[kind]
        spot = slots((chip - by) % EXPERTS, on)
        return pltpu.make_async_remote_copy(
            src_ref=target.at[spot],
            dst_ref=target.at[spot],
            send_sem=share_send.at[kind, by],
            recv_sem=share_recv.at[kind, by],
            device_id=at(chip, other),
            device_id_type=MESH,
        )

    def exchange(kind):
        return pltpu.make_async_remote_copy(
            src_ref=twin_out.at[kind],
            dst_ref=twin_in.at[kind],
            send_sem=half_send.at[kind],
            recv_sem=half_recv.at[kind],
            device_id=at(chip, other),
            device_id_type=MESH,
        )

    returned = (back_rows_ref, back_grads_ref)

    def give_back(kind, by):
        where = (chip + by) % EXPERTS
        return pltpu.make_async_remote_copy(
            src_ref=sums_ref.at[kind, chunk(where)],
            dst_ref=returned[kind].at[chunk(chip)],
            send_sem=ret_send.at[kind, by - 1],
            recv_sem=ret_recv.at[kind, by - 1],
            device_id=at(where, core),
            device_id_type=MESH,
        )

    started = []
    for kind in (0, 1):
        for by in range(1, EXPERTS):
            copy = dispatch(kind, by)
            copy.start()
            started.append(copy)
    for copy in loads:
        copy.start()
    for kind in (0, 1):
        source, target = buffers[kind]
        copy = pltpu.make_async_copy(
            source.at[chunk(chip)], target.at[slots(chip, core)], own_sem.at[kind]
        )
        copy.start()
        copy.wait()
        copy = share(kind, 0, core)
        copy.start()
        started.append(copy)

    def arrive(kind):
        for by in range(1, EXPERTS):
            dispatch(kind, by).wait_recv()
            copy = share(kind, by, core)
            copy.start()
            started.append(copy)

    def arrive_shared(kind):
        for by in range(EXPERTS):
            share(kind, by, other).wait_recv()

    def tiles(on, body):
        def step(index, carry):
            start = pl.multiple_of(on * half + index * 256, 256)
            body(pl.ds(start, 256), pl.ds(pl.multiple_of(index * 256, 256), 256))
            return carry

        lax.fori_loop(0, half // 256, step, 0)

    def forward(on, keep):
        def tile(rows, inner):
            x = x_ref[rows]
            gate, up = dot(x, gate_w[...]), dot(x, up_w[...])
            gate_ref[rows], up_ref[rows] = gate, up
            hidden = (gate * jax.nn.sigmoid(gate) * up).astype(jnp.bfloat16)
            hidden_ref[rows] = hidden
            keep(inner, dot(hidden, down_w[...]))

        tiles(on, tile)

    def backward(on, keep):
        def tile(rows, inner):
            hidden_grad = dot_nt(g_ref[rows], down_w[...])
            gate, up = gate_ref[rows], up_ref[rows]
            sigmoid = jax.nn.sigmoid(gate)
            d_gate[rows] = (
                hidden_grad * up * sigmoid * (1.0 + gate * (1.0 - sigmoid))
            ).astype(jnp.bfloat16)
            d_up[rows] = (hidden_grad * gate * sigmoid).astype(jnp.bfloat16)
            keep(inner, dot_nt(d_gate[rows], gate_w[...]) + dot_nt(d_up[rows], up_w[...]))

        tiles(on, tile)

    def keep_mine(kind):
        def keep(rows, values):
            mine_ref[kind, rows] = values

        return keep

    def keep_twin(kind):
        def keep(rows, values):
            twin_out[kind, rows] = values.astype(jnp.bfloat16)

        return keep

    def finish(kind):
        exchange(kind).wait_recv()

        def step(index, carry):
            rows = pl.ds(pl.multiple_of(index * 128, 128), 128)
            sums_ref[kind, rows] = (
                mine_ref[kind, rows] + twin_in[kind, rows].astype(jnp.float32)
            ).astype(jnp.bfloat16)
            return carry

        lax.fori_loop(0, half // 128, step, 0)
        for by in range(1, EXPERTS):
            copy = give_back(kind, by)
            copy.start()
            started.append(copy)
        copy = pltpu.make_async_copy(
            sums_ref.at[kind, chunk(chip)], returned[kind].at[chunk(chip)], own_sem.at[kind]
        )
        copy.start()
        copy.wait()

    arrive(0)
    for copy in loads:
        copy.wait()
    forward(core, keep_mine(0))
    arrive(1)
    arrive_shared(0)
    forward(other, keep_twin(0))
    copy = exchange(0)
    copy.start()
    started.append(copy)
    backward(core, keep_mine(1))
    finish(0)
    arrive_shared(1)
    backward(other, keep_twin(1))
    copy = exchange(1)
    copy.start()
    started.append(copy)

    def down_tile(index, carry):
        lanes = pl.ds(pl.multiple_of(index * 256, 256), 256)
        part = dot_tn(hidden_ref[:, lanes], g_ref[...]).astype(jnp.bfloat16)
        d_down_ref[2 * index] = part[:128]
        d_down_ref[2 * index + 1] = part[128:]
        return carry

    lax.fori_loop(0, 4, down_tile, 0)
    finish(1)

    def gate_tile(index, carry):
        lanes = pl.ds(pl.multiple_of(index * 256, 256), 256)
        for start, grad in ((0, d_gate), (96, d_up)):
            part = dot_tn(x_ref[...], grad[:, lanes]).astype(jnp.bfloat16)
            for piece in range(8):
                d_gate_up_ref[piece, start : start + 96, lanes] = part[piece * 96 : piece * 96 + 96]
        return carry

    lax.fori_loop(0, 4, gate_tile, 0)
    for kind in (0, 1):
        for by in range(1, EXPERTS):
            give_back(kind, by).wait_recv()
    for copy in started:
        copy.wait_send()


def run_experts(rows, grads, gate_up, down):
    vmem, anywhere = pl.BlockSpec(memory_space=pltpu.VMEM), pl.BlockSpec(memory_space=pl.ANY)
    low, wide = jnp.bfloat16, jnp.float32
    half, whole = EXPERTS * SLOTS, 2 * EXPERTS * SLOTS
    dma = pltpu.SemaphoreType.DMA
    return pl.pallas_call(
        experts_kernel,
        out_shape=[
            jax.ShapeDtypeStruct((half, WIDTH), low),
            jax.ShapeDtypeStruct((half, WIDTH), low),
            jax.ShapeDtypeStruct((8, 192, 1024), low),
            jax.ShapeDtypeStruct((8, 128, WIDTH), low),
        ],
        in_specs=[vmem, vmem, anywhere, anywhere],
        out_specs=[vmem] * 4,
        scratch_shapes=[
            pltpu.VMEM((WIDTH, 1024), low),
            pltpu.VMEM((WIDTH, 1024), low),
            pltpu.VMEM((1024, WIDTH), low),
            pltpu.VMEM((whole, WIDTH), low),
            pltpu.VMEM((whole, WIDTH), low),
            pltpu.VMEM((whole, 1024), wide),
            pltpu.VMEM((whole, 1024), wide),
            pltpu.VMEM((whole, 1024), low),
            pltpu.VMEM((whole, 1024), low),
            pltpu.VMEM((whole, 1024), low),
            pltpu.VMEM((2, half, WIDTH), wide),
            pltpu.VMEM((2, half, WIDTH), low),
            pltpu.VMEM((2, half, WIDTH), low),
            pltpu.VMEM((2, half, WIDTH), low),
            dma((24,)),
            dma((2, 7)),
            dma((2, 7)),
            dma((2, 8)),
            dma((2, 8)),
            dma((2,)),
            dma((2,)),
            dma((2, 7)),
            dma((2, 7)),
            dma((2,)),
        ],
        name="run_experts",
        compiler_params=pltpu.CompilerParams(
            collective_id=3, has_side_effects=True, vmem_limit_bytes=56 * 2**20
        ),
    )(rows, grads, gate_up, down)


def over_ctx(array):
    return lax.all_to_all(jnp.broadcast_to(array[None], (8, *array.shape)), "ctx", 0, 0, tiled=True)


def on_device(
    tokens, prev_logits, routes, segments, rank_order, norm_first, w_query, w_key, w_value, w_output,
    norm_second, w_router, w_residual, w_constant, v_constant, w_gate, w_up, w_down, cotangent,
):
    own = pack_own(
        [w_query, w_key, w_value, w_output],
        [w_router, w_constant, v_constant, norm_first[:, None], norm_second[:, None]],
    )
    marks = jnp.pad(segments.astype(jnp.bfloat16), ((0, 15), (0, WIDTH - BLK)))
    *parts, blocks = gather_shards(own, jnp.concatenate([tokens[0], marks], axis=0))
    gate_up, down = jnp.concatenate([w_gate[0], w_up[0]], axis=0), w_down[0]
    gate_up, down, parts = lax.optimization_barrier((gate_up, down, parts))
    gate_up, down = over_ctx(gate_up), over_ctx(down)
    weights, smalls = unpack_shards(parts)
    seg_wide = blocks[:, BLK, :BLK].astype(jnp.float32)
    seg_int = seg_wide.astype(jnp.int32)
    prev = jnp.pad(prev_logits[0], ((0, 0), (0, 116)))
    wres = jnp.pad(w_residual, ((0, 116), (0, 116)))
    state, normed, att, lse, q, keys, values, rows, grads, info, proj = attend(
        seg_int, seg_wide, blocks, weights, smalls, prev, wres, routes[0],
        rank_order[0].astype(jnp.float32), cotangent[0],
    )
    returned, returned_grad, d_gate_up, d_down = run_experts(rows, grads, gate_up, down)

    def sum_over_ctx(array):
        return jnp.sum(lax.all_to_all(array, "ctx", 0, 0, tiled=True).astype(jnp.float32), axis=0)

    gate_up_sum, down_sum = sum_over_ctx(d_gate_up), sum_over_ctx(d_down)
    out, prev_grad, res_grad, dw, dsmall, others, first, state_grad = unattend(
        seg_int, seg_wide, blocks, weights, smalls, prev, wres, routes[0], cotangent[0],
        (state, normed, att, lse, q, keys, values, info, proj), returned, returned_grad,
    )
    summed, residual_total, tokens_grad = scatter_shards(
        pack_shards(dw, dsmall), res_grad, others, first, state_grad, tokens[0],
        smalls[:, 18].astype(jnp.float32)[None],
    )
    (sum_query, sum_key, sum_value, sum_output), small_sum = unpack_own(summed)
    return (
        out[None],
        tokens_grad[None],
        prev_grad[None, :, :12],
        small_sum[:, 18],
        sum_query,
        sum_key,
        sum_value,
        sum_output,
        small_sum[:, 19],
        small_sum[:, :12],
        residual_total[:12, :12],
        small_sum[:, 12:16],
        small_sum[:, 16:18],
        gate_up_sum[None, :96],
        gate_up_sum[None, 96:],
        down_sum[None],
    )


def solution(mesh):
    in_specs = (
        P("fsdp", "ctx", None),
        P("fsdp", "ctx", None),
        P("fsdp", "ctx", None),
        P("fsdp", "ctx"),
        P("fsdp", "ctx", None),
        P(("ctx", "fsdp")),
        P(("ctx", "fsdp"), None),
        P(("ctx", "fsdp"), None),
        P(("ctx", "fsdp"), None),
        P(("ctx", "fsdp"), None),
        P(("ctx", "fsdp")),
        P(("ctx", "fsdp"), None),
        P(),
        P(("ctx", "fsdp"), None),
        P(("ctx", "fsdp"), None),
        P("fsdp", "ctx", None),
        P("fsdp", "ctx", None),
        P("fsdp", "ctx", None),
        P("fsdp", "ctx", None),
    )
    out_specs = (
        P("fsdp", "ctx", None),
        P("fsdp", "ctx", None),
        P("fsdp", "ctx", None),
        P(("ctx", "fsdp")),
        P(("ctx", "fsdp"), None),
        P(("ctx", "fsdp"), None),
        P(("ctx", "fsdp"), None),
        P(("ctx", "fsdp"), None),
        P(("ctx", "fsdp")),
        P(("ctx", "fsdp"), None),
        P(),
        P(("ctx", "fsdp"), None),
        P(("ctx", "fsdp"), None),
        P("fsdp", "ctx", None),
        P("fsdp", "ctx", None),
        P("fsdp", "ctx", None),
    )
    return jax.shard_map(
        on_device, mesh=mesh, in_specs=in_specs, out_specs=out_specs, check_vma=False
    )
```

time: 732 us -> 382 us (0.52); the launches traced: 718 us -> 379 us
  waiting for transfers between devices: 189 us -> 45.7 us
  matrix products: 133 us -> 0 us
  Pallas kernels: 126 us -> 252 us
  local copies, waits for them, and re-layouts: 134 us -> 33.7 us
  starting transfers between devices: 90.1 us -> 36.4 us
  other arithmetic: 44.3 us -> 10.1 us
    dot_general x56 -> x0, matrix products: 133 us -> none  [the longest x3 15.9 us: grad_body(): jnp.einsum('hqk,qhd->khd', weights.astype(jnp.bfloat16), attended_grad, p...]
    pallas_call x0 -> x3, Pallas kernels: none -> 100 us  [the longest x1 55.5 us: run_experts(): pl.pallas_call(experts_kernel, out_shape=[jax.ShapeDtypeStruct((half, WID...]
    all_to_all x6 -> x2, waiting for transfers between devices: 111 us -> 19.6 us  [sum_over_ctx(): lax.all_to_all(array, 'ctx', 0, 0, tiled=True).astype(jnp.float32)]
    all_to_all x3 -> x2, waiting for transfers between devices: 78.3 us -> 26.1 us  [over_ctx(): lax.all_to_all(jnp.broadcast_to(array[None], (8, *array.shape)), 'ctx', 0...]
    all_to_all x6 -> x2, starting transfers between devices: 67.5 us -> 15.7 us  [sum_over_ctx(): lax.all_to_all(array, 'ctx', 0, 0, tiled=True).astype(jnp.float32)]
    pallas_call x1, Pallas kernels: 30.4 us -> 82.1 us  [scatter_shards(): pl.pallas_call(scatter_kernel, out_shape=[jax.ShapeDtypeStruct((16, 1280)...]
    pallas_call x1, Pallas kernels: 85 us -> 59.7 us  [gather_shards(): pl.pallas_call(gather_kernel, out_shape=[jax.ShapeDtypeStruct((4, 4, 4, 2...]
    another operation x9 -> x0, local copies, waits for them, and re-layouts: 21.9 us -> none  [the longest x1 5.97 us: on_device(): value_blocks = values_all.reshape(block_count, key_block, HEADS, HDIM)]
  transfers between devices with their start and end apart: 9 -> 4, of which waited for: 6 -> 3; matrix products, arithmetic and copies ran while one was open for 25% -> 3% of each run, Pallas kernels for 12% -> 36%
where the time goes in v2:
time: 382 us; the launch traced here: 379 us
  Pallas kernels  252 us (66%)
  waiting for transfers between devices  45.7 us (12%)
  starting transfers between devices  36.4 us (10%)
  local copies, waits for them, and re-layouts  33.7 us (9%)
  other arithmetic  10.1 us (3%)
    pallas_call x1, Pallas kernels, scatter_shards(): pl.pallas_call(scatter_kernel, out_shape=[jax.ShapeDtypeStruct((16, 1280)...  82.1 us
    pallas_call x1, Pallas kernels, gather_shards(): pl.pallas_call(gather_kernel, out_shape=[jax.ShapeDtypeStruct((4, 4, 4, 2...  59.7 us
    pallas_call x1, Pallas kernels, run_experts(): pl.pallas_call(experts_kernel, out_shape=[jax.ShapeDtypeStruct((half, WID...  55.5 us
    pallas_call x1, Pallas kernels, unattend(): pl.pallas_call(backward_kernel, out_shape=[shape((BLK, WIDTH), low), shap...  28.2 us
    all_to_all x2, waiting for transfers between devices, over_ctx(): lax.all_to_all(jnp.broadcast_to(array[None], (8, *array.shape)), 'ctx', 0...  26.1 us
    all_to_all x2, starting transfers between devices, over_ctx(): lax.all_to_all(jnp.broadcast_to(array[None], (8, *array.shape)), 'ctx', 0...  20.7 us
    unnamed x93, local copies, waits for them, and re-layouts  19.9 us
    all_to_all x2, waiting for transfers between devices, sum_over_ctx(): lax.all_to_all(array, 'ctx', 0, 0, tiled=True).astype(jnp.float32)  19.6 us
  transfers between devices with their start and end apart: 4, of which 3 were waited for; matrix products, arithmetic and copies ran while one was open for 3% of the time, Pallas kernels for 36%

profile of v2, /device:TPU:4, one launch (start us, length us, event | category | flops | bytes accessed | tf_op | source)
XLA Modules:
  0.0 379.2 jit_solution(15536556844638167503)
XLA Ops:
  0.6 0.7 convert_element_type.43
  1.3 0.8 copy.59
  2.1 0.8 copy.60
  2.9 0.8 copy.61
  3.6 0.8 copy.62
  4.4 1.8 fusion.1.tokens_ref
  6.1 0.8 concatenate.32
  6.9 1.5 fusion.11.own_ref
  8.4 59.7 %gather_shards.1 = (bf16[4,4,4,2,16,512]{5,4,3,2,1,0:T(8,128)(2,1)}, bf16[4,4,4,2,16,384]{5,4,3,2,1,0:T(8,128)(2,1)}, bf16[4,4,4,2,16,384]{5,4,3,2,1,0:T(8,128)(2,1)}, bf16[8,272,768]{2,1,0:T(8,128)(2,1)}) custom-call(bf16[16,1280]{1,0:T(8,128)(2,1)} %fusion.11.own_ref, bf16[272,768]{1,0:T(8,128)(2,1)} %fusion.1.tokens_ref), custom_call_target="tpu_custom_call" | custom-call | tf_op jit(solution)/shard_map/gather_shards/pallas_call | solution.py:181
  68.0 1.1 pad_maximum_fusion
  69.1 2.2 broadcast_in_dim.40
  71.3 12.5 %all-to-all-start.1 = ((bf16[8,128,768]{2,1,0:T(8,128)(2,1)}), bf16[8,128,768]{2,1,0:T(8,128)(2,1)}, u32[]{:S(2)}, u32[]{:S(2)}) async-start(bf16[8,128,768]{2,1,0:T(8,128)(2,1)} %broadcast_in_dim.40), calls=%async_computation.1 | async-start | bytes 3145728 | tf_op jit(solution)/shard_map/all_to_all | solution.py:1264
  83.9 0.0 copy-start.16
  83.9 0.0 copy-start.17
  83.9 0.0 copy-start.20
  83.9 4.9 %copy.63 = bf16[8,272,768]{2,0,1:T(8,128)(2,1)} copy(bf16[8,272,768]{2,1,0:T(8,128)(2,1)} %get-tuple-element.53.tok_ref) | data formatting | bytes 6684672 | tf_op jit(solution)/shard_map/gather_shards/pallas_call | solution.py:181
  88.8 0.1 copy.64
  88.9 0.1 copy.65
  89.1 0.0 copy-done.39
  89.1 0.0 copy-start.15
  89.1 0.0 copy-start.18
  89.1 0.0 copy-done.2
  89.2 1.4 copy-done.4
  90.6 1.4 copy-done.5
  92.0 4.4 %unpack_shards.1 = (bf16[4,768,768]{2,1,0:T(8,128)(2,1)S(1)}, bf16[768,128]{1,0:T(8,128)(2,1)S(1)}) custom-call(bf16[16,128,512]{2,1,0:T(8,128)(2,1)S(1)} %bitcast.33, bf16[16,128,384]{2,1,0:T(8,128)(2,1)S(1)} %bitcast.36, bf16[16,128,384]{2,1,0:T(8,128)(2,1)S(1)} %bitcast.37, bf16[192,256]{1,0:T(8,128)(2,1)S(1)} %copy-done.16, ...), custom_call_target="tpu_custom_call" | custom-call | tf_op jit(solution)/shard_map/unpack_shards/pallas_call | solution.py:482
  96.4 2.2 copy-done.24
  98.6 0.7 fusion.20
  99.3 5.8 %all-to-all-done.1.down_ref = bf16[8,128,768]{2,1,0:T(8,128)(2,1)} async-done(((bf16[8,128,768]{2,1,0:T(8,128)(2,1)}), bf16[8,128,768]{2,1,0:T(8,128)(2,1)}, u32[]{:S(2)}, u32[]{:S(2)}) %all-to-all-start.1) | async-done | bytes 1572896 | tf_op jit(solution)/shard_map/all_to_all | solution.py:1264
  105.1 2.0 broadcast_in_dim.39
  107.2 0.0 copy-start.29
  107.2 8.2 %all-to-all-start = ((bf16[8,192,1024]{2,1,0:T(8,128)(2,1)}), bf16[8,192,1024]{2,1,0:T(8,128)(2,1)}, u32[]{:S(2)}, u32[]{:S(2)}) async-start(bf16[8,192,1024]{2,1,0:T(8,128)(2,1)} %broadcast_in_dim.39), calls=%async_computation | async-start | bytes 6291456 | tf_op jit(solution)/shard_map/all_to_all | solution.py:1264
  115.4 16.5 %attend.1 = (f32[256,768]{1,0:T(8,128)S(1)}, bf16[256,768]{1,0:T(8,128)(2,1)S(1)}, f32[768,256]{1,0:T(8,128)S(1)}, f32[16,256]{1,0:T(8,128)S(1)}, bf16[6,256,128...) custom-call(s32[8,256]{1,0:T(8,128)S(1)} %get-tuple-element.125.segs, ...), custom_call_target="tpu_custom_call" | custom-call | flops 30000001024 | bytes 10000000 | tf_op jit(solution)/shard_map/attend/pallas_call | solution.py:725
  131.9 0.9 copy-done.8
  132.8 0.9 copy-done.9
  133.8 0.9 copy-done.31
  134.7 0.7 copy-done.33
  135.4 0.6 copy-done.34
  136.1 0.6 copy-done.36
  136.7 20.3 %all-to-all-done.gate_up_ref = bf16[8,192,1024]{2,1,0:T(8,128)(2,1)} async-done(((bf16[8,192,1024]{2,1,0:T(8,128)(2,1)}), bf16[8,192,1024]{2,1,0:T(8,128)(2,1)}, u32[]{:S(2)}, u32[]{:S(2)}) %all-to-all-start) | async-done | bytes 3145760 | tf_op jit(solution)/shard_map/all_to_all | solution.py:1264
  156.9 55.5 %run_experts.1 = (bf16[512,768]{1,0:T(8,128)(2,1)}, bf16[512,768]{1,0:T(8,128)(2,1)}, bf16[8,192,1024]{2,1,0:T(8,128)(2,1)}, bf16[8,128,768]{2,1,0:T(8,128)(2,1)}) custom-call(bf16[512,768]{1,0:T(8,128)(2,1)} %copy-done.8, bf16[512,768]{1,0:T(8,128)(2,1)} %copy-done.9, bf16[8,192,1024]{2,1,0:T(8,128)(2,1)} %all-to-all-done.gate_up_ref, ...), custom_call_target="tpu_custom_call" | custom-call | tf_op jit(solution)/shard_map/run_experts/pallas_call | solution.py:1220
  212.5 7.5 %all-to-all-start.3 = ((bf16[8,128,768]{2,1,0:T(8,128)(2,1)}), bf16[8,128,768]{2,1,0:T(8,128)(2,1)S(1)}, u32[]{:S(2)}, u32[]{:S(2)}) async-start(bf16[8,128,768]{2,1,0:T(8,128)(2,1)} %get-tuple-element.89), calls=%async_computation.3 | async-start | bytes 3145728 | tf_op jit(solution)/shard_map/all_to_all | solution.py:1292
  220.0 0.2 convert_reduce_fusion.2
  220.3 19.6 %all-to-all-done.3 = bf16[8,128,768]{2,1,0:T(8,128)(2,1)S(1)} async-done(((bf16[8,128,768]{2,1,0:T(8,128)(2,1)}), bf16[8,128,768]{2,1,0:T(8,128)(2,1)S(1)}, u32[]{:S(2)}, u32[]{:S(2)}) %all-to-all-start.3) | async-done | bytes 1572896 | tf_op jit(solution)/shard_map/all_to_all | solution.py:1292
  239.9 8.2 %all-to-all-start.2 = ((bf16[8,192,1024]{2,1,0:T(8,128)(2,1)}), bf16[8,192,1024]{2,1,0:T(8,128)(2,1)}, u32[]{:S(2)}, u32[]{:S(2)}) async-start(bf16[8,192,1024]{2,1,0:T(8,128)(2,1)} %get-tuple-element.88), calls=%async_computation.2 | async-start | bytes 6291456 | tf_op jit(solution)/shard_map/all_to_all | solution.py:1292
  248.1 28.2 %unattend.1 = (bf16[256,768]{1,0:T(8,128)(2,1)}, f32[256,128]{1,0:T(8,128)}, f32[16,128]{1,0:T(8,128)}, f32[4,768,768]{2,1,0:T(8,128)}, f32[768,128]{1,0:T(8,128...) custom-call(s32[8,256]{1,0:T(8,128)} %copy-done.23, f32[8,256]{1,0:T(8,128)} %copy-done.22, ...), custom_call_target="tpu_custom_call" | custom-call | flops 40000000000 | bytes 10000000 | tf_op jit(solution)/shard_map/unattend/pallas_call | solution.py:953
  276.3 3.7 copy-done
  280.0 1.0 copy-done.10
  281.0 0.0 copy-start.21
  281.0 5.9 %pack_shards.1 = bf16[16,128,1280]{2,1,0:T(8,128)(2,1)S(1)} custom-call(f32[4,768,768]{2,1,0:T(8,128)S(1)} %copy-done, f32[768,128]{1,0:T(8,128)S(1)} %copy-done.10, bf16[256,192]{1,0:T(8,128)(2,1)S(1)} %copy-done.12, bf16[256,192]{1,0:T(8,128)(2,1)S(1)} %copy-done.13, bf16[128,48]{1,0:T(8,128)(2,1)S(1)} %copy-done.19), custom_call_target="tpu_custom_call" | custom-call | tf_op jit(solution)/shard_map/pack_shards/pallas_call | solution.py:520
  287.0 82.1 %scatter_shards.1 = (f32[16,1280]{1,0:T(8,128)S(1)}, f32[16,128]{1,0:T(8,128)S(1)}, f32[256,768]{1,0:T(8,128)S(1)}) custom-call(bf16[4,4,4,2,16,1280]{5,4,3,2,1,0:T(8,128)(2,1)S(1)} %bitcast.32, f32[16,128]{1,0:T(8,128)S(1)} %copy-done.21, bf16[8,256,768]{2,1,0:T(8,128)(2,1)S(1)} %copy-done.1, f32[256,768]{1,0:T(8,128)S(1)} %copy-done.6, ...), custom_call_target="tpu_custom_call" | custom-call | tf_op jit(solution)/shard_map/scatter_shards/pallas_call | solution.py:400
  369.2 0.1 slice.91
  369.2 0.1 slice.92
  369.3 0.6 slice.89
  369.9 0.7 copy.67
  370.6 0.6 copy.68
  371.2 0.7 copy.66
  371.9 0.7 slice_reduce_fusion
  372.6 0.6 pad_maximum_fusion.3
  373.3 1.0 convert_reduce_fusion.1
  374.2 0.0 all-to-all-done.2
  374.2 2.6 convert_reduce_fusion
  376.8 0.9 slice_bitcast_fusion
  377.8 0.9 copy.71
  378.6 0.6 copy.72
  (71 shorter events, 0.2 us)
Async XLA Ops:
  71.3 33.8 %all-to-all-start.1 = ((bf16[8,128,768]{2,1,0:T(8,128)(2,1)}), bf16[8,128,768]{2,1,0:T(8,128)(2,1)}, u32[]{:S(2)}, u32[]{:S(2)}) async-start(bf16[8,128,768]{2,1,0:T(8,128)(2,1)} %broadcast_in_dim.40), calls=%async_computation.1 | async-start | bytes 3145728 | tf_op jit(solution)/shard_map/all_to_all | solution.py:1264
  83.8 4.9 %copy-start.38 = (f32[1,256,12]{1,0,2:T(1,128)S(1)}, f32[1,256,12]{1,0,2:T(1,128)}, u32[]{:S(2)}) copy-start(f32[1,256,12]{1,0,2:T(1,128)} %param.34) | copy-start | bytes 36868
  83.8 5.0 %copy-start.40 = (s32[1,256,2]{1,2,0:T(2,128)S(1)}, s32[1,256,2]{1,2,0:T(2,128)}, u32[]{:S(2)}) copy-start(s32[1,256,2]{1,2,0:T(2,128)} %param.35) | copy-start | bytes 6148
  83.8 5.2 %copy-start.39 = (f32[12,12]{1,0:T(8,128)S(1)}, f32[12,12]{1,0:T(8,128)}, u32[]{:S(2)}) copy-start(f32[12,12]{1,0:T(8,128)} %param.45) | copy-start | bytes 1732
  83.9 5.3 %copy-start.2 = (bf16[4,4,4,2,16,512]{5,4,3,2,1,0:T(8,128)(2,1)S(1)}, bf16[4,4,4,2,16,512]{5,4,3,2,1,0:T(8,128)(2,1)}, u32[]{:S(2)}) copy-start(bf16[4,4,4,2,16,512]{5,4,3,2,1,0:T(8,128)(2,1)} %get-tuple-element.57) | copy-start | bytes 6291460
  83.9 5.3 %copy-start.16 = (bf16[192,256]{1,0:T(8,128)(2,1)S(1)}, bf16[192,256]{1,0:T(8,128)(2,1)}, u32[]{:S(2)}) copy-start(bf16[192,256]{1,0:T(8,128)(2,1)} %constant.26.clone.left_ref) | copy-start | bytes 294916
  83.9 5.3 %copy-start.17 = (bf16[192,256]{1,0:T(8,128)(2,1)S(1)}, bf16[192,256]{1,0:T(8,128)(2,1)}, u32[]{:S(2)}) copy-start(bf16[192,256]{1,0:T(8,128)(2,1)} %constant.27.clone.right_ref) | copy-start | bytes 294916
  83.9 5.3 %copy-start.20 = (bf16[48,128]{1,0:T(8,128)(2,1)S(1)}, bf16[48,128]{1,0:T(8,128)(2,1)}, u32[]{:S(2)}) copy-start(bf16[48,128]{1,0:T(8,128)(2,1)} %constant.28.clone.small_ref) | copy-start | bytes 36868
  88.8 9.9 %copy-start.41 = (s32[1,1,256]{2,1,0:T(1,128)S(1)}, s32[1,1,256]{2,1,0:T(1,128)}, u32[]{:S(2)}) copy-start(s32[1,1,256]{2,1,0:T(1,128)} %param.37) | copy-start | bytes 3076
  89.0 26.3 %copy-start.14 = (s32[1,256,2]{2,1,0:T(8,128)}, s32[1,256,2]{2,1,0:T(8,128)S(1)}, u32[]{:S(2)}) copy-start(s32[1,256,2]{2,1,0:T(8,128)S(1)} %copy.65) | copy-start | bytes 6148
  89.1 26.3 %copy-start.15 = (f32[256,128]{1,0:T(8,128)}, f32[256,128]{1,0:T(8,128)S(1)}, u32[]{:S(2)}) copy-start(f32[256,128]{1,0:T(8,128)S(1)} %pad.18.prev_ref) | copy-start | bytes 393220
  89.1 26.2 %copy-start.18 = (f32[128,128]{1,0:T(8,128)}, f32[128,128]{1,0:T(8,128)S(1)}, u32[]{:S(2)}) copy-start(f32[128,128]{1,0:T(8,128)S(1)} %pad.19.wres_ref) | copy-start | bytes 196612
  89.2 1.4 copy-start.4
  90.6 1.4 copy-start.5
  96.4 2.2 copy-start.24
  98.6 121.4 %copy-start.11 = (bf16[768,128]{1,0:T(8,128)(2,1)}, bf16[768,128]{1,0:T(8,128)(2,1)S(1)}, u32[]{:S(2)}) copy-start(bf16[768,128]{1,0:T(8,128)(2,1)S(1)} %get-tuple-element.61.small_ref) | copy-start | bytes 589828
  99.3 16.0 %copy-start.22 = (f32[8,256]{1,0:T(8,128)}, f32[8,256]{1,0:T(8,128)S(1)}, u32[]{:S(2)}) copy-start(f32[8,256]{1,0:T(8,128)S(1)} %get-tuple-element.124.segments_ref) | copy-start | bytes 24580
  99.3 16.0 %copy-start.23 = (s32[8,256]{1,0:T(8,128)}, s32[8,256]{1,0:T(8,128)S(1)}, u32[]{:S(2)}) copy-start(s32[8,256]{1,0:T(8,128)S(1)} %get-tuple-element.125.segs_ref) | copy-start | bytes 24580
  107.1 8.2 %copy-start.25 = (bf16[1,256,768]{2,1,0:T(8,128)(2,1)S(1)}, bf16[1,256,768]{2,1,0:T(8,128)(2,1)}, u32[]{:S(2)}) copy-start(bf16[1,256,768]{2,1,0:T(8,128)(2,1)} %param.51) | copy-start | bytes 1179652
  107.1 8.2 %copy-start.26 = (f32[256,128]{1,0:T(8,128)S(1)}, f32[256,128]{1,0:T(8,128)}, u32[]{:S(2)}) copy-start(f32[256,128]{1,0:T(8,128)} %constant.29.clone.cos_in) | copy-start | bytes 393220
  107.1 8.2 %copy-start.27 = (f32[256,128]{1,0:T(8,128)S(1)}, f32[256,128]{1,0:T(8,128)}, u32[]{:S(2)}) copy-start(f32[256,128]{1,0:T(8,128)} %constant.30.clone.sin_in) | copy-start | bytes 393220
  107.2 8.3 %copy-start.28 = (f32[8,128]{1,0:T(8,128)S(1)}, f32[8,128]{1,0:T(8,128)}, u32[]{:S(2)}) copy-start(f32[8,128]{1,0:T(8,128)} %constant.31.clone.cos_out) | copy-start | bytes 12292
  107.2 8.3 %copy-start.29 = (f32[8,128]{1,0:T(8,128)S(1)}, f32[8,128]{1,0:T(8,128)}, u32[]{:S(2)}) copy-start(f32[8,128]{1,0:T(8,128)} %constant.32.clone.sin_out) | copy-start | bytes 12292
  107.2 49.8 %all-to-all-start = ((bf16[8,192,1024]{2,1,0:T(8,128)(2,1)}), bf16[8,192,1024]{2,1,0:T(8,128)(2,1)}, u32[]{:S(2)}, u32[]{:S(2)}) async-start(bf16[8,192,1024]{2,1,0:T(8,128)(2,1)} %broadcast_in_dim.39), calls=%async_computation | async-start | bytes 6291456 | tf_op jit(solution)/shard_map/all_to_all | solution.py:1264
  131.9 0.9 copy-start.8
  132.8 0.9 copy-start.9
  133.8 0.9 copy-start.31
  134.7 0.7 copy-start.33
  135.4 0.7 copy-start.34
  136.1 0.6 copy-start.36
  136.7 75.8 %copy-start.30 = (f32[256,768]{1,0:T(8,128)}, f32[256,768]{1,0:T(8,128)S(1)}, u32[]{:S(2)}) copy-start(f32[256,768]{1,0:T(8,128)S(1)} %get-tuple-element.62.state_ref) | copy-start | bytes 2359300
  136.7 75.8 %copy-start.32 = (bf16[256,768]{1,0:T(8,128)(2,1)}, bf16[256,768]{1,0:T(8,128)(2,1)S(1)}, u32[]{:S(2)}) copy-start(bf16[256,768]{1,0:T(8,128)(2,1)S(1)} %get-tuple-element.63.normed_ref) | copy-start | bytes 1179652
  136.7 75.8 %copy-start.35 = (f32[256,128]{1,0:T(8,128)}, f32[256,128]{1,0:T(8,128)S(1)}, u32[]{:S(2)}) copy-start(f32[256,128]{1,0:T(8,128)S(1)} %get-tuple-element.70.proj_ref) | copy-start | bytes 393220
  212.5 27.4 %all-to-all-start.3 = ((bf16[8,128,768]{2,1,0:T(8,128)(2,1)}), bf16[8,128,768]{2,1,0:T(8,128)(2,1)S(1)}, u32[]{:S(2)}, u32[]{:S(2)}) async-start(bf16[8,128,768]{2,1,0:T(8,128)(2,1)} %get-tuple-element.89), calls=%async_computation.3 | async-start | bytes 3145728 | tf_op jit(solution)/shard_map/all_to_all | solution.py:1292
  239.9 134.4 %all-to-all-start.2 = ((bf16[8,192,1024]{2,1,0:T(8,128)(2,1)}), bf16[8,192,1024]{2,1,0:T(8,128)(2,1)}, u32[]{:S(2)}, u32[]{:S(2)}) async-start(bf16[8,192,1024]{2,1,0:T(8,128)(2,1)} %get-tuple-element.88), calls=%async_computation.2 | async-start | bytes 6291456 | tf_op jit(solution)/shard_map/all_to_all | solution.py:1292
  248.1 28.2 %copy-start.12 = (bf16[256,192]{1,0:T(8,128)(2,1)S(1)}, bf16[256,192]{1,0:T(8,128)(2,1)}, u32[]{:S(2)}) copy-start(bf16[256,192]{1,0:T(8,128)(2,1)} %constant.33.clone.left_ref) | copy-start | bytes 294916
  248.1 28.2 %copy-start.13 = (bf16[256,192]{1,0:T(8,128)(2,1)S(1)}, bf16[256,192]{1,0:T(8,128)(2,1)}, u32[]{:S(2)}) copy-start(bf16[256,192]{1,0:T(8,128)(2,1)} %constant.34.clone.right_ref) | copy-start | bytes 294916
  248.1 28.2 %copy-start.19 = (bf16[128,48]{1,0:T(8,128)(2,1)S(1)}, bf16[128,48]{1,0:T(8,128)(2,1)}, u32[]{:S(2)}) copy-start(bf16[128,48]{1,0:T(8,128)(2,1)} %constant.35.clone.small_ref) | copy-start | bytes 36868
  276.3 3.7 copy-start
  280.0 1.0 copy-start.10
  281.0 6.0 %copy-start.1 = (bf16[8,256,768]{2,1,0:T(8,128)(2,1)S(1)}, bf16[8,256,768]{2,1,0:T(8,128)(2,1)}, u32[]{:S(2)}) copy-start(bf16[8,256,768]{2,1,0:T(8,128)(2,1)} %get-tuple-element.81.others_ref) | copy-start | bytes 9437188
  281.0 6.0 %copy-start.3 = (bf16[1,256,768]{2,1,0:T(8,128)(2,1)S(1)}, bf16[1,256,768]{2,1,0:T(8,128)(2,1)}, u32[]{:S(2)}) copy-start(bf16[1,256,768]{2,1,0:T(8,128)(2,1)} %param.33) | copy-start | bytes 1179652
  281.0 6.0 %copy-start.6 = (f32[256,768]{1,0:T(8,128)S(1)}, f32[256,768]{1,0:T(8,128)}, u32[]{:S(2)}) copy-start(f32[256,768]{1,0:T(8,128)} %get-tuple-element.82.first_ref) | copy-start | bytes 2359300
  281.0 6.0 %copy-start.7 = (f32[256,768]{1,0:T(8,128)S(1)}, f32[256,768]{1,0:T(8,128)}, u32[]{:S(2)}) copy-start(f32[256,768]{1,0:T(8,128)} %get-tuple-element.83.state_grad_ref) | copy-start | bytes 2359300
  281.0 6.0 %copy-start.21 = (f32[16,128]{1,0:T(8,128)S(1)}, f32[16,128]{1,0:T(8,128)}, u32[]{:S(2)}) copy-start(f32[16,128]{1,0:T(8,128)} %get-tuple-element.80.small_ref) | copy-start | bytes 24580
  287.0 84.2 %copy-start.37 = (f32[256,128]{1,0:T(8,128)S(1)}, f32[256,128]{1,0:T(8,128)}, u32[]{:S(2)}) copy-start(f32[256,128]{1,0:T(8,128)} %get-tuple-element.85) | copy-start | bytes 393220

commit v3 on v2

v3 whole, which is shorter than its diff:
```python
import functools

import jax
import jax.numpy as jnp
import numpy as np
from jax import lax
from jax.experimental import pallas as pl
from jax.experimental.pallas import tpu as pltpu
from jax.sharding import PartitionSpec as P

HEADS = 12
HDIM = 64
EXPERTS = 8
NALL = 12
CAP = 54
WIDTH = HEADS * HDIM
PAIRS = HEADS // 2
BLK = 256
SLOTS = 64

highest = lax.Precision.HIGHEST
masked_score = -1e30
epsilon = 1e-06

MESH = pl.DeviceIdType.MESH
PART_LANES = (512, 384, 384)
PART_START = (0, 512, 896)
PART_ORDER = ((0, 1, 2), (1, 2, 0), (2, 0, 1))


def place():
    ctx = lax.axis_index("ctx")
    fsdp = lax.axis_index("fsdp")
    return ctx // 2, (ctx % 2) * 2 + fsdp // 8, (fsdp // 2) % 4, fsdp % 2


def device_at(x, z, y, core):
    return {"ctx": x * 2 + z // 2, "fsdp": (z % 2) * 8 + y * 2 + core}


def shifted(spot, axis, by):
    moved = list(spot)
    moved[axis] = (moved[axis] + by) % 4
    return tuple(moved)


def greet(devices):
    barrier = pltpu.get_barrier_semaphore()
    for device in devices:
        pl.semaphore_signal(barrier, inc=1, device_id=device, device_id_type=MESH)
    pl.semaphore_wait(barrier, len(devices))


def torus_peers(spot, core):
    peers = [device_at(*shifted(spot, axis, by), core) for axis in range(3) for by in (1, 2, 3)]
    return peers + [device_at(*spot, 1 - core)]


def sequence_peers(spot, core):
    x, z, y = spot
    return [device_at((x + by) % 4, (z + 2) % 4, y, core) for by in (1, 2, 3)]


def region(ref, spot, core, whole):
    return ref.at[
        tuple(slice(None) if axis in whole else spot[axis] for axis in range(3)) + (core,)
    ]


def placing_tables():
    left = np.zeros((192, 256), np.float32)
    right = np.zeros((192, 256), np.float32)
    small = np.zeros((48, 128), np.float32)
    for device in range(8):
        for weight in range(4):
            for row in range(6):
                at, line = weight * 48 + device * 6 + row, weight * 6 + row
                if line < 16:
                    left[at, device * 16 + line] = right[at, device * 16 + line] = 1
                else:
                    left[at, 128 + device * 16 + line - 16] = 1
                    right[at, 128 + device * 16 + line - 8] = 1
        for row in range(6):
            small[device * 6 + row, device * 16 + row] = 1
    return left, right, small


def rope_tables():
    frequency = 10000.0 ** (-2.0 * (np.arange(128) % 32) / HDIM)
    inner = np.arange(BLK)[:, None] * frequency
    outer = (np.arange(8) * BLK)[:, None] * frequency
    return [jnp.asarray(t, jnp.float32) for t in (np.cos(inner), np.sin(inner), np.cos(outer), np.sin(outer))]


def turning(index, tables):
    cos_in, sin_in, cos_out, sin_out = tables
    ca, sa = cos_out[pl.ds(index, 1), :], sin_out[pl.ds(index, 1), :]
    cb, sb = cos_in[...], sin_in[...]
    lower = lax.broadcasted_iota(jnp.int32, (BLK, 128), 1) % HDIM < HDIM // 2
    sine = sa * cb + ca * sb
    return ca * cb - sa * sb, jnp.where(lower, -sine, sine)


def swapped(values):
    lower = lax.broadcasted_iota(jnp.int32, values.shape, 1) % HDIM < HDIM // 2
    return jnp.where(lower, pltpu.roll(values, 96, 1), pltpu.roll(values, 32, 1))


def dot(left, right):
    return jnp.dot(left, right, preferred_element_type=jnp.float32)


def dot_nt(left, right):
    return lax.dot_general(left, right, (((1,), (1,)), ((), ())), preferred_element_type=jnp.float32)


def column(row):
    return jnp.broadcast_to(row, (128, row.shape[1])).T[:, 0:1]


def mask_bias(key_block, query_block, bias_ref, ctx, index):
    key_seg = column(key_block[BLK:, :BLK].astype(jnp.float32)[:1])
    query_seg = query_block[BLK:, :BLK].astype(jnp.float32)[:1]
    key_pos = lax.broadcasted_iota(jnp.int32, (BLK, BLK), 0)
    query_pos = lax.broadcasted_iota(jnp.int32, (BLK, BLK), 1)
    reach = jnp.where(index == ctx, 0, BLK)
    allowed = (key_seg == query_seg) & (key_pos <= query_pos + reach)
    bias_ref[...] = jnp.where(allowed, 0.0, masked_score)


def rms_rows(values):
    return lax.rsqrt(jnp.mean(values * values, axis=-1, keepdims=True) + epsilon)


def pick(onehot, values):
    return jnp.sum(jnp.where(onehot, values, 0.0), axis=1, keepdims=True)


def lane_is(lanes):
    return lax.broadcasted_iota(jnp.int32, (BLK, 128), 1) == lanes


def dot_tn(left, right):
    return lax.dot_general(left, right, (((0,), (0,)), ((), ())), preferred_element_type=jnp.float32)


def row_tile(values):
    *weights, small = values
    rows = jnp.concatenate([w.astype(jnp.float32) for w in weights], axis=0)
    tail = jnp.concatenate([rows[16:, :384], rows[16:, 384:]], axis=0)
    return jnp.concatenate([rows[:16], tail, small], axis=1).astype(jnp.bfloat16)


def front_kernel(
    wq_ref, wk_ref, wv_ref, wo_ref, router_ref, constant_ref, vector_ref, gain_one_ref, gain_two_ref,
    tokens_ref, segments_in, gate_in, up_in,
    left_ref, right_ref, place_ref, cos_in, sin_in, cos_out, sin_out,
    prev_ref, wres_ref, routes_ref, rank_ref, cot_ref,
    state_ref, normed_ref, att_ref, lse_ref, q_ref, keys_ref, values_ref, rows_ref, grads_ref,
    info_ref, proj_ref, blocks_ref, w_ref, small_ref, gate_up_ref,
    part_a, part_b, part_c, own_ref, qt_ref, vt_ref, bias_ref, max_ref, sum_ref, acc_ref,
    prev_pad, wres_pad, few_wide, few_tall,
    net_send, net_recv, twin_send, twin_recv, own_sem, seq_send, seq_recv, fwd_send, fwd_recv,
):
    parts = (part_a, part_b, part_c)
    tables = (cos_in, sin_in, cos_out, sin_out)
    ctx, fsdp = lax.axis_index("ctx"), lax.axis_index("fsdp")
    along, side = ctx // 2, ctx % 2
    *spot, core = place()
    spot = tuple(spot)
    twin = device_at(*spot, 1 - core)
    few_wide[...] = jnp.zeros_like(few_wide)
    few_wide[12:16, :6] = constant_ref[...].astype(jnp.float32)
    few_wide[16:18, :6] = vector_ref[...].astype(jnp.float32)
    few_wide[18:19, :6] = gain_one_ref[...].astype(jnp.float32)
    few_wide[19:20, :6] = gain_two_ref[...].astype(jnp.float32)
    few_tall[...] = few_wide[...].T[:16]
    few_tall[:6, :NALL] = router_ref[...].astype(jnp.float32)
    own_ref[...] = row_tile([wq_ref[...], wk_ref[...], wv_ref[...], wo_ref[...], few_tall[...]])
    marks = jnp.concatenate(
        [segments_in[...].astype(jnp.float32), jnp.zeros((1, WIDTH - BLK), jnp.float32)], axis=1
    )
    blocks_ref[ctx, :BLK] = tokens_ref[...]
    blocks_ref[ctx, BLK:] = jnp.broadcast_to(marks, (16, WIDTH)).astype(jnp.bfloat16)
    greet(torus_peers(spot, core) + sequence_peers(spot, core))

    def net(part, step, by, source, target):
        axis = PART_ORDER[part][step]
        return pltpu.make_async_remote_copy(
            src_ref=source,
            dst_ref=target,
            send_sem=net_send.at[part, step, by - 1],
            recv_sem=net_recv.at[part, step, by - 1],
            device_id=device_at(*shifted(spot, axis, by), core),
            device_id_type=MESH,
        )

    def share(part, slot, source, target):
        return pltpu.make_async_remote_copy(
            src_ref=source,
            dst_ref=target,
            send_sem=twin_send.at[part, slot],
            recv_sem=twin_recv.at[part, slot],
            device_id=twin,
            device_id_type=MESH,
        )

    payloads = ((blocks_ref, 128, BLK + 16), (gate_up_ref, 96, 192))

    def seq(kind, route, by, source, rows):
        array = payloads[kind][0]
        to_side = side if route in (1, 3) else 1 - side
        target = ((along + by) % 4) * 2 + to_side
        semaphores = (fwd_send, fwd_recv) if route == 3 else (seq_send, seq_recv)
        slot = {0: 0, 1: by, 2: 3 + by, 3: by - 1}[route]
        view = array.at[source, rows]
        return pltpu.make_async_remote_copy(
            src_ref=view,
            dst_ref=view,
            send_sem=semaphores[0].at[kind, slot],
            recv_sem=semaphores[1].at[kind, slot],
            device_id={"ctx": target, "fsdp": fsdp},
            device_id_type=MESH,
        )

    def rows_of(kind, route):
        array, cut, end = payloads[kind]
        return (pl.ds(0, end), pl.ds(0, end), pl.ds(0, cut), pl.ds(cut, end - cut))[route]

    def needed(kind, by):
        return along + by < 4 if kind == 0 else along >= 0

    def send_own(kind):
        seq(kind, 0, 0, ctx, rows_of(kind, 0)).start()
        for by in (1, 2, 3):

            @pl.when(needed(kind, by))
            def _(by=by):
                seq(kind, 1, by, ctx, rows_of(kind, 1)).start()
                seq(kind, 2, by, ctx, rows_of(kind, 2)).start()

    def beside():
        return along * 2 + 1 - side

    def send_on(kind):
        seq(kind, 0, 0, beside(), rows_of(kind, 0)).wait_recv()
        for by in (1, 2, 3):

            @pl.when(needed(kind, by))
            def _(by=by):
                seq(kind, 3, by, beside(), rows_of(kind, 3)).start()

    def behind(by, on_side):
        return ((along - by + 4) % 4) * 2 + on_side

    def wait_along(kind, by):
        seq(kind, 1, by, behind(by, side), rows_of(kind, 1)).wait_recv()

    def wait_across(kind, by):
        seq(kind, 2, by, behind(by, 1 - side), rows_of(kind, 2)).wait_recv()
        seq(kind, 3, by, behind(by, 1 - side), rows_of(kind, 3)).wait_recv()

    def wait_sent(kind):
        seq(kind, 0, 0, ctx, rows_of(kind, 0)).wait_send()
        for by in (1, 2, 3):

            @pl.when(needed(kind, by))
            def _(by=by):
                seq(kind, 1, by, ctx, rows_of(kind, 1)).wait_send()
                seq(kind, 2, by, ctx, rows_of(kind, 2)).wait_send()
                seq(kind, 3, by, beside(), rows_of(kind, 3)).wait_send()

    started = []
    kept = []
    for part in range(3):
        own = own_ref.at[:, pl.ds(PART_START[part], PART_LANES[part])]
        mine = region(parts[part], spot, core, ())
        for by in (1, 2, 3):
            copy = net(part, 0, by, own, mine)
            copy.start()
            started.append(copy)
    for part in range(3):
        own = own_ref.at[:, pl.ds(PART_START[part], PART_LANES[part])]
        mine = region(parts[part], spot, core, ())
        copy = pltpu.make_async_copy(own, mine, own_sem.at[part])
        copy.start()
        kept.append(copy)
        copy = share(part, 0, own, mine)
        copy.start()
        started.append(copy)
    own_experts = [
        pltpu.make_async_copy(gate_in, gate_up_ref.at[ctx, :96], own_sem.at[3]),
        pltpu.make_async_copy(up_in, gate_up_ref.at[ctx, 96:], own_sem.at[4]),
    ]
    for copy in own_experts:
        copy.start()
    for copy in kept + own_experts:
        copy.wait()
    for step in range(3):
        for part in range(3):
            order = PART_ORDER[part]
            axis = order[step]
            whole = order[:step]
            for by in (1, 2, 3):
                here = region(parts[part], shifted(spot, axis, -by), core, whole)
                net(part, step, by, here, here).wait_recv()
                copy = share(part, 1 + step * 3 + by - 1, here, here)
                copy.start()
                started.append(copy)
            if step < 2:
                held = region(parts[part], spot, core, order[: step + 1])
                for by in (1, 2, 3):
                    copy = net(part, step + 1, by, held, held)
                    copy.start()
                    started.append(copy)
        if step == 1:
            send_own(0)
    for part in range(3):
        order = PART_ORDER[part]
        first = region(parts[part], spot, 1 - core, ())
        share(part, 0, first, first).wait_recv()
        for step in range(3):
            for by in (1, 2, 3):
                here = region(
                    parts[part], shifted(spot, order[step], -by), 1 - core, order[:step]
                )
                share(part, 1 + step * 3 + by - 1, here, here).wait_recv()

    def unpack(group, carry):
        a, b, c = (
            part[group // 4, group % 4].reshape(128, lanes)
            for part, lanes in zip(parts, PART_LANES, strict=True)
        )
        tail = jnp.concatenate([b[:, 256:], c[:, :256]], axis=1)
        left = dot(left_ref[...], jnp.concatenate([a[:, :384], tail], axis=0))
        right_rows = jnp.concatenate([a[:, 384:], b[:, :256]], axis=1)
        right = dot(right_ref[...], jnp.concatenate([right_rows, tail], axis=0))
        rows = pl.ds(pl.multiple_of(group * 48, 16), 48)
        for weight in range(4):
            w_ref[weight, rows, :384] = left[weight * 48 : weight * 48 + 48].astype(jnp.bfloat16)
            w_ref[weight, rows, 384:] = right[weight * 48 : weight * 48 + 48].astype(jnp.bfloat16)
        small_ref[rows] = dot(place_ref[...], c[:, 256:]).astype(jnp.bfloat16)
        return carry

    lax.fori_loop(0, 16, unpack, 0)
    across = small_ref[...].astype(jnp.float32).T
    gain_one, gain_two = across[18:19], across[19:20]

    def normed_block(index):
        wide = blocks_ref[index, :BLK].astype(jnp.float32)
        return (wide * rms_rows(wide) * gain_one).astype(jnp.bfloat16)

    query = dot(normed_block(ctx), w_ref[0])
    cosine, sine = turning(ctx, tables)
    for pair in range(PAIRS):
        part = query[:, pair * 128 : pair * 128 + 128]
        turned = (part * cosine + swapped(part) * sine) * (HDIM**-0.5)
        q_ref[pair] = turned.astype(jnp.bfloat16)
        across_q = turned.T.astype(jnp.bfloat16)
        blank = jnp.zeros((HDIM, BLK), jnp.bfloat16)
        qt_ref[2 * pair] = jnp.concatenate([across_q[:HDIM], blank], axis=0)
        qt_ref[2 * pair + 1] = jnp.concatenate([blank, across_q[HDIM:]], axis=0)
    max_ref[...] = jnp.full(max_ref.shape, masked_score, jnp.float32)
    sum_ref[...] = jnp.zeros_like(sum_ref)
    acc_ref[...] = jnp.zeros_like(acc_ref)

    def block(step, carry):
        index = ctx - step

        @pl.when((step > 0) & (step % 2 == 0))
        def _():
            wait_along_at(step // 2)

        @pl.when((step % 2 == 1) & ((step + 1) // 2 - side > 0))
        def _():
            wait_across_at((step + 1) // 2 - side)

        normed = normed_block(index)
        key = dot(normed, w_ref[1])
        value = dot(normed, w_ref[2])
        cosine, sine = turning(index, tables)
        for pair in range(PAIRS):
            lanes = slice(pair * 128, pair * 128 + 128)
            part = key[:, lanes]
            keys_ref[index, pair] = (part * cosine + swapped(part) * sine).astype(jnp.bfloat16)
            values_ref[index, pair] = value[:, lanes].astype(jnp.bfloat16)
            vt_ref[lanes, :] = value[:, lanes].T.astype(jnp.bfloat16)
        mask_bias(blocks_ref.at[index], blocks_ref.at[ctx], bias_ref, ctx, index)
        for head in range(HEADS):
            rows = slice(head * HDIM, head * HDIM + HDIM)
            scores = dot(keys_ref[index, head // 2], qt_ref[head]) + bias_ref[...]
            before = max_ref[head : head + 1]
            top = jnp.maximum(before, jnp.max(scores, axis=0, keepdims=True))
            weights = jnp.exp(scores - top)
            shrink = jnp.exp(before - top)
            sum_ref[head : head + 1] = sum_ref[head : head + 1] * shrink + jnp.sum(
                weights, axis=0, keepdims=True
            )
            max_ref[head : head + 1] = top
            acc_ref[rows] = acc_ref[rows] * shrink + dot(vt_ref[rows, :], weights.astype(jnp.bfloat16))

        @pl.when(step == 0)
        def _():
            send_on(0)
            send_own(1)

        @pl.when(step == jnp.minimum(ctx, 3))
        def _():
            send_on(1)

        return carry

    def wait_along_at(by):
        source = (along - by) * 2 + side
        seq_at(1, by, source).wait_recv()

    def wait_across_at(by):
        source = (along - by) * 2 + 1 - side
        seq_at(2, by, source).wait_recv()
        seq_at(3, by, source).wait_recv()

    def seq_at(route, by, source):
        view = blocks_ref.at[source, rows_of(0, route)]
        semaphores = (fwd_send, fwd_recv) if route == 3 else (seq_send, seq_recv)
        slot = {1: by, 2: 3 + by, 3: by - 1}[route]
        return pltpu.make_async_remote_copy(
            src_ref=view,
            dst_ref=view,
            send_sem=semaphores[0].at[0, slot],
            recv_sem=semaphores[1].at[0, slot],
            device_id=twin,
            device_id_type=MESH,
        )

    lax.fori_loop(0, ctx + 1, block, 0)
    for head in range(HEADS):
        rows = slice(head * HDIM, head * HDIM + HDIM)
        att_ref[rows] = acc_ref[rows] / sum_ref[head : head + 1]
    lse_ref[...] = max_ref[...] + jnp.log(jnp.maximum(sum_ref[...], 1e-30))
    attended = att_ref[...].T.astype(jnp.bfloat16)
    state = blocks_ref[ctx, :BLK].astype(jnp.float32) + dot(attended, w_ref[3])
    state_ref[...] = state
    normed_two = (state * rms_rows(state) * gain_two).astype(jnp.bfloat16)
    normed_ref[...] = normed_two

    proj = dot(normed_two, small_ref[...])
    proj_ref[...] = proj
    pad_routing(prev_ref, wres_ref, prev_pad, wres_pad)
    logits = proj + jnp.dot(
        prev_pad[...].T, wres_pad[...], precision=highest, preferred_element_type=jnp.float32
    )
    lanes = lax.broadcasted_iota(jnp.int32, (BLK, 128), 1).astype(jnp.float32)
    routes = routes_ref[...].astype(jnp.float32)
    route_0, route_1 = column(routes[0:1]), column(routes[1:2])
    hot_0, hot_1 = lanes == route_0, lanes == route_1
    chosen_0, chosen_1 = pick(hot_0, logits), pick(hot_1, logits)
    top = jnp.maximum(chosen_0, chosen_1)
    chosen_0, chosen_1 = jnp.exp(chosen_0 - top), jnp.exp(chosen_1 - top)
    gate_0, gate_1 = chosen_0 / (chosen_0 + chosen_1), chosen_1 / (chosen_0 + chosen_1)
    rank = rank_ref[...].astype(jnp.float32)
    earlier = (rank < column(rank)).astype(jnp.float32).astype(jnp.bfloat16)
    slots = dot(earlier, (hot_0 | hot_1).astype(jnp.float32).astype(jnp.bfloat16))

    def target(route, hot):
        slot = pick(hot, slots)
        return jnp.where(
            (route < EXPERTS) & (slot < CAP), route * SLOTS + slot, -1.0
        )

    target_0, target_1 = target(route_0, hot_0), target(route_1, hot_1)
    info = jnp.where(lanes == 0, gate_0, 0.0) + jnp.where(lanes == 1, gate_1, 0.0)
    info = info + jnp.where(lanes == 2, target_0, 0.0) + jnp.where(lanes == 3, target_1, 0.0)
    info_ref[...] = info
    targets = info.T
    rows = lax.broadcasted_iota(jnp.int32, (EXPERTS * SLOTS, BLK), 0).astype(jnp.float32)
    table_0 = (rows == targets[2:3]).astype(jnp.float32).astype(jnp.bfloat16)
    table_1 = (rows == targets[3:4]).astype(jnp.float32).astype(jnp.bfloat16)
    rows_ref[...] = dot(table_0 + table_1, normed_two).astype(jnp.bfloat16)
    upstream = cot_ref[...].astype(jnp.float32)
    grads_ref[...] = dot(
        jnp.concatenate([table_0, table_1], axis=1),
        jnp.concatenate([gate_0 * upstream, gate_1 * upstream], axis=0).astype(jnp.bfloat16),
    ).astype(jnp.bfloat16)
    for by in (1, 2, 3):
        wait_along(1, by)
        wait_across(1, by)
    for kind in (0, 1):
        wait_sent(kind)
    for copy in started:
        copy.wait_send()


def pad_routing(prev_ref, wres_ref, prev_pad, wres_pad):
    prev_pad[...] = jnp.zeros_like(prev_pad)
    prev_pad[:NALL] = prev_ref[:, 0, :]
    wres_pad[...] = jnp.zeros_like(wres_pad)
    wres_pad[:NALL, :NALL] = wres_ref[...]


def run_front(weights, few, tokens, segments, gate, up, prev, wres, routes, rank, cot):
    vmem, anywhere = pl.BlockSpec(memory_space=pltpu.VMEM), pl.BlockSpec(memory_space=pl.ANY)
    shape = jax.ShapeDtypeStruct
    low, wide = jnp.bfloat16, jnp.float32
    dma = pltpu.SemaphoreType.DMA
    left, right, small = (jnp.asarray(t, low) for t in placing_tables())
    return pl.pallas_call(
        front_kernel,
        out_shape=[
            shape((BLK, WIDTH), wide),
            shape((BLK, WIDTH), low),
            shape((WIDTH, BLK), wide),
            shape((16, BLK), wide),
            shape((PAIRS, BLK, 128), low),
            shape((8, PAIRS, BLK, 128), low),
            shape((8, PAIRS, BLK, 128), low),
            shape((EXPERTS * SLOTS, WIDTH), low),
            shape((EXPERTS * SLOTS, WIDTH), low),
            shape((BLK, 128), wide),
            shape((BLK, 128), wide),
            shape((8, BLK + 16, WIDTH), low),
            shape((4, WIDTH, WIDTH), low),
            shape((WIDTH, 128), low),
            shape((8, 192, 1024), low),
        ],
        in_specs=[vmem] * 25,
        out_specs=[vmem] * 14 + [anywhere],
        scratch_shapes=[
            *(pltpu.VMEM((4, 4, 4, 2, 16, lanes), low) for lanes in PART_LANES),
            pltpu.VMEM((16, 1280), low),
            pltpu.VMEM((HEADS, 128, BLK), low),
            pltpu.VMEM((WIDTH, BLK), low),
            pltpu.VMEM((BLK, BLK), wide),
            pltpu.VMEM((16, BLK), wide),
            pltpu.VMEM((16, BLK), wide),
            pltpu.VMEM((WIDTH, BLK), wide),
            pltpu.VMEM((128, BLK), wide),
            pltpu.VMEM((128, 128), wide),
            pltpu.VMEM((128, 128), wide),
            pltpu.VMEM((16, 128), wide),
            dma((3, 3, 3)),
            dma((3, 3, 3)),
            dma((3, 10)),
            dma((3, 10)),
            dma((5,)),
            dma((2, 7)),
            dma((2, 7)),
            dma((2, 3)),
            dma((2, 3)),
        ],
        name="front",
        compiler_params=pltpu.CompilerParams(
            collective_id=1, has_side_effects=True, vmem_limit_bytes=56 * 2**20
        ),
    )(
        *weights, *few, tokens, segments, gate, up, left, right, small, *rope_tables(),
        prev, wres, routes, rank, cot,
    )


def experts_kernel(
    rows_ref, grads_ref, gate_up_ref, down_ref,
    back_rows_ref, back_grads_ref, d_gate_up_ref, d_down_ref,
    gate_w, up_w, down_w, x_ref, g_ref, gate_ref, up_ref, hidden_ref, d_gate, d_up,
    mine_ref, twin_out, twin_in, sums_ref,
    down_send, down_recv, load_sem, send_sem, recv_sem, share_send, share_recv, half_send, half_recv, ret_send, ret_recv,
    own_sem,
):
    ctx, fsdp = lax.axis_index("ctx"), lax.axis_index("fsdp")
    chip, core = fsdp // 2, fsdp % 2
    other = 1 - core
    half = EXPERTS * SLOTS

    def at(where, on):
        return {"ctx": ctx, "fsdp": where * 2 + on}

    greet(
        [at((chip + by) % EXPERTS, core) for by in range(1, EXPERTS)]
        + [at(chip, other)]
        + [{"ctx": (ctx + by) % 8, "fsdp": fsdp} for by in range(1, 8)]
    )

    def down(by, owner):
        spot = down_w.at[pl.ds(pl.multiple_of(owner * 128, 128), 128)]
        return pltpu.make_async_remote_copy(
            src_ref=down_ref,
            dst_ref=spot,
            send_sem=down_send.at[by - 1],
            recv_sem=down_recv.at[by - 1],
            device_id={"ctx": (ctx + by) % 8, "fsdp": fsdp},
            device_id_type=MESH,
        )

    loads = []
    for index in range(8):
        for source, target, size in (
            (gate_up_ref.at[index, :96], gate_w, 96),
            (gate_up_ref.at[index, 96:], up_w, 96),
        ):
            copy = pltpu.make_async_copy(
                source, target.at[pl.ds(index * size, size)], load_sem.at[len(loads)]
            )
            loads.append(copy)
    loads.append(
        pltpu.make_async_copy(
            down_ref, down_w.at[pl.ds(pl.multiple_of(ctx * 128, 128), 128)], load_sem.at[16]
        )
    )

    def slots(index, on):
        return pl.ds(pl.multiple_of((on * EXPERTS + index) * SLOTS, SLOTS), SLOTS)

    def chunk(index):
        return pl.ds(pl.multiple_of(index * SLOTS, SLOTS), SLOTS)

    buffers = ((rows_ref, x_ref), (grads_ref, g_ref))

    def dispatch(kind, by):
        source, target = buffers[kind]
        where = (chip + by) % EXPERTS
        return pltpu.make_async_remote_copy(
            src_ref=source.at[chunk(where)],
            dst_ref=target.at[slots(chip, core)],
            send_sem=send_sem.at[kind, by - 1],
            recv_sem=recv_sem.at[kind, by - 1],
            device_id=at(where, core),
            device_id_type=MESH,
        )

    def share(kind, by, on):
        source, target = buffers[kind]
        spot = slots((chip - by) % EXPERTS, on)
        return pltpu.make_async_remote_copy(
            src_ref=target.at[spot],
            dst_ref=target.at[spot],
            send_sem=share_send.at[kind, by],
            recv_sem=share_recv.at[kind, by],
            device_id=at(chip, other),
            device_id_type=MESH,
        )

    def exchange(kind):
        return pltpu.make_async_remote_copy(
            src_ref=twin_out.at[kind],
            dst_ref=twin_in.at[kind],
            send_sem=half_send.at[kind],
            recv_sem=half_recv.at[kind],
            device_id=at(chip, other),
            device_id_type=MESH,
        )

    returned = (back_rows_ref, back_grads_ref)

    def give_back(kind, by):
        where = (chip + by) % EXPERTS
        return pltpu.make_async_remote_copy(
            src_ref=sums_ref.at[kind, chunk(where)],
            dst_ref=returned[kind].at[chunk(chip)],
            send_sem=ret_send.at[kind, by - 1],
            recv_sem=ret_recv.at[kind, by - 1],
            device_id=at(where, core),
            device_id_type=MESH,
        )

    started = []
    for kind in (0, 1):
        for by in range(1, EXPERTS):
            copy = dispatch(kind, by)
            copy.start()
            started.append(copy)
    for by in range(1, 8):
        copy = down(by, ctx)
        copy.start()
        started.append(copy)
    for copy in loads:
        copy.start()
    for kind in (0, 1):
        source, target = buffers[kind]
        copy = pltpu.make_async_copy(
            source.at[chunk(chip)], target.at[slots(chip, core)], own_sem.at[kind]
        )
        copy.start()
        copy.wait()
        copy = share(kind, 0, core)
        copy.start()
        started.append(copy)

    def arrive(kind):
        for by in range(1, EXPERTS):
            dispatch(kind, by).wait_recv()
            copy = share(kind, by, core)
            copy.start()
            started.append(copy)

    def arrive_shared(kind):
        for by in range(EXPERTS):
            share(kind, by, other).wait_recv()

    def tiles(on, body):
        def step(index, carry):
            start = pl.multiple_of(on * half + index * 256, 256)
            body(pl.ds(start, 256), pl.ds(pl.multiple_of(index * 256, 256), 256))
            return carry

        lax.fori_loop(0, half // 256, step, 0)

    def forward(on, keep):
        def tile(rows, inner):
            x = x_ref[rows]
            gate, up = dot(x, gate_w[...]), dot(x, up_w[...])
            gate_ref[rows], up_ref[rows] = gate, up
            hidden_ref[rows] = (gate * jax.nn.sigmoid(gate) * up).astype(jnp.bfloat16)

        def result(rows, inner):
            keep(inner, dot(hidden_ref[rows], down_w[...]))

        tiles(on, tile)
        if on is core:
            for by in range(1, 8):
                down(by, (ctx - by + 8) % 8).wait_recv()
        tiles(on, result)

    def backward(on, keep):
        def tile(rows, inner):
            hidden_grad = dot_nt(g_ref[rows], down_w[...])
            gate, up = gate_ref[rows], up_ref[rows]
            sigmoid = jax.nn.sigmoid(gate)
            d_gate[rows] = (
                hidden_grad * up * sigmoid * (1.0 + gate * (1.0 - sigmoid))
            ).astype(jnp.bfloat16)
            d_up[rows] = (hidden_grad * gate * sigmoid).astype(jnp.bfloat16)
            keep(inner, dot_nt(d_gate[rows], gate_w[...]) + dot_nt(d_up[rows], up_w[...]))

        tiles(on, tile)

    def keep_mine(kind):
        def keep(rows, values):
            mine_ref[kind, rows] = values

        return keep

    def keep_twin(kind):
        def keep(rows, values):
            twin_out[kind, rows] = values.astype(jnp.bfloat16)

        return keep

    def finish(kind):
        exchange(kind).wait_recv()

        def step(index, carry):
            rows = pl.ds(pl.multiple_of(index * 128, 128), 128)
            sums_ref[kind, rows] = (
                mine_ref[kind, rows] + twin_in[kind, rows].astype(jnp.float32)
            ).astype(jnp.bfloat16)
            return carry

        lax.fori_loop(0, half // 128, step, 0)
        for by in range(1, EXPERTS):
            copy = give_back(kind, by)
            copy.start()
            started.append(copy)
        copy = pltpu.make_async_copy(
            sums_ref.at[kind, chunk(chip)], returned[kind].at[chunk(chip)], own_sem.at[kind]
        )
        copy.start()
        copy.wait()

    arrive(0)
    for copy in loads:
        copy.wait()
    forward(core, keep_mine(0))
    arrive(1)
    arrive_shared(0)
    forward(other, keep_twin(0))
    copy = exchange(0)
    copy.start()
    started.append(copy)
    backward(core, keep_mine(1))
    finish(0)
    arrive_shared(1)
    backward(other, keep_twin(1))
    copy = exchange(1)
    copy.start()
    started.append(copy)

    def down_tile(index, carry):
        lanes = pl.ds(pl.multiple_of(index * 256, 256), 256)
        part = dot_tn(hidden_ref[:, lanes], g_ref[...]).astype(jnp.bfloat16)
        d_down_ref[2 * index] = part[:128]
        d_down_ref[2 * index + 1] = part[128:]
        return carry

    lax.fori_loop(0, 4, down_tile, 0)
    finish(1)

    def gate_tile(index, carry):
        lanes = pl.ds(pl.multiple_of(index * 256, 256), 256)
        for start, grad in ((0, d_gate), (96, d_up)):
            part = dot_tn(x_ref[...], grad[:, lanes]).astype(jnp.bfloat16)
            for piece in range(8):
                d_gate_up_ref[piece, start : start + 96, lanes] = part[piece * 96 : piece * 96 + 96]
        return carry

    lax.fori_loop(0, 4, gate_tile, 0)
    for kind in (0, 1):
        for by in range(1, EXPERTS):
            give_back(kind, by).wait_recv()
    for copy in started:
        copy.wait_send()


def run_experts(rows, grads, gate_up, down):
    vmem, anywhere = pl.BlockSpec(memory_space=pltpu.VMEM), pl.BlockSpec(memory_space=pl.ANY)
    low, wide = jnp.bfloat16, jnp.float32
    half, whole = EXPERTS * SLOTS, 2 * EXPERTS * SLOTS
    dma = pltpu.SemaphoreType.DMA
    return pl.pallas_call(
        experts_kernel,
        out_shape=[
            jax.ShapeDtypeStruct((half, WIDTH), low),
            jax.ShapeDtypeStruct((half, WIDTH), low),
            jax.ShapeDtypeStruct((8, 192, 1024), low),
            jax.ShapeDtypeStruct((8, 128, WIDTH), low),
        ],
        in_specs=[vmem, vmem, anywhere, anywhere],
        out_specs=[vmem] * 4,
        scratch_shapes=[
            pltpu.VMEM((WIDTH, 1024), low),
            pltpu.VMEM((WIDTH, 1024), low),
            pltpu.VMEM((1024, WIDTH), low),
            pltpu.VMEM((whole, WIDTH), low),
            pltpu.VMEM((whole, WIDTH), low),
            pltpu.VMEM((whole, 1024), wide),
            pltpu.VMEM((whole, 1024), wide),
            pltpu.VMEM((whole, 1024), low),
            pltpu.VMEM((whole, 1024), low),
            pltpu.VMEM((whole, 1024), low),
            pltpu.VMEM((2, half, WIDTH), wide),
            pltpu.VMEM((2, half, WIDTH), low),
            pltpu.VMEM((2, half, WIDTH), low),
            pltpu.VMEM((2, half, WIDTH), low),
            dma((7,)),
            dma((7,)),
            dma((17,)),
            dma((2, 7)),
            dma((2, 7)),
            dma((2, 8)),
            dma((2, 8)),
            dma((2,)),
            dma((2,)),
            dma((2, 7)),
            dma((2, 7)),
            dma((2,)),
        ],
        name="run_experts",
        compiler_params=pltpu.CompilerParams(
            collective_id=3, has_side_effects=True, vmem_limit_bytes=56 * 2**20
        ),
    )(rows, grads, gate_up, down)


def split(values):
    high = values.astype(jnp.bfloat16)
    low = (values - high.astype(jnp.float32)).astype(jnp.bfloat16)
    return jnp.concatenate([high, low], axis=1)


def back_kernel(
    blocks_ref, w_ref, small_ref, cos_in, sin_in, cos_out, sin_out, left_ref, right_ref, place_ref,
    prev_ref, wres_ref, routes_ref, cot_ref,
    state_ref, normed_ref, att_ref, lse_ref, q_ref, keys_ref, values_ref, info_ref, proj_ref,
    back_rows_ref, back_grads_ref, d_gate_up, d_down,
    out_ref, prev_grad_ref, total_ref, tokens_grad_ref, sums_ref, few_ref,
    gate_out, up_out, down_out,
    *scratch,
):
    (
        qt_ref, ot_ref, o_ref, qm_ref, bias_ref, inner_ref, dqt_ref, gain_ref, dk_ref, dv_ref,
        prev_pad, wres_pad, dw_ref, few_sum, kv_ref, tok_ref, mine_ref, kv_sem, own_ref, state_grad_ref, others_ref, grads_ref, block_in,
        gate_up_in, down_in, small_in, small_sum,
        block_send, block_recv, exp_send, exp_recv, load_sem,
        net_send, net_recv, twin_send, twin_recv, small_send, small_recv,
        *more,
    ) = scratch
    twin_in, held, in_one, in_two, in_three, sum_one, sum_two = (
        more[0], more[1], more[2:5], more[5:8], more[8:11], more[11:14], more[14:17]
    )
    tables = (cos_in, sin_in, cos_out, sin_out)
    ctx, fsdp = lax.axis_index("ctx"), lax.axis_index("fsdp")
    *spot, core = place()
    spot = tuple(spot)
    twin = device_at(*spot, 1 - core)
    started = []
    greet(torus_peers(spot, core) + sequence_peers(spot, core))

    def expert(kind, by):
        source, target = ((d_gate_up, gate_up_in), (d_down, down_in))[kind]
        where = (ctx + by) % 8
        return pltpu.make_async_remote_copy(
            src_ref=source.at[where],
            dst_ref=target.at[by],
            send_sem=exp_send.at[kind, by - 1],
            recv_sem=exp_recv.at[kind, by - 1],
            device_id={"ctx": where, "fsdp": fsdp},
            device_id_type=MESH,
        )

    for kind in (0, 1):
        for by in range(1, 8):
            copy = expert(kind, by)
            copy.start()
            started.append(copy)
    kept = [
        pltpu.make_async_copy(d_gate_up.at[ctx], gate_up_in.at[0], load_sem.at[0]),
        pltpu.make_async_copy(d_down.at[ctx], down_in.at[0], load_sem.at[1]),
    ]
    own_block = pltpu.make_async_copy(blocks_ref.at[ctx], mine_ref, load_sem.at[2])
    own_block.start()
    for copy in kept:
        copy.start()

    def load_kv(index, slot):
        return [
            pltpu.make_async_copy(source.at[index], kv_ref.at[slot, kind], kv_sem.at[slot, kind])
            for kind, source in enumerate((keys_ref, values_ref))
        ] + [pltpu.make_async_copy(blocks_ref.at[index], tok_ref.at[slot], kv_sem.at[slot, 2])]

    for copy in load_kv(0, 0):
        copy.start()

    def block_copy(by, target):
        return pltpu.make_async_remote_copy(
            src_ref=others_ref.at[target],
            dst_ref=block_in.at[by - 1],
            send_sem=block_send.at[by - 1],
            recv_sem=block_recv.at[by - 1],
            device_id={"ctx": target, "fsdp": fsdp},
            device_id_type=MESH,
        )

    across = small_ref[...].astype(jnp.float32).T
    gain_one, gain_two = across[18:19], across[19:20]
    value_rows = across[16:18]

    lanes = lax.broadcasted_iota(jnp.int32, (BLK, 128), 1)
    info = info_ref[...]
    gates = (info[:, 0:1], info[:, 1:2])
    slots = lax.broadcasted_iota(jnp.int32, (BLK, EXPERTS * SLOTS), 1).astype(jnp.float32)
    tables_of = [
        (slots == info[:, 2 + k : 3 + k]).astype(jnp.float32).astype(jnp.bfloat16) for k in (0, 1)
    ]
    route_rows = routes_ref[...].astype(jnp.float32)
    routes = (column(route_rows[0:1]), column(route_rows[1:2]))
    hots = [lanes.astype(jnp.float32) == routes[k] for k in (0, 1)]
    named = [
        [(routes[k] == EXPERTS + 1 + kind).astype(jnp.float32) for kind in range(3)] for k in (0, 1)
    ]
    proj = proj_ref[...]
    mixes = []
    for c in (0, 1):
        first, second = proj[:, 12 + 2 * c : 13 + 2 * c], proj[:, 13 + 2 * c : 14 + 2 * c]
        top = jnp.maximum(first, second)
        first, second = jnp.exp(first - top), jnp.exp(second - top)
        mixes.append((first / (first + second), second / (first + second)))
    normed_low = normed_ref[...]
    normed_two = normed_low.astype(jnp.float32)
    upstream_low = cot_ref[...]
    upstream = upstream_low.astype(jnp.float32)
    state = state_ref[...]
    back_rows = back_rows_ref[...]
    result = state
    gate_grads = []
    for k in (0, 1):
        copy, one, two = named[k]
        pair = dot(tables_of[k], back_rows)
        pair = pair + (copy + one * mixes[0][0] + two * mixes[1][0]) * normed_two
        pair = pair + (one * mixes[0][1]) * value_rows[0:1] + (two * mixes[1][1]) * value_rows[1:2]
        result = result + gates[k] * pair
        gate_grads.append(jnp.sum(pair * upstream, axis=1, keepdims=True))
    out_ref[...] = result.astype(jnp.bfloat16)
    inner = gates[0] * gate_grads[0] + gates[1] * gate_grads[1]
    logit_grad = jnp.zeros((BLK, 128), jnp.float32)
    for k in (0, 1):
        logit_grad = logit_grad + jnp.where(hots[k], gates[k] * (gate_grads[k] - inner), 0.0)
    pad_routing(prev_ref, wres_ref, prev_pad, wres_pad)
    prev_grad_ref[...] = lax.dot_general(
        wres_pad[...], logit_grad, (((1,), (1,)), ((), ())),
        precision=highest, preferred_element_type=jnp.float32,
    )[:16]
    small_sum[3] = jnp.dot(
        prev_pad[...], logit_grad, precision=highest, preferred_element_type=jnp.float32
    )[:16]
    on_normed = jnp.sum(normed_two * upstream, axis=1, keepdims=True)
    on_vectors = dot(upstream_low, small_ref[...])
    flat = logit_grad
    weight_up = gates[0] * named[0][0] + gates[1] * named[1][0]
    vector_weights = jnp.zeros((BLK, 128), jnp.float32)
    for c in (0, 1):
        scale = gates[0] * named[0][1 + c] + gates[1] * named[1][1 + c]
        mix_0, mix_1 = mixes[c]
        m_0, m_1 = scale * on_normed, scale * on_vectors[:, 16 + c : 17 + c]
        mean = mix_0 * m_0 + mix_1 * m_1
        flat = flat + jnp.where(lanes == 12 + 2 * c, mix_0 * (m_0 - mean), 0.0)
        flat = flat + jnp.where(lanes == 13 + 2 * c, mix_1 * (m_1 - mean), 0.0)
        weight_up = weight_up + mix_0 * scale
        vector_weights = vector_weights + jnp.where(lanes == 16 + c, mix_1 * scale, 0.0)
    flat_split = split(flat)
    normed_grad = dot_nt(flat_split, jnp.concatenate([small_ref[...]] * 2, axis=1))
    normed_grad = normed_grad + weight_up * upstream
    normed_grad = normed_grad + dot(tables_of[0] + tables_of[1], back_grads_ref[...])
    normed_across = normed_two.T.astype(jnp.bfloat16)
    upstream_across = upstream.T.astype(jnp.bfloat16)
    small_grad = dot(normed_across, flat_split)
    small_vector = dot(upstream_across, split(vector_weights))
    small_grad = small_grad[:, :128] + small_grad[:, 128:] + small_vector[:, :128] + small_vector[:, 128:]
    scale_two = rms_rows(state)
    weighted = normed_grad * gain_two
    state_grad = (
        upstream
        + scale_two * weighted
        - state * (scale_two**3 * jnp.mean(weighted * state, axis=-1, keepdims=True))
    )
    state_grad_ref[...] = state_grad
    gain_two_row = jnp.sum(normed_grad * state * scale_two, axis=0, keepdims=True)
    state_low = state_grad.astype(jnp.bfloat16)
    attended = att_ref[...]
    dw_ref[3] = dot(attended.astype(jnp.bfloat16), state_low)
    att_grad = dot_nt(state_low, w_ref[3])
    blank = jnp.zeros((HDIM, BLK), jnp.bfloat16)
    low_half = lax.broadcasted_iota(jnp.int32, (BLK, 128), 1) < HDIM
    none = jnp.zeros((BLK, 128), jnp.bfloat16)
    inner_ref[...] = jnp.zeros_like(inner_ref)
    for pair in range(PAIRS):
        part = att_grad[:, pair * 128 : pair * 128 + 128].astype(jnp.bfloat16)
        across_o = part.astype(jnp.float32).T
        products = across_o * attended[pair * 128 : pair * 128 + 128]
        across_o = across_o.astype(jnp.bfloat16)
        across_q = q_ref[pair].astype(jnp.float32).T.astype(jnp.bfloat16)
        for half in (0, 1):
            head = 2 * pair + half
            rows = slice(half * HDIM, half * HDIM + HDIM)
            inner_ref[head : head + 1] = jnp.sum(products[rows], axis=0, keepdims=True)
            order = (lambda a, b: [a, b]) if half == 0 else (lambda a, b: [b, a])
            ot_ref[head] = jnp.concatenate(order(across_o[rows], blank), axis=0)
            qt_ref[head] = jnp.concatenate(order(across_q[rows], blank), axis=0)
        o_ref[pair, :BLK] = jnp.where(low_half, part, none)
        o_ref[pair, BLK:] = jnp.where(low_half, none, part)
        qm_ref[pair, :BLK] = jnp.where(low_half, q_ref[pair], none)
        qm_ref[pair, BLK:] = jnp.where(low_half, none, q_ref[pair])
    dqt_ref[...] = jnp.zeros_like(dqt_ref)
    dw_ref[1] = jnp.zeros((WIDTH, WIDTH), jnp.float32)
    dw_ref[2] = jnp.zeros((WIDTH, WIDTH), jnp.float32)
    gain_ref[...] = jnp.zeros_like(gain_ref)

    own_block.wait()

    def normed_block(array):
        wide = array[:BLK].astype(jnp.float32)
        scaled = wide * rms_rows(wide)
        return scaled, (scaled * gain_one).T.astype(jnp.bfloat16)

    def block(index, carry):
        slot = index % 2
        for copy in load_kv(index, slot):
            copy.wait()

        @pl.when(index < ctx)
        def _():
            for copy in load_kv(index + 1, 1 - slot):
                copy.start()

        mask_bias(tok_ref.at[slot], mine_ref, bias_ref, ctx, index)
        cosine, sine = turning(index, tables)
        for pair in range(PAIRS):
            key, value = kv_ref[slot, 0, pair], kv_ref[slot, 1, pair]
            key_across = key.astype(jnp.float32).T.astype(jnp.bfloat16)
            weights, score_grads = [], []
            for half in (0, 1):
                head = 2 * pair + half
                scores = dot(key, qt_ref[head]) + bias_ref[...]
                weight = jnp.exp(scores - lse_ref[head : head + 1])
                weight_grad = dot(value, ot_ref[head])
                score_grad = (weight * (weight_grad - inner_ref[head : head + 1])).astype(jnp.bfloat16)
                weights.append(weight.astype(jnp.bfloat16))
                score_grads.append(score_grad)
                rows = slice(head * HDIM, head * HDIM + HDIM)
                dqt_ref[rows] += dot(key_across[half * HDIM : half * HDIM + HDIM], score_grad)
            lanes = slice(pair * 128, pair * 128 + 128)
            dv_ref[:, lanes] = dot(jnp.concatenate(weights, axis=1), o_ref[pair]).astype(jnp.bfloat16)
            dk = dot(jnp.concatenate(score_grads, axis=1), qm_ref[pair])
            dk_ref[:, lanes] = (dk * cosine - swapped(dk) * sine).astype(jnp.bfloat16)
        scaled, normed_across = normed_block(tok_ref.at[slot])
        dw_ref[1] += dot(normed_across, dk_ref[...])
        dw_ref[2] += dot(normed_across, dv_ref[...])
        first = dot_nt(dk_ref[...], w_ref[1]) + dot_nt(dv_ref[...], w_ref[2])
        gain_ref[...] += jnp.sum(first * scaled, axis=0, keepdims=True)

        @pl.when(index < ctx)
        def _():
            others_ref[index] = first.astype(jnp.bfloat16)
            block_copy(ctx - index, index).start()

        @pl.when(index == ctx)
        def _():
            own_ref[...] = first

        return carry

    lax.fori_loop(0, ctx + 1, block, 0)
    cosine, sine = turning(ctx, tables)
    for pair in range(PAIRS):
        lanes = slice(pair * 128, pair * 128 + 128)
        dq = dqt_ref[lanes, :].T * (HDIM**-0.5)
        dk_ref[:, lanes] = (dq * cosine - swapped(dq) * sine).astype(jnp.bfloat16)
    scaled, normed_across = normed_block(mine_ref)
    dw_ref[0] = dot(normed_across, dk_ref[...])
    first = dot_nt(dk_ref[...], w_ref[0])
    own_ref[...] += first
    gain_one_row = gain_ref[...] + jnp.sum(first * scaled, axis=0, keepdims=True)
    lanes = lax.broadcasted_iota(jnp.int32, (WIDTH, 128), 1)
    ones = jnp.broadcast_to(gain_one_row, (128, WIDTH)).T
    twos = jnp.broadcast_to(gain_two_row, (128, WIDTH)).T
    few = jnp.where(lanes == 18, ones, jnp.where(lanes == 19, twos, small_grad))
    few_sum[...] = few

    def share(x):
        return pltpu.make_async_remote_copy(
            src_ref=grads_ref.at[x, :, :, 1 - core],
            dst_ref=twin_in.at[x],
            send_sem=twin_send.at[x],
            recv_sem=twin_recv.at[x],
            device_id=twin,
            device_id_type=MESH,
        )

    def pack(group, carry):
        rows = pl.ds(pl.multiple_of(group * 48, 16), 48)

        def lane_half(start):
            return jnp.concatenate(
                [dw_ref[w, rows, start : start + 384] for w in range(4)], axis=0
            ).astype(jnp.bfloat16)

        from_left = dot(left_ref[...], lane_half(0))
        from_right = dot(right_ref[...], lane_half(384))
        placed = dot(place_ref[...], few_sum[rows].astype(jnp.bfloat16))
        whole = jnp.concatenate(
            [from_left[:128], from_right[:128], from_left[128:] + from_right[128:], placed], axis=1
        )
        grads_ref[group // 4, group % 4] = whole.astype(jnp.bfloat16).reshape(4, 2, 16, 1280)
        return carry

    for x in range(4):
        lax.fori_loop(4 * x, 4 * x + 4, pack, 0)
        copy = share(x)
        copy.start()
        started.append(copy)

    def net(part, step, by, source, target):
        axis = PART_ORDER[part][2 - step]
        return pltpu.make_async_remote_copy(
            src_ref=source,
            dst_ref=target,
            send_sem=net_send.at[part, step, by - 1],
            recv_sem=net_recv.at[part, step, by - 1],
            device_id=device_at(*shifted(spot, axis, by), core),
            device_id_type=MESH,
        )

    def small(axis, by, source, slot):
        device = twin if axis == 3 else device_at(*shifted(spot, axis, by), core)
        return pltpu.make_async_remote_copy(
            src_ref=source,
            dst_ref=small_in.at[axis, slot],
            send_sem=small_send.at[axis, by - 1],
            recv_sem=small_recv.at[axis, by - 1],
            device_id=device,
            device_id_type=MESH,
        )

    copy = small(3, 1, small_sum.at[3], core)
    copy.start()
    started.append(copy)

    for x in range(4):
        share(x).wait_recv()

        def add_pair(index, carry, x=x):
            z, y = index // 4, index % 4
            held[x, z, y] = (
                grads_ref[x, z, y, core].astype(jnp.float32) + twin_in[x, z, y].astype(jnp.float32)
            ).astype(jnp.bfloat16)
            return carry

        lax.fori_loop(0, 16, add_pair, 0, unroll=2)

    def lanes_of(part):
        return pl.ds(PART_START[part], PART_LANES[part])

    for part in range(3):
        axis = PART_ORDER[part][2]
        for by in (1, 2, 3):
            at = shifted(spot, axis, by)[axis]
            index = tuple(at if a == axis else slice(None) for a in range(3))
            copy = net(
                part, 0, by, held.at[(*index, slice(None), lanes_of(part))], in_one[part].at[by - 1]
            )
            copy.start()
            started.append(copy)

    small(3, 1, small_sum.at[3], 1 - core).wait_recv()
    small_in[3, core] = small_sum[3]
    small_sum[0] = small_in[3, 0] + small_in[3, 1]
    for by in (1, 2, 3):
        copy = small(0, by, small_sum.at[0], spot[0])
        copy.start()
        started.append(copy)

    def small_step(axis):
        for by in (1, 2, 3):
            small(axis, by, small_sum.at[axis], shifted(spot, axis, -by)[axis]).wait_recv()
        small_in[axis, spot[axis]] = small_sum[axis]
        total = small_in[axis, 0] + small_in[axis, 1] + small_in[axis, 2] + small_in[axis, 3]
        if axis == 2:
            total_ref[...] = total
            return
        small_sum[axis + 1] = total
        for by in (1, 2, 3):
            copy = small(axis + 1, by, small_sum.at[axis + 1], spot[axis + 1])
            copy.start()
            started.append(copy)

    for part in range(3):
        first, second, third = PART_ORDER[part]
        for by in (1, 2, 3):
            net(part, 0, by, in_one[part].at[by - 1], in_one[part].at[by - 1]).wait_recv()
        rest = tuple(a for a in (0, 1, 2) if a != third)
        lanes = slice(PART_START[part], PART_START[part] + PART_LANES[part])

        def add_four(index, carry, part=part, third=third, rest=rest, lanes=lanes):
            at = {rest[0]: index // 4, rest[1]: index % 4, third: spot[third]}
            total = held[at[0], at[1], at[2], :, lanes].astype(jnp.float32)
            for by in range(3):
                total = total + in_one[part][by, index // 4, index % 4].astype(jnp.float32)
            sum_one[part][index // 4, index % 4] = total.astype(jnp.bfloat16)
            return carry

        lax.fori_loop(0, 16, add_four, 0, unroll=2)
        for by in (1, 2, 3):
            at = shifted(spot, second, by)[second]
            source = sum_one[part].at[at] if second == rest[0] else sum_one[part].at[:, at]
            copy = net(part, 1, by, source, in_two[part].at[by - 1])
            copy.start()
            started.append(copy)
    small_step(0)

    for copy in kept:
        copy.wait()
    for kind in (0, 1):
        for by in range(1, 8):
            expert(kind, by).wait_recv()

    def sum_eight(source, rows):
        total = source[0, rows].astype(jnp.float32)
        for by in range(1, 8):
            total = total + source[by, rows].astype(jnp.float32)
        return total

    def expert_rows(index, carry):
        rows = pl.ds(pl.multiple_of(index * 16, 16), 16)
        gate_out[rows] = sum_eight(gate_up_in, rows)
        up_out[rows] = sum_eight(gate_up_in, pl.ds(pl.multiple_of(96 + index * 16, 16), 16))
        return carry

    lax.fori_loop(0, 6, expert_rows, 0)

    def down_rows(index, carry):
        rows = pl.ds(pl.multiple_of(index * 16, 16), 16)
        down_out[rows] = sum_eight(down_in, rows)
        return carry

    lax.fori_loop(0, 8, down_rows, 0)

    for part in range(3):
        first, second, third = PART_ORDER[part]
        for by in (1, 2, 3):
            net(part, 1, by, in_two[part].at[by - 1], in_two[part].at[by - 1]).wait_recv()
        rest = tuple(a for a in (0, 1, 2) if a != third)
        for index in range(4):
            if second == rest[0]:
                total = sum_one[part][spot[second], index].astype(jnp.float32)
            else:
                total = sum_one[part][index, spot[second]].astype(jnp.float32)
            for by in range(3):
                total = total + in_two[part][by, index].astype(jnp.float32)
            sum_two[part][index] = total.astype(jnp.bfloat16)
        for by in (1, 2, 3):
            at = shifted(spot, first, by)[first]
            copy = net(part, 2, by, sum_two[part].at[at], in_three[part].at[by - 1])
            copy.start()
            started.append(copy)
    small_step(1)

    for by in range(1, 8):

        @pl.when(ctx + by < 8)
        def _(by=by):
            block_copy(by, ctx).wait_recv()
            own_ref[...] += block_in[by - 1].astype(jnp.float32)

        @pl.when(ctx - by >= 0)
        def _(by=by):
            block_copy(by, ctx - by).wait_send()

    wide = mine_ref[:BLK].astype(jnp.float32)
    scale = rms_rows(wide)
    weighted = own_ref[...] * gain_one
    tokens_grad_ref[...] = (
        state_grad_ref[...]
        + scale * weighted
        - wide * (scale**3 * jnp.mean(weighted * wide, axis=-1, keepdims=True))
    )
    finals = []
    for part in range(3):
        first = PART_ORDER[part][0]
        for by in (1, 2, 3):
            net(part, 2, by, in_three[part].at[by - 1], in_three[part].at[by - 1]).wait_recv()
        total = sum_two[part][spot[first]].astype(jnp.float32)
        for by in range(3):
            total = total + in_three[part][by].astype(jnp.float32)
        finals.append(total)
    final = jnp.concatenate(finals, axis=1)
    sums_ref[:16] = final[:, :768]
    sums_ref[16:] = jnp.concatenate([final[:8, 768:1152], final[8:, 768:1152]], axis=1)
    few_ref[...] = final[:8, 1152:]
    small_step(2)
    for copy in started:
        copy.wait_send()


def run_back(blocks, weights, smalls, prev, wres, routes, cot, kept, back_rows, back_grads, d_gate_up, d_down):
    vmem, anywhere = pl.BlockSpec(memory_space=pltpu.VMEM), pl.BlockSpec(memory_space=pl.ANY)
    shape = jax.ShapeDtypeStruct
    low, wide = jnp.bfloat16, jnp.float32
    dma = pltpu.SemaphoreType.DMA
    left, right, small = (jnp.asarray(t.T, low) for t in placing_tables())
    by_part = lambda *lead: [pltpu.VMEM((*lead, 16, lanes), low) for lanes in PART_LANES]
    return pl.pallas_call(
        back_kernel,
        out_shape=[
            shape((BLK, WIDTH), low),
            shape((16, BLK), wide),
            shape((16, 128), wide),
            shape((BLK, WIDTH), wide),
            shape((24, WIDTH), wide),
            shape((8, 128), wide),
            shape((96, 1024), wide),
            shape((96, 1024), wide),
            shape((128, WIDTH), wide),
        ],
        in_specs=[anywhere] + [vmem] * 18 + [anywhere] * 2 + [vmem] * 4 + [anywhere] * 2,
        out_specs=[vmem] * 9,
        scratch_shapes=[
            pltpu.VMEM((HEADS, 128, BLK), low),
            pltpu.VMEM((HEADS, 128, BLK), low),
            pltpu.VMEM((PAIRS, 2 * BLK, 128), low),
            pltpu.VMEM((PAIRS, 2 * BLK, 128), low),
            pltpu.VMEM((BLK, BLK), wide),
            pltpu.VMEM((16, BLK), wide),
            pltpu.VMEM((WIDTH, BLK), wide),
            pltpu.VMEM((1, WIDTH), wide),
            pltpu.VMEM((BLK, WIDTH), low),
            pltpu.VMEM((BLK, WIDTH), low),
            pltpu.VMEM((128, BLK), wide),
            pltpu.VMEM((128, 128), wide),
            pltpu.VMEM((4, WIDTH, WIDTH), wide),
            pltpu.VMEM((WIDTH, 128), wide),
            pltpu.VMEM((2, 2, PAIRS, BLK, 128), low),
            pltpu.VMEM((2, BLK + 16, WIDTH), low),
            pltpu.VMEM((BLK + 16, WIDTH), low),
            dma((2, 3)),
            pltpu.VMEM((BLK, WIDTH), wide),
            pltpu.VMEM((BLK, WIDTH), wide),
            pltpu.VMEM((8, BLK, WIDTH), low),
            pltpu.VMEM((4, 4, 4, 2, 16, 1280), low),
            pltpu.VMEM((7, BLK, WIDTH), low),
            pltpu.VMEM((8, 192, 1024), low),
            pltpu.VMEM((8, 128, WIDTH), low),
            pltpu.VMEM((4, 4, 16, 128), wide),
            pltpu.VMEM((4, 16, 128), wide),
            dma((7,)),
            dma((7,)),
            dma((2, 7)),
            dma((2, 7)),
            dma((3,)),
            dma((3, 3, 3)),
            dma((3, 3, 3)),
            dma((4,)),
            dma((4,)),
            dma((4, 3)),
            dma((4, 3)),
            pltpu.VMEM((4, 4, 4, 16, 1280), low),
            pltpu.VMEM((4, 4, 4, 16, 1280), low),
            *by_part(3, 4, 4),
            *by_part(3, 4),
            *by_part(3),
            *by_part(4, 4),
            *by_part(4),
        ],
        name="back",
        compiler_params=pltpu.CompilerParams(
            collective_id=2, has_side_effects=True, vmem_limit_bytes=62 * 2**20
        ),
    )(
        blocks, weights, smalls, *rope_tables(), left, right, small, prev, wres, routes, cot,
        *kept, back_rows, back_grads, d_gate_up, d_down,
    )


def finish_kernel(
    out_in, tokens_in, gate_in, up_in, down_in, prev_in, total_in, sums_in, few_in,
    out, tokens_grad, gate, up, down, prev, total, sum_q, sum_k, sum_v, sum_o,
    gain_one, gain_two, router, constant, vectors, prev_at, total_at, sums_at, few_at, sems,
):
    pairs = (
        (prev_in, prev_at), (total_in, total_at), (sums_in, sums_at), (few_in, few_at),
        (tokens_in, tokens_grad), (out_in, out), (gate_in, gate), (up_in, up), (down_in, down),
    )
    copies = [
        pltpu.make_async_copy(source, target, sems.at[index])
        for index, (source, target) in enumerate(pairs)
    ]
    for copy in copies:
        copy.start()
    for copy in copies[:4]:
        copy.wait()
    prev[:, 0, :] = prev_at[:NALL]
    total[...] = total_at[:NALL, :NALL]
    for weight, ref in enumerate((sum_q, sum_k, sum_v, sum_o)):
        ref[...] = sums_at[weight * 6 : weight * 6 + 6]
    few = few_at[...]
    router[...] = few[:6, :NALL]
    tall = jnp.concatenate([few, jnp.zeros((120, 128), jnp.float32)], axis=0).T
    constant[...] = tall[12:16, :6]
    vectors[...] = tall[16:18, :6]
    gain_one[...] = tall[18:19, :6]
    gain_two[...] = tall[19:20, :6]
    for copy in copies[4:]:
        copy.wait()


def finish(out, tokens_grad, gate, up, down, prev, total, sums, few):
    vmem = pl.BlockSpec(memory_space=pltpu.VMEM)
    shape = jax.ShapeDtypeStruct
    wide = jnp.float32
    like = [shape(a.shape, a.dtype) for a in (out, tokens_grad, gate, up, down)]
    few_shapes = [(1, 6), (1, 6), (6, NALL), (4, 6), (2, 6)]
    return pl.pallas_call(
        finish_kernel,
        out_shape=like
        + [shape((NALL, 1, BLK), wide), shape((NALL, NALL), wide)]
        + [shape((6, WIDTH), wide)] * 4
        + [shape(s, wide) for s in few_shapes],
        in_specs=[pl.BlockSpec(memory_space=pl.ANY)] * 9,
        out_specs=[vmem] * 16,
        scratch_shapes=[
            *(pltpu.VMEM(a.shape, a.dtype) for a in (prev, total, sums, few)),
            pltpu.SemaphoreType.DMA((9,)),
        ],
        name="finish",
        compiler_params=pltpu.CompilerParams(vmem_limit_bytes=62 * 2**20),
    )(out, tokens_grad, gate, up, down, prev, total, sums, few)


def on_device(
    tokens, prev_logits, routes, segments, rank_order, norm_first, w_query, w_key, w_value, w_output,
    norm_second, w_router, w_residual, w_constant, v_constant, w_gate, w_up, w_down, cotangent,
):
    few = [w_router, w_constant.T, v_constant.T, norm_first[None], norm_second[None]]
    prev = jnp.transpose(prev_logits, (2, 0, 1))
    (
        state, normed, att, lse, q, keys, values, rows, grads, info, proj, blocks, weights, smalls, gate_up,
    ) = run_front(
        [w_query, w_key, w_value, w_output], few, tokens[0], segments, w_gate[0], w_up[0],
        prev, w_residual, routes[0].T, rank_order[0], cotangent[0],
    )
    back_rows, back_grads, d_gate_up, d_down = run_experts(rows, grads, gate_up, w_down[0])
    (
        out, prev_grad, residual, tokens_grad, sums, small, d_gate, d_up, d_down,
    ) = run_back(
        blocks, weights, smalls, prev, w_residual, routes[0].T, cotangent[0],
        (state, normed, att, lse, q, keys, values, info, proj), back_rows, back_grads,
        d_gate_up, d_down,
    )
    (
        out, tokens_grad, d_gate, d_up, d_down, prev_grad, residual, sum_q, sum_k, sum_v, sum_o,
        gain_one, gain_two, router, constant, vectors,
    ) = finish(out, tokens_grad, d_gate, d_up, d_down, prev_grad, residual, sums, small)
    return (
        out[None],
        tokens_grad[None],
        jnp.transpose(prev_grad, (1, 2, 0)),
        gain_one[0],
        sum_q,
        sum_k,
        sum_v,
        sum_o,
        gain_two[0],
        router,
        residual,
        constant.T,
        vectors.T,
        d_gate[None],
        d_up[None],
        d_down[None],
    )


def solution(mesh):
    in_specs = (
        P("fsdp", "ctx", None),
        P("fsdp", "ctx", None),
        P("fsdp", "ctx", None),
        P("fsdp", "ctx"),
        P("fsdp", "ctx", None),
        P(("ctx", "fsdp")),
        P(("ctx", "fsdp"), None),
        P(("ctx", "fsdp"), None),
        P(("ctx", "fsdp"), None),
        P(("ctx", "fsdp"), None),
        P(("ctx", "fsdp")),
        P(("ctx", "fsdp"), None),
        P(),
        P(("ctx", "fsdp"), None),
        P(("ctx", "fsdp"), None),
        P("fsdp", "ctx", None),
        P("fsdp", "ctx", None),
        P("fsdp", "ctx", None),
        P("fsdp", "ctx", None),
    )
    out_specs = (
        P("fsdp", "ctx", None),
        P("fsdp", "ctx", None),
        P("fsdp", "ctx", None),
        P(("ctx", "fsdp")),
        P(("ctx", "fsdp"), None),
        P(("ctx", "fsdp"), None),
        P(("ctx", "fsdp"), None),
        P(("ctx", "fsdp"), None),
        P(("ctx", "fsdp")),
        P(("ctx", "fsdp"), None),
        P(),
        P(("ctx", "fsdp"), None),
        P(("ctx", "fsdp"), None),
        P("fsdp", "ctx", None),
        P("fsdp", "ctx", None),
        P("fsdp", "ctx", None),
    )
    return jax.shard_map(
        on_device, mesh=mesh, in_specs=in_specs, out_specs=out_specs, check_vma=False
    )
```

time: 382 us -> 312 us (0.82)
  Pallas kernels: 252 us -> 311 us
  waiting for transfers between devices: 45.7 us -> 0 us
  starting transfers between devices: 36.4 us -> 0 us
  local copies, waits for them, and re-layouts: 33.7 us -> 0 us
  other arithmetic: 10.1 us -> 0 us
    all_to_all x4 -> x0, waiting for transfers between devices: 45.7 us -> none  [the longest x2 26.1 us: over_ctx(): lax.all_to_all(jnp.broadcast_to(array[None], (8, *array.shape)), 'ctx', 0...]
    pallas_call x6 -> x3, Pallas kernels: 197 us -> 242 us  [the longest x1 136 us: run_back(): pl.pallas_call(back_kernel, out_shape=[shape((BLK, WIDTH), low), shape((1...]
    all_to_all x4 -> x0, starting transfers between devices: 36.4 us -> none  [the longest x2 20.7 us: over_ctx(): lax.all_to_all(jnp.broadcast_to(array[None], (8, *array.shape)), 'ctx', 0...]
    unnamed x93 -> x0, local copies, waits for them, and re-layouts: 19.9 us -> none
    pallas_call x1, Pallas kernels: 55.5 us -> 68.3 us  [run_experts(): pl.pallas_call(experts_kernel, out_shape=[jax.ShapeDtypeStruct((half, WID...]
    broadcast_in_dim x6 -> x0, local copies, waits for them, and re-layouts: 6.71 us -> none  [the longest x2 4.26 us: over_ctx(): jnp.broadcast_to(array[None], (8, *array.shape))]
    concatenate x4 -> x0, other arithmetic: 4.94 us -> none  [the longest x1 1.78 us: on_device(): jnp.concatenate([tokens[0], marks], axis=0)]
    pallas_call x1 -> x0, local copies, waits for them, and re-layouts: 4.86 us -> none  [gather_shards(): pl.pallas_call(gather_kernel, out_shape=[jax.ShapeDtypeStruct((4, 4, 4, 2...]
  transfers between devices with their start and end apart: 4 -> 0, of which waited for: 3 -> 0; matrix products, arithmetic and copies ran while one was open for 3% -> 0% of each run, Pallas kernels for 36% -> 0%
where the time goes in v3:
time: 312 us; the launch traced here: 311 us
  Pallas kernels  311 us (100%)
    pallas_call x1, Pallas kernels, run_back(): pl.pallas_call(back_kernel, out_shape=[shape((BLK, WIDTH), low), shape((1...  136 us
    pallas_call x1, Pallas kernels, run_front(): pl.pallas_call(front_kernel, out_shape=[shape((BLK, WIDTH), wide), shape(...  103 us
    pallas_call x1, Pallas kernels, run_experts(): pl.pallas_call(experts_kernel, out_shape=[jax.ShapeDtypeStruct((half, WID...  68.3 us

profile of v3, /device:TPU:4, one launch (start us, length us, event | category | flops | bytes accessed | tf_op | source)
XLA Modules:
  0.0 311.5 jit_solution(2985200107381184088)
XLA Ops:
  0.7 102.6 %front.1 = (f32[256,768]{1,0:T(8,128)}, bf16[256,768]{1,0:T(8,128)(2,1)}, f32[768,256]{1,0:T(8,128)}, f32[16,256]{1,0:T(8,128)}, bf16[6,256,128]{2,1,0:T(8,128)(...) custom-call(bf16[6,768]{1,0:T(8,128)(2,1)} %wq_ref.1, ...), custom_call_target="tpu_custom_call" | custom-call | tf_op jit(solution)/shard_map/front/pallas_call | solution.py:506
  103.3 68.3 %run_experts.1 = (bf16[512,768]{1,0:T(8,128)(2,1)}, bf16[512,768]{1,0:T(8,128)(2,1)}, bf16[8,192,1024]{2,1,0:T(8,128)(2,1)}, bf16[8,128,768]{2,1,0:T(8,128)(2,1)}) custom-call(bf16[512,768]{1,0:T(8,128)(2,1)} %get-tuple-element.72.rows_ref, bf16[512,768]{1,0:T(8,128)(2,1)} %get-tuple-element.73.grads_ref, ...), custom_call_target="tpu_custom_call" | custom-call | tf_op jit(solution)/shard_map/run_experts/pallas_call | solution.py:817
  171.6 136.5 %back.1 = (bf16[256,768]{1,0:T(8,128)(2,1)}, f32[16,256]{1,0:T(8,128)}, f32[16,128]{1,0:T(8,128)}, f32[256,768]{1,0:T(8,128)}, f32[24,768]{1,0:T(8,128)}, /*inde...) custom-call(bf16[8,272,768]{2,1,0:T(8,128)(2,1)} %get-tuple-element.60.blocks_ref, ...), custom_call_target="tpu_custom_call" | custom-call | tf_op jit(solution)/shard_map/back/pallas_call | solution.py:1348
  308.1 3.2 %finish.1 = (bf16[256,768]{1,0:T(8,128)(2,1)}, f32[256,768]{1,0:T(8,128)}, f32[96,1024]{1,0:T(8,128)}, f32[96,1024]{1,0:T(8,128)}, f32[128,768]{1,0:T(8,128)}, /...) custom-call(bf16[256,768]{1,0:T(8,128)(2,1)} %get-tuple-element.79.o, ...), custom_call_target="tpu_custom_call" | custom-call | tf_op jit(solution)/shard_map/finish/pallas_call | solution.py:1458

commit v4 on v3

--- a/solution.py
+++ b/solution.py
@@ -151,16 +151,21 @@
     return jnp.concatenate([rows[:16], tail, small], axis=1).astype(jnp.bfloat16)
 
 
-def front_kernel(
+def forward_kernel(
     wq_ref, wk_ref, wv_ref, wo_ref, router_ref, constant_ref, vector_ref, gain_one_ref, gain_two_ref,
-    tokens_ref, segments_in, gate_in, up_in,
+    tokens_ref, segments_in, gate_in, up_in, down_in,
     left_ref, right_ref, place_ref, cos_in, sin_in, cos_out, sin_out,
     prev_ref, wres_ref, routes_ref, rank_ref, cot_ref,
-    state_ref, normed_ref, att_ref, lse_ref, q_ref, keys_ref, values_ref, rows_ref, grads_ref,
-    info_ref, proj_ref, blocks_ref, w_ref, small_ref, gate_up_ref,
+    state_ref, normed_ref, att_ref, lse_ref, q_ref, keys_ref, values_ref,
+    info_ref, proj_ref, blocks_ref, w_ref, small_ref, pay_ref,
+    back_rows_ref, back_grads_ref, d_gate_up_ref, d_down_ref,
     part_a, part_b, part_c, own_ref, qt_ref, vt_ref, bias_ref, max_ref, sum_ref, acc_ref,
-    prev_pad, wres_pad, few_wide, few_tall,
-    net_send, net_recv, twin_send, twin_recv, own_sem, seq_send, seq_recv, fwd_send, fwd_recv,
+    prev_pad, wres_pad, few_wide, few_tall, kv_ref, rows_ref, grads_ref,
+    gate_w, up_w, down_w, x_ref, g_ref, gate_ref, up_ref, hidden_ref, d_gate, d_up,
+    mine_ref, twin_out, twin_in,
+    net_send, net_recv, twin_send, twin_recv, own_sem, ring_send, ring_recv, kv_sem,
+    load_sem, send_sem, recv_sem, share_send, share_recv, half_send, half_recv, ret_send, ret_recv,
+    keep_sem,
 ):
     parts = (part_a, part_b, part_c)
     tables = (cos_in, sin_in, cos_out, sin_out)
@@ -182,7 +187,15 @@
     )
     blocks_ref[ctx, :BLK] = tokens_ref[...]
     blocks_ref[ctx, BLK:] = jnp.broadcast_to(marks, (16, WIDTH)).astype(jnp.bfloat16)
-    greet(torus_peers(spot, core) + sequence_peers(spot, core))
+    chip = fsdp // 2
+
+    def at_expert(where, on):
+        return {"ctx": ctx, "fsdp": where * 2 + on}
+
+    greet(
+        torus_peers(spot, core)
+        + [at_expert((chip + by) % EXPERTS, core) for by in range(1, EXPERTS)]
+    )
 
     def net(part, step, by, source, target):
         axis = PART_ORDER[part][step]
@@ -205,70 +218,49 @@
             device_id_type=MESH,
         )
 
-    payloads = ((blocks_ref, 128, BLK + 16), (gate_up_ref, 96, 192))
-
-    def seq(kind, route, by, source, rows):
-        array = payloads[kind][0]
-        to_side = side if route in (1, 3) else 1 - side
-        target = ((along + by) % 4) * 2 + to_side
-        semaphores = (fwd_send, fwd_recv) if route == 3 else (seq_send, seq_recv)
-        slot = {0: 0, 1: by, 2: 3 + by, 3: by - 1}[route]
-        view = array.at[source, rows]
+    payloads = ((blocks_ref, (0, 64, 144, 224, BLK + 16)), (pay_ref, (0, 64, 144, 224, 288)))
+    spans = {"all": (0, 4), "p": (1, 3), "h1": (0, 2), "h2": (2, 4), "q1": (0, 1), "p1": (1, 2), "p2": (2, 3), "q2": (3, 4)}
+    messages = (
+        (1, (0, 0), "all"), (-1, (0, 0), "all"), (0, (0, 0), "all"),
+        (1, (0, 1), "p"), (-1, (0, 1), "p"),
+        (1, (-1, 0), "h1"), (-1, (1, 0), "h2"),
+        (0, (-1, 0), "q1"), (0, (-1, 0), "q2"), (0, (1, 0), "q1"), (0, (1, 0), "q2"),
+        (1, (-1, 1), "p1"), (-1, (1, 1), "p2"),
+        (0, (2, 0), "q1"), (0, (2, 0), "q2"),
+    )
+
+    def ring(kind, number, arriving=False):
+        to, (steps, across_it), rows = messages[number]
+        if arriving:
+            steps = steps - to
+            across_it = across_it if to else 1 - across_it
+        array, cuts = payloads[kind]
+        first, last = (cuts[i] for i in spans[rows])
+        on = side if across_it == 0 else 1 - side
+        view = array.at[((along + steps + 4) % 4) * 2 + on, pl.ds(first, last - first)]
+        target = ((along + to + 4) % 4) * 2 + (side if to else 1 - side)
         return pltpu.make_async_remote_copy(
             src_ref=view,
             dst_ref=view,
-            send_sem=semaphores[0].at[kind, slot],
-            recv_sem=semaphores[1].at[kind, slot],
+            send_sem=ring_send.at[kind, number],
+            recv_sem=ring_recv.at[kind, number],
             device_id={"ctx": target, "fsdp": fsdp},
             device_id_type=MESH,
         )
 
-    def rows_of(kind, route):
-        array, cut, end = payloads[kind]
-        return (pl.ds(0, end), pl.ds(0, end), pl.ds(0, cut), pl.ds(cut, end - cut))[route]
-
-    def needed(kind, by):
-        return along + by < 4 if kind == 0 else along >= 0
-
-    def send_own(kind):
-        seq(kind, 0, 0, ctx, rows_of(kind, 0)).start()
-        for by in (1, 2, 3):
-
-            @pl.when(needed(kind, by))
-            def _(by=by):
-                seq(kind, 1, by, ctx, rows_of(kind, 1)).start()
-                seq(kind, 2, by, ctx, rows_of(kind, 2)).start()
-
-    def beside():
-        return along * 2 + 1 - side
-
-    def send_on(kind):
-        seq(kind, 0, 0, beside(), rows_of(kind, 0)).wait_recv()
-        for by in (1, 2, 3):
-
-            @pl.when(needed(kind, by))
-            def _(by=by):
-                seq(kind, 3, by, beside(), rows_of(kind, 3)).start()
-
-    def behind(by, on_side):
-        return ((along - by + 4) % 4) * 2 + on_side
-
-    def wait_along(kind, by):
-        seq(kind, 1, by, behind(by, side), rows_of(kind, 1)).wait_recv()
-
-    def wait_across(kind, by):
-        seq(kind, 2, by, behind(by, 1 - side), rows_of(kind, 2)).wait_recv()
-        seq(kind, 3, by, behind(by, 1 - side), rows_of(kind, 3)).wait_recv()
-
-    def wait_sent(kind):
-        seq(kind, 0, 0, ctx, rows_of(kind, 0)).wait_send()
-        for by in (1, 2, 3):
-
-            @pl.when(needed(kind, by))
-            def _(by=by):
-                seq(kind, 1, by, ctx, rows_of(kind, 1)).wait_send()
-                seq(kind, 2, by, ctx, rows_of(kind, 2)).wait_send()
-                seq(kind, 3, by, beside(), rows_of(kind, 3)).wait_send()
+    def pass_on(kind, stage):
+        plan = (
+            ((None, (0, 1, 2)),),
+            ((2, (3, 4)),),
+            ((0, (5, 7, 8)), (1, (6, 9, 10))),
+            ((3, (11,)), (4, (12,)), (5, (13,)), (6, (14,))),
+            tuple((number, ()) for number in range(7, 15)),
+        )[stage]
+        for number, then in plan:
+            if number is not None:
+                ring(kind, number, arriving=True).wait_recv()
+            for follow in then:
+                ring(kind, follow).start()
 
     started = []
     kept = []
@@ -288,9 +280,14 @@
         copy = share(part, 0, own, mine)
         copy.start()
         started.append(copy)
+    tail = [(down_in.at[:96], pay_ref.at[ctx, 192:, pl.ds(0, WIDTH)])] + [
+        (down_in.at[96:, pl.ds(256 * m, 256)], pay_ref.at[ctx, pl.ds(192 + 32 * m, 32), pl.ds(WIDTH, 256)])
+        for m in range(3)
+    ]
+    pieces = [(gate_in, pay_ref.at[ctx, :96]), (up_in, pay_ref.at[ctx, 96:192]), *tail]
     own_experts = [
-        pltpu.make_async_copy(gate_in, gate_up_ref.at[ctx, :96], own_sem.at[3]),
-        pltpu.make_async_copy(up_in, gate_up_ref.at[ctx, 96:], own_sem.at[4]),
+        pltpu.make_async_copy(source, target, own_sem.at[3 + number])
+        for number, (source, target) in enumerate(pieces)
     ]
     for copy in own_experts:
         copy.start()
@@ -314,7 +311,7 @@
                     copy.start()
                     started.append(copy)
         if step == 1:
-            send_own(0)
+            pass_on(0, 0)
     for part in range(3):
         order = PART_ORDER[part]
         first = region(parts[part], spot, 1 - core, ())
@@ -342,6 +339,7 @@
         small_ref[rows] = dot(place_ref[...], c[:, 256:]).astype(jnp.bfloat16)
         return carry
 
+    pass_on(0, 1)
     lax.fori_loop(0, 16, unpack, 0)
     across = small_ref[...].astype(jnp.float32).T
     gain_one, gain_two = across[18:19], across[19:20]
@@ -364,16 +362,25 @@
     sum_ref[...] = jnp.zeros_like(sum_ref)
     acc_ref[...] = jnp.zeros_like(acc_ref)
 
+    def keep_block(index, slot):
+        return [
+            pltpu.make_async_copy(kv_ref.at[slot, kind], target.at[index], kv_sem.at[slot, kind])
+            for kind, target in enumerate((keys_ref, values_ref))
+        ]
+
+    def block_at(step):
+        odd = step % 2
+        x = along - (step + odd) // 2 + odd * side
+        return jnp.where(step == 0, ctx, x * 2 + 1 - odd)
+
     def block(step, carry):
-        index = ctx - step
-
-        @pl.when((step > 0) & (step % 2 == 0))
+        index = block_at(step)
+        slot = step % 2
+
+        @pl.when(step >= 2)
         def _():
-            wait_along_at(step // 2)
-
-        @pl.when((step % 2 == 1) & ((step + 1) // 2 - side > 0))
-        def _():
-            wait_across_at((step + 1) // 2 - side)
+            for copy in keep_block(block_at(step - 2), slot):
+                copy.wait()
 
         normed = normed_block(index)
         key = dot(normed, w_ref[1])
@@ -382,13 +389,13 @@
         for pair in range(PAIRS):
             lanes = slice(pair * 128, pair * 128 + 128)
             part = key[:, lanes]
-            keys_ref[index, pair] = (part * cosine + swapped(part) * sine).astype(jnp.bfloat16)
-            values_ref[index, pair] = value[:, lanes].astype(jnp.bfloat16)
+            kv_ref[slot, 0, pair] = (part * cosine + swapped(part) * sine).astype(jnp.bfloat16)
+            kv_ref[slot, 1, pair] = value[:, lanes].astype(jnp.bfloat16)
             vt_ref[lanes, :] = value[:, lanes].T.astype(jnp.bfloat16)
         mask_bias(blocks_ref.at[index], blocks_ref.at[ctx], bias_ref, ctx, index)
         for head in range(HEADS):
             rows = slice(head * HDIM, head * HDIM + HDIM)
-            scores = dot(keys_ref[index, head // 2], qt_ref[head]) + bias_ref[...]
+            scores = dot(kv_ref[slot, 0, head // 2], qt_ref[head]) + bias_ref[...]
             before = max_ref[head : head + 1]
             top = jnp.maximum(before, jnp.max(scores, axis=0, keepdims=True))
             weights = jnp.exp(scores - top)
@@ -399,38 +406,21 @@
             max_ref[head : head + 1] = top
             acc_ref[rows] = acc_ref[rows] * shrink + dot(vt_ref[rows, :], weights.astype(jnp.bfloat16))
 
-        @pl.when(step == 0)
-        def _():
-            send_on(0)
-            send_own(1)
-
-        @pl.when(step == jnp.minimum(ctx, 3))
-        def _():
-            send_on(1)
+        for copy in keep_block(index, slot):
+            copy.start()
+        for when, todo in (
+            (0, ((0, 2),)),
+            (1, ((0, 3), (0, 4), (1, 0))),
+            (4, ((1, 1), (1, 2))),
+            (6, ((1, 3),)),
+        ):
+
+            @pl.when(step == jnp.minimum(ctx, when))
+            def _(todo=todo):
+                for kind, stage in todo:
+                    pass_on(kind, stage)
 
         return carry
-
-    def wait_along_at(by):
-        source = (along - by) * 2 + side
-        seq_at(1, by, source).wait_recv()
-
-    def wait_across_at(by):
-        source = (along - by) * 2 + 1 - side
-        seq_at(2, by, source).wait_recv()
-        seq_at(3, by, source).wait_recv()
-
-    def seq_at(route, by, source):
-        view = blocks_ref.at[source, rows_of(0, route)]
-        semaphores = (fwd_send, fwd_recv) if route == 3 else (seq_send, seq_recv)
-        slot = {1: by, 2: 3 + by, 3: by - 1}[route]
-        return pltpu.make_async_remote_copy(
-            src_ref=view,
-            dst_ref=view,
-            send_sem=semaphores[0].at[0, slot],
-            recv_sem=semaphores[1].at[0, slot],
-            device_id=twin,
-            device_id_type=MESH,
-        )
 
     lax.fori_loop(0, ctx + 1, block, 0)
     for head in range(HEADS):
@@ -481,130 +471,15 @@
         jnp.concatenate([table_0, table_1], axis=1),
         jnp.concatenate([gate_0 * upstream, gate_1 * upstream], axis=0).astype(jnp.bfloat16),
     ).astype(jnp.bfloat16)
-    for by in (1, 2, 3):
-        wait_along(1, by)
-        wait_across(1, by)
-    for kind in (0, 1):
-        wait_sent(kind)
-    for copy in started:
-        copy.wait_send()
-
-
-def pad_routing(prev_ref, wres_ref, prev_pad, wres_pad):
-    prev_pad[...] = jnp.zeros_like(prev_pad)
-    prev_pad[:NALL] = prev_ref[:, 0, :]
-    wres_pad[...] = jnp.zeros_like(wres_pad)
-    wres_pad[:NALL, :NALL] = wres_ref[...]
-
-
-def run_front(weights, few, tokens, segments, gate, up, prev, wres, routes, rank, cot):
-    vmem, anywhere = pl.BlockSpec(memory_space=pltpu.VMEM), pl.BlockSpec(memory_space=pl.ANY)
-    shape = jax.ShapeDtypeStruct
-    low, wide = jnp.bfloat16, jnp.float32
-    dma = pltpu.SemaphoreType.DMA
-    left, right, small = (jnp.asarray(t, low) for t in placing_tables())
-    return pl.pallas_call(
-        front_kernel,
-        out_shape=[
-            shape((BLK, WIDTH), wide),
-            shape((BLK, WIDTH), low),
-            shape((WIDTH, BLK), wide),
-            shape((16, BLK), wide),
-            shape((PAIRS, BLK, 128), low),
-            shape((8, PAIRS, BLK, 128), low),
-            shape((8, PAIRS, BLK, 128), low),
-            shape((EXPERTS * SLOTS, WIDTH), low),
-            shape((EXPERTS * SLOTS, WIDTH), low),
-            shape((BLK, 128), wide),
-            shape((BLK, 128), wide),
-            shape((8, BLK + 16, WIDTH), low),
-            shape((4, WIDTH, WIDTH), low),
-            shape((WIDTH, 128), low),
-            shape((8, 192, 1024), low),
-        ],
-        in_specs=[vmem] * 25,
-        out_specs=[vmem] * 14 + [anywhere],
-        scratch_shapes=[
-            *(pltpu.VMEM((4, 4, 4, 2, 16, lanes), low) for lanes in PART_LANES),
-            pltpu.VMEM((16, 1280), low),
-            pltpu.VMEM((HEADS, 128, BLK), low),
-            pltpu.VMEM((WIDTH, BLK), low),
-            pltpu.VMEM((BLK, BLK), wide),
-            pltpu.VMEM((16, BLK), wide),
-            pltpu.VMEM((16, BLK), wide),
-            pltpu.VMEM((WIDTH, BLK), wide),
-            pltpu.VMEM((128, BLK), wide),
-            pltpu.VMEM((128, 128), wide),
-            pltpu.VMEM((128, 128), wide),
-            pltpu.VMEM((16, 128), wide),
-            dma((3, 3, 3)),
-            dma((3, 3, 3)),
-            dma((3, 10)),
-            dma((3, 10)),
-            dma((5,)),
-            dma((2, 7)),
-            dma((2, 7)),
-            dma((2, 3)),
-            dma((2, 3)),
-        ],
-        name="front",
-        compiler_params=pltpu.CompilerParams(
-            collective_id=1, has_side_effects=True, vmem_limit_bytes=56 * 2**20
-        ),
-    )(
-        *weights, *few, tokens, segments, gate, up, left, right, small, *rope_tables(),
-        prev, wres, routes, rank, cot,
-    )
-
-
-def experts_kernel(
-    rows_ref, grads_ref, gate_up_ref, down_ref,
-    back_rows_ref, back_grads_ref, d_gate_up_ref, d_down_ref,
-    gate_w, up_w, down_w, x_ref, g_ref, gate_ref, up_ref, hidden_ref, d_gate, d_up,
-    mine_ref, twin_out, twin_in, sums_ref,
-    down_send, down_recv, load_sem, send_sem, recv_sem, share_send, share_recv, half_send, half_recv, ret_send, ret_recv,
-    own_sem,
-):
-    ctx, fsdp = lax.axis_index("ctx"), lax.axis_index("fsdp")
-    chip, core = fsdp // 2, fsdp % 2
+    for back in (0, 1):
+
+        @pl.when(ctx - back >= 0)
+        def _(back=back):
+            for copy in keep_block(block_at(ctx - back), (ctx - back) % 2):
+                copy.wait()
+
     other = 1 - core
     half = EXPERTS * SLOTS
-
-    def at(where, on):
-        return {"ctx": ctx, "fsdp": where * 2 + on}
-
-    greet(
-        [at((chip + by) % EXPERTS, core) for by in range(1, EXPERTS)]
-        + [at(chip, other)]
-        + [{"ctx": (ctx + by) % 8, "fsdp": fsdp} for by in range(1, 8)]
-    )
-
-    def down(by, owner):
-        spot = down_w.at[pl.ds(pl.multiple_of(owner * 128, 128), 128)]
-        return pltpu.make_async_remote_copy(
-            src_ref=down_ref,
-            dst_ref=spot,
-            send_sem=down_send.at[by - 1],
-            recv_sem=down_recv.at[by - 1],
-            device_id={"ctx": (ctx + by) % 8, "fsdp": fsdp},
-            device_id_type=MESH,
-        )
-
-    loads = []
-    for index in range(8):
-        for source, target, size in (
-            (gate_up_ref.at[index, :96], gate_w, 96),
-            (gate_up_ref.at[index, 96:], up_w, 96),
-        ):
-            copy = pltpu.make_async_copy(
-                source, target.at[pl.ds(index * size, size)], load_sem.at[len(loads)]
-            )
-            loads.append(copy)
-    loads.append(
-        pltpu.make_async_copy(
-            down_ref, down_w.at[pl.ds(pl.multiple_of(ctx * 128, 128), 128)], load_sem.at[16]
-        )
-    )
 
     def slots(index, on):
         return pl.ds(pl.multiple_of((on * EXPERTS + index) * SLOTS, SLOTS), SLOTS)
@@ -622,7 +497,7 @@
             dst_ref=target.at[slots(chip, core)],
             send_sem=send_sem.at[kind, by - 1],
             recv_sem=recv_sem.at[kind, by - 1],
-            device_id=at(where, core),
+            device_id=at_expert(where, core),
             device_id_type=MESH,
         )
 
@@ -634,7 +509,7 @@
             dst_ref=target.at[spot],
             send_sem=share_send.at[kind, by],
             recv_sem=share_recv.at[kind, by],
-            device_id=at(chip, other),
+            device_id=at_expert(chip, other),
             device_id_type=MESH,
         )
 
@@ -644,7 +519,7 @@
             dst_ref=twin_in.at[kind],
             send_sem=half_send.at[kind],
             recv_sem=half_recv.at[kind],
-            device_id=at(chip, other),
+            device_id=at_expert(chip, other),
             device_id_type=MESH,
         )
 
@@ -653,30 +528,23 @@
     def give_back(kind, by):
         where = (chip + by) % EXPERTS
         return pltpu.make_async_remote_copy(
-            src_ref=sums_ref.at[kind, chunk(where)],
+            src_ref=mine_ref.at[kind, chunk(where)],
             dst_ref=returned[kind].at[chunk(chip)],
             send_sem=ret_send.at[kind, by - 1],
             recv_sem=ret_recv.at[kind, by - 1],
-            device_id=at(where, core),
+            device_id=at_expert(where, core),
             device_id_type=MESH,
         )
 
-    started = []
     for kind in (0, 1):
         for by in range(1, EXPERTS):
             copy = dispatch(kind, by)
             copy.start()
             started.append(copy)
-    for by in range(1, 8):
-        copy = down(by, ctx)
-        copy.start()
-        started.append(copy)
-    for copy in loads:
-        copy.start()
     for kind in (0, 1):
         source, target = buffers[kind]
         copy = pltpu.make_async_copy(
-            source.at[chunk(chip)], target.at[slots(chip, core)], own_sem.at[kind]
+            source.at[chunk(chip)], target.at[slots(chip, core)], keep_sem.at[kind]
         )
         copy.start()
         copy.wait()
@@ -714,9 +582,6 @@
             keep(inner, dot(hidden_ref[rows], down_w[...]))
 
         tiles(on, tile)
-        if on is core:
-            for by in range(1, 8):
-                down(by, (ctx - by + 8) % 8).wait_recv()
         tiles(on, result)
 
     def backward(on, keep):
@@ -734,7 +599,7 @@
 
     def keep_mine(kind):
         def keep(rows, values):
-            mine_ref[kind, rows] = values
+            mine_ref[kind, rows] = values.astype(jnp.bfloat16)
 
         return keep
 
@@ -749,8 +614,8 @@
 
         def step(index, carry):
             rows = pl.ds(pl.multiple_of(index * 128, 128), 128)
-            sums_ref[kind, rows] = (
-                mine_ref[kind, rows] + twin_in[kind, rows].astype(jnp.float32)
+            mine_ref[kind, rows] = (
+                mine_ref[kind, rows].astype(jnp.float32) + twin_in[kind, rows].astype(jnp.float32)
             ).astype(jnp.bfloat16)
             return carry
 
@@ -760,14 +625,39 @@
             copy.start()
             started.append(copy)
         copy = pltpu.make_async_copy(
-            sums_ref.at[kind, chunk(chip)], returned[kind].at[chunk(chip)], own_sem.at[kind]
+            mine_ref.at[kind, chunk(chip)], returned[kind].at[chunk(chip)], keep_sem.at[kind]
         )
         copy.start()
         copy.wait()
 
+    def load(owner):
+        parts = [
+            (pay_ref.at[owner, :96], gate_w.at[pl.ds(pl.multiple_of(owner * 96, 16), 96)]),
+            (pay_ref.at[owner, 96:192], up_w.at[pl.ds(pl.multiple_of(owner * 96, 16), 96)]),
+            (
+                pay_ref.at[owner, 192:, pl.ds(0, WIDTH)],
+                down_w.at[pl.ds(pl.multiple_of(owner * 128, 16), 96)],
+            ),
+        ] + [
+            (
+                pay_ref.at[owner, pl.ds(192 + 32 * m, 32), pl.ds(WIDTH, 256)],
+                down_w.at[pl.ds(pl.multiple_of(owner * 128 + 96, 16), 32), pl.ds(256 * m, 256)],
+            )
+            for m in range(3)
+        ]
+        return [
+            pltpu.make_async_copy(source, target, load_sem.at[owner, number])
+            for number, (source, target) in enumerate(parts)
+        ]
+
+    pass_on(1, 4)
+    for owner in range(8):
+        for copy in load(owner):
+            copy.start()
     arrive(0)
-    for copy in loads:
-        copy.wait()
+    for owner in range(8):
+        for copy in load(owner):
+            copy.wait()
     forward(core, keep_mine(0))
     arrive(1)
     arrive_shared(0)
@@ -805,26 +695,66 @@
     for kind in (0, 1):
         for by in range(1, EXPERTS):
             give_back(kind, by).wait_recv()
+    for kind in (0, 1):
+        for number in range(len(messages)):
+            ring(kind, number).wait_send()
     for copy in started:
         copy.wait_send()
 
 
-def run_experts(rows, grads, gate_up, down):
+def pad_routing(prev_ref, wres_ref, prev_pad, wres_pad):
+    prev_pad[...] = jnp.zeros_like(prev_pad)
+    prev_pad[:NALL] = prev_ref[:, 0, :]
+    wres_pad[...] = jnp.zeros_like(wres_pad)
+    wres_pad[:NALL, :NALL] = wres_ref[...]
+
+
+def run_forward(weights, few, tokens, segments, experts, prev, wres, routes, rank, cot):
     vmem, anywhere = pl.BlockSpec(memory_space=pltpu.VMEM), pl.BlockSpec(memory_space=pl.ANY)
+    shape = jax.ShapeDtypeStruct
     low, wide = jnp.bfloat16, jnp.float32
+    dma = pltpu.SemaphoreType.DMA
     half, whole = EXPERTS * SLOTS, 2 * EXPERTS * SLOTS
-    dma = pltpu.SemaphoreType.DMA
+    left, right, small = (jnp.asarray(t, low) for t in placing_tables())
     return pl.pallas_call(
-        experts_kernel,
+        forward_kernel,
         out_shape=[
-            jax.ShapeDtypeStruct((half, WIDTH), low),
-            jax.ShapeDtypeStruct((half, WIDTH), low),
-            jax.ShapeDtypeStruct((8, 192, 1024), low),
-            jax.ShapeDtypeStruct((8, 128, WIDTH), low),
+            shape((BLK, WIDTH), wide),
+            shape((BLK, WIDTH), low),
+            shape((WIDTH, BLK), wide),
+            shape((16, BLK), wide),
+            shape((PAIRS, BLK, 128), low),
+            shape((8, PAIRS, BLK, 128), low),
+            shape((8, PAIRS, BLK, 128), low),
+            shape((BLK, 128), wide),
+            shape((BLK, 128), wide),
+            shape((8, BLK + 16, WIDTH), low),
+            shape((4, WIDTH, WIDTH), low),
+            shape((WIDTH, 128), low),
+            shape((8, 288, 1024), low),
+            shape((half, WIDTH), low),
+            shape((half, WIDTH), low),
+            shape((8, 192, 1024), low),
+            shape((8, 128, WIDTH), low),
         ],
-        in_specs=[vmem, vmem, anywhere, anywhere],
-        out_specs=[vmem] * 4,
+        in_specs=[vmem] * 26,
+        out_specs=[vmem] * 5 + [anywhere] * 2 + [vmem] * 5 + [anywhere] + [vmem] * 4,
         scratch_shapes=[
+            *(pltpu.VMEM((4, 4, 4, 2, 16, lanes), low) for lanes in PART_LANES),
+            pltpu.VMEM((16, 1280), low),
+            pltpu.VMEM((HEADS, 128, BLK), low),
+            pltpu.VMEM((WIDTH, BLK), low),
+            pltpu.VMEM((BLK, BLK), wide),
+            pltpu.VMEM((16, BLK), wide),
+            pltpu.VMEM((16, BLK), wide),
+            pltpu.VMEM((WIDTH, BLK), wide),
+            pltpu.VMEM((128, BLK), wide),
+            pltpu.VMEM((128, 128), wide),
+            pltpu.VMEM((128, 128), wide),
+            pltpu.VMEM((16, 128), wide),
+            pltpu.VMEM((2, 2, PAIRS, BLK, 128), low),
+            pltpu.VMEM((half, WIDTH), low),
+            pltpu.VMEM((half, WIDTH), low),
             pltpu.VMEM((WIDTH, 1024), low),
             pltpu.VMEM((WIDTH, 1024), low),
             pltpu.VMEM((1024, WIDTH), low),
@@ -835,13 +765,18 @@
             pltpu.VMEM((whole, 1024), low),
             pltpu.VMEM((whole, 1024), low),
             pltpu.VMEM((whole, 1024), low),
-            pltpu.VMEM((2, half, WIDTH), wide),
             pltpu.VMEM((2, half, WIDTH), low),
             pltpu.VMEM((2, half, WIDTH), low),
             pltpu.VMEM((2, half, WIDTH), low),
-            dma((7,)),
-            dma((7,)),
-            dma((17,)),
+            dma((3, 3, 3)),
+            dma((3, 3, 3)),
+            dma((3, 10)),
+            dma((3, 10)),
+            dma((9,)),
+            dma((2, 15)),
+            dma((2, 15)),
+            dma((2, 2)),
+            dma((8, 6)),
             dma((2, 7)),
             dma((2, 7)),
             dma((2, 8)),
@@ -852,11 +787,14 @@
             dma((2, 7)),
             dma((2,)),
         ],
-        name="run_experts",
+        name="forward",
         compiler_params=pltpu.CompilerParams(
-            collective_id=3, has_side_effects=True, vmem_limit_bytes=56 * 2**20
+            collective_id=1, has_side_effects=True, vmem_limit_bytes=63 * 2**20
         ),
-    )(rows, grads, gate_up, down)
+    )(
+        *weights, *few, tokens, segments, *experts, left, right, small, *rope_tables(),
+        prev, wres, routes, rank, cot,
+    )
 
 
 def split(values):
@@ -1479,12 +1417,12 @@
     few = [w_router, w_constant.T, v_constant.T, norm_first[None], norm_second[None]]
     prev = jnp.transpose(prev_logits, (2, 0, 1))
     (
-        state, normed, att, lse, q, keys, values, rows, grads, info, proj, blocks, weights, smalls, gate_up,
-    ) = run_front(
-        [w_query, w_key, w_value, w_output], few, tokens[0], segments, w_gate[0], w_up[0],
+        state, normed, att, lse, q, keys, values, info, proj, blocks, weights, smalls, _,
+        back_rows, back_grads, d_gate_up, d_down,
+    ) = run_forward(
+        [w_query, w_key, w_value, w_output], few, tokens[0], segments, (w_gate[0], w_up[0], w_down[0]),
         prev, w_residual, routes[0].T, rank_order[0], cotangent[0],
     )
-    back_rows, back_grads, d_gate_up, d_down = run_experts(rows, grads, gate_up, w_down[0])
     (
         out, prev_grad, residual, tokens_grad, sums, small, d_gate, d_up, d_down,
     ) = run_back(

time: 312 us -> 277 us (0.89)
  Pallas kernels: 311 us -> 275 us
    pallas_call x2 -> x1, Pallas kernels: 171 us -> 141 us  [run_forward(): pl.pallas_call(forward_kernel, out_shape=[shape((BLK, WIDTH), wide), shap...]
    pallas_call x1, Pallas kernels: 136 us -> 131 us  [run_back(): pl.pallas_call(back_kernel, out_shape=[shape((BLK, WIDTH), low), shape((1...]
where the time goes in v4:
time: 277 us; the launch traced here: 276 us
  Pallas kernels  275 us (99%)
    pallas_call x1, Pallas kernels, run_forward(): pl.pallas_call(forward_kernel, out_shape=[shape((BLK, WIDTH), wide), shap...  141 us
    pallas_call x1, Pallas kernels, run_back(): pl.pallas_call(back_kernel, out_shape=[shape((BLK, WIDTH), low), shape((1...  131 us

profile of v4, /device:TPU:4, one launch (start us, length us, event | category | flops | bytes accessed | tf_op | source)
XLA Modules:
  0.0 275.8 jit_solution(17871126068200164940)
XLA Ops:
  0.7 141.1 %forward.1 = (f32[256,768]{1,0:T(8,128)}, bf16[256,768]{1,0:T(8,128)(2,1)}, f32[768,256]{1,0:T(8,128)}, f32[16,256]{1,0:T(8,128)}, bf16[6,256,128]{2,1,0:T(8,128...) custom-call(bf16[6,768]{1,0:T(8,128)(2,1)} %wq_ref.1, ...), custom_call_target="tpu_custom_call" | custom-call | tf_op jit(solution)/shard_map/forward/pallas_call | solution.py:719
  141.8 130.6 %back.1 = (bf16[256,768]{1,0:T(8,128)(2,1)}, f32[16,256]{1,0:T(8,128)}, f32[16,128]{1,0:T(8,128)}, f32[256,768]{1,0:T(8,128)}, f32[24,768]{1,0:T(8,128)}, /*inde...) custom-call(bf16[8,272,768]{2,1,0:T(8,128)(2,1)} %get-tuple-element.57.blocks_ref, ...), custom_call_target="tpu_custom_call" | custom-call | tf_op jit(solution)/shard_map/back/pallas_call | solution.py:1286
  272.4 3.2 %finish.1 = (bf16[256,768]{1,0:T(8,128)(2,1)}, f32[256,768]{1,0:T(8,128)}, f32[96,1024]{1,0:T(8,128)}, f32[96,1024]{1,0:T(8,128)}, f32[128,768]{1,0:T(8,128)}, /...) custom-call(bf16[256,768]{1,0:T(8,128)(2,1)} %get-tuple-element.73.o, ...), custom_call_target="tpu_custom_call" | custom-call | tf_op jit(solution)/shard_map/finish/pallas_call | solution.py:1396

commit v5 on v4

--- a/solution.py
+++ b/solution.py
@@ -26,6 +26,18 @@
 PART_LANES = (512, 384, 384)
 PART_START = (0, 512, 896)
 PART_ORDER = ((0, 1, 2), (1, 2, 0), (2, 0, 1))
+
+BLOCK_CUTS = (0, 64, 144, 224, 272)
+PAY_CUTS = (0, 64, 144, 224, 288)
+SPANS = {"all": (0, 4), "p": (1, 3), "h1": (0, 2), "h2": (2, 4), "q1": (0, 1), "p1": (1, 2), "p2": (2, 3), "q2": (3, 4)}
+MESSAGES = (
+    (1, (0, 0), "all"), (-1, (0, 0), "all"), (0, (0, 0), "all"),
+    (1, (0, 1), "p"), (-1, (0, 1), "p"),
+    (1, (-1, 0), "h1"), (-1, (1, 0), "h2"),
+    (0, (-1, 0), "q1"), (0, (-1, 0), "q2"), (0, (1, 0), "q1"), (0, (1, 0), "q2"),
+    (1, (-1, 1), "p1"), (-1, (1, 1), "p2"),
+    (0, (2, 0), "q1"), (0, (2, 0), "q2"),
+)
 
 
 def place():
@@ -158,7 +170,7 @@
     prev_ref, wres_ref, routes_ref, rank_ref, cot_ref,
     state_ref, normed_ref, att_ref, lse_ref, q_ref, keys_ref, values_ref,
     info_ref, proj_ref, blocks_ref, w_ref, small_ref, pay_ref,
-    back_rows_ref, back_grads_ref, d_gate_up_ref, d_down_ref,
+    back_rows_ref, back_grads_ref, d_pay_ref,
     part_a, part_b, part_c, own_ref, qt_ref, vt_ref, bias_ref, max_ref, sum_ref, acc_ref,
     prev_pad, wres_pad, few_wide, few_tall, kv_ref, rows_ref, grads_ref,
     gate_w, up_w, down_w, x_ref, g_ref, gate_ref, up_ref, hidden_ref, d_gate, d_up,
@@ -218,24 +230,15 @@
             device_id_type=MESH,
         )
 
-    payloads = ((blocks_ref, (0, 64, 144, 224, BLK + 16)), (pay_ref, (0, 64, 144, 224, 288)))
-    spans = {"all": (0, 4), "p": (1, 3), "h1": (0, 2), "h2": (2, 4), "q1": (0, 1), "p1": (1, 2), "p2": (2, 3), "q2": (3, 4)}
-    messages = (
-        (1, (0, 0), "all"), (-1, (0, 0), "all"), (0, (0, 0), "all"),
-        (1, (0, 1), "p"), (-1, (0, 1), "p"),
-        (1, (-1, 0), "h1"), (-1, (1, 0), "h2"),
-        (0, (-1, 0), "q1"), (0, (-1, 0), "q2"), (0, (1, 0), "q1"), (0, (1, 0), "q2"),
-        (1, (-1, 1), "p1"), (-1, (1, 1), "p2"),
-        (0, (2, 0), "q1"), (0, (2, 0), "q2"),
-    )
+    payloads = ((blocks_ref, BLOCK_CUTS), (pay_ref, PAY_CUTS))
 
     def ring(kind, number, arriving=False):
-        to, (steps, across_it), rows = messages[number]
+        to, (steps, across_it), rows = MESSAGES[number]
         if arriving:
             steps = steps - to
             across_it = across_it if to else 1 - across_it
         array, cuts = payloads[kind]
-        first, last = (cuts[i] for i in spans[rows])
+        first, last = (cuts[i] for i in SPANS[rows])
         on = side if across_it == 0 else 1 - side
         view = array.at[((along + steps + 4) % 4) * 2 + on, pl.ds(first, last - first)]
         target = ((along + to + 4) % 4) * 2 + (side if to else 1 - side)
@@ -341,6 +344,7 @@
 
     pass_on(0, 1)
     lax.fori_loop(0, 16, unpack, 0)
+    pass_on(0, 2)
     across = small_ref[...].astype(jnp.float32).T
     gain_one, gain_two = across[18:19], across[19:20]
 
@@ -409,8 +413,8 @@
         for copy in keep_block(index, slot):
             copy.start()
         for when, todo in (
-            (0, ((0, 2),)),
-            (1, ((0, 3), (0, 4), (1, 0))),
+            (0, ((0, 3),)),
+            (1, ((0, 4), (1, 0))),
             (4, ((1, 1), (1, 2))),
             (6, ((1, 3),)),
         ):
@@ -536,11 +540,14 @@
             device_id_type=MESH,
         )
 
-    for kind in (0, 1):
-        for by in range(1, EXPERTS):
-            copy = dispatch(kind, by)
-            copy.start()
-            started.append(copy)
+    for by in range(1, EXPERTS):
+        dispatch(0, by).start()
+    for by in range(1, EXPERTS):
+        dispatch(0, by).wait_send()
+    for by in range(1, EXPERTS):
+        copy = dispatch(1, by)
+        copy.start()
+        started.append(copy)
     for kind in (0, 1):
         source, target = buffers[kind]
         copy = pltpu.make_async_copy(
@@ -676,8 +683,13 @@
     def down_tile(index, carry):
         lanes = pl.ds(pl.multiple_of(index * 256, 256), 256)
         part = dot_tn(hidden_ref[:, lanes], g_ref[...]).astype(jnp.bfloat16)
-        d_down_ref[2 * index] = part[:128]
-        d_down_ref[2 * index + 1] = part[128:]
+        for piece in (0, 1):
+            rows = part[piece * 128 : piece * 128 + 128]
+            d_pay_ref[2 * index + piece, 192:, :WIDTH] = rows[:96]
+            for m in range(3):
+                d_pay_ref[2 * index + piece, 192 + 32 * m : 224 + 32 * m, WIDTH:] = rows[
+                    96:, 256 * m : 256 * m + 256
+                ]
         return carry
 
     lax.fori_loop(0, 4, down_tile, 0)
@@ -688,7 +700,7 @@
         for start, grad in ((0, d_gate), (96, d_up)):
             part = dot_tn(x_ref[...], grad[:, lanes]).astype(jnp.bfloat16)
             for piece in range(8):
-                d_gate_up_ref[piece, start : start + 96, lanes] = part[piece * 96 : piece * 96 + 96]
+                d_pay_ref[piece, start : start + 96, lanes] = part[piece * 96 : piece * 96 + 96]
         return carry
 
     lax.fori_loop(0, 4, gate_tile, 0)
@@ -696,7 +708,7 @@
         for by in range(1, EXPERTS):
             give_back(kind, by).wait_recv()
     for kind in (0, 1):
-        for number in range(len(messages)):
+        for number in range(len(MESSAGES)):
             ring(kind, number).wait_send()
     for copy in started:
         copy.wait_send()
@@ -734,11 +746,10 @@
             shape((8, 288, 1024), low),
             shape((half, WIDTH), low),
             shape((half, WIDTH), low),
-            shape((8, 192, 1024), low),
-            shape((8, 128, WIDTH), low),
+            shape((8, 288, 1024), low),
         ],
         in_specs=[vmem] * 26,
-        out_specs=[vmem] * 5 + [anywhere] * 2 + [vmem] * 5 + [anywhere] + [vmem] * 4,
+        out_specs=[vmem] * 5 + [anywhere] * 2 + [vmem] * 5 + [anywhere] + [vmem] * 3,
         scratch_shapes=[
             *(pltpu.VMEM((4, 4, 4, 2, 16, lanes), low) for lanes in PART_LANES),
             pltpu.VMEM((16, 1280), low),
@@ -807,21 +818,21 @@
     blocks_ref, w_ref, small_ref, cos_in, sin_in, cos_out, sin_out, left_ref, right_ref, place_ref,
     prev_ref, wres_ref, routes_ref, cot_ref,
     state_ref, normed_ref, att_ref, lse_ref, q_ref, keys_ref, values_ref, info_ref, proj_ref,
-    back_rows_ref, back_grads_ref, d_gate_up, d_down,
+    back_rows_ref, back_grads_ref, d_pay_ref,
     out_ref, prev_grad_ref, total_ref, tokens_grad_ref, sums_ref, few_ref,
     gate_out, up_out, down_out,
     *scratch,
 ):
     (
         qt_ref, ot_ref, o_ref, qm_ref, bias_ref, inner_ref, dqt_ref, gain_ref, dk_ref, dv_ref,
-        prev_pad, wres_pad, dw_ref, few_sum, kv_ref, tok_ref, mine_ref, kv_sem, own_ref, state_grad_ref, others_ref, grads_ref, block_in,
-        gate_up_in, down_in, small_in, small_sum,
+        prev_pad, wres_pad, dw_ref, dw_low, few_sum, kv_ref, tok_ref, mine_ref, kv_sem, own_ref, state_grad_ref, others_ref, grads_ref, block_in,
+        pay_ref, pay_in, small_in, small_sum,
         block_send, block_recv, exp_send, exp_recv, load_sem,
         net_send, net_recv, twin_send, twin_recv, small_send, small_recv,
         *more,
     ) = scratch
-    twin_in, held, in_one, in_two, in_three, sum_one, sum_two = (
-        more[0], more[1], more[2:5], more[5:8], more[8:11], more[11:14], more[14:17]
+    twin_in, in_one, in_two, in_three, sum_one, sum_two = (
+        more[0], more[1:4], more[4:7], more[7:10], more[10:13], more[13:16]
     )
     tables = (cos_in, sin_in, cos_out, sin_out)
     ctx, fsdp = lax.axis_index("ctx"), lax.axis_index("fsdp")
@@ -831,31 +842,63 @@
     started = []
     greet(torus_peers(spot, core) + sequence_peers(spot, core))
 
-    def expert(kind, by):
-        source, target = ((d_gate_up, gate_up_in), (d_down, down_in))[kind]
-        where = (ctx + by) % 8
+    along, side = ctx // 2, ctx % 2
+
+    def rows_of(number):
+        first, last = (PAY_CUTS[i] for i in SPANS[MESSAGES[number][2]])
+        return first, last - first
+
+    def owner(steps, across_it):
+        return ((along + steps + 4) % 4) * 2 + (side if across_it == 0 else 1 - side)
+
+    def expert(number):
+        to, (steps, across_it), _ = MESSAGES[number]
+        first, count = rows_of(number)
+        landing = sum(rows_of(before)[1] for before in range(number))
         return pltpu.make_async_remote_copy(
-            src_ref=source.at[where],
-            dst_ref=target.at[by],
-            send_sem=exp_send.at[kind, by - 1],
-            recv_sem=exp_recv.at[kind, by - 1],
-            device_id={"ctx": where, "fsdp": fsdp},
+            src_ref=pay_ref.at[
+                owner(steps - to, across_it if to else 1 - across_it), pl.ds(first, count)
+            ],
+            dst_ref=pay_in.at[pl.ds(landing, count)],
+            send_sem=exp_send.at[number],
+            recv_sem=exp_recv.at[number],
+            device_id={"ctx": owner(-to, 0 if to else 1), "fsdp": fsdp},
             device_id_type=MESH,
         )
 
-    for kind in (0, 1):
-        for by in range(1, 8):
-            copy = expert(kind, by)
-            copy.start()
-            started.append(copy)
-    kept = [
-        pltpu.make_async_copy(d_gate_up.at[ctx], gate_up_in.at[0], load_sem.at[0]),
-        pltpu.make_async_copy(d_down.at[ctx], down_in.at[0], load_sem.at[1]),
+    def send_experts(numbers):
+        for number in numbers:
+            expert(number).start()
+
+    def add_experts(numbers):
+        for number in numbers:
+            expert(number).wait_recv()
+            _, (steps, across_it), _ = MESSAGES[number]
+            first, count = rows_of(number)
+            landing = sum(rows_of(before)[1] for before in range(number))
+            at = owner(steps, across_it)
+
+            def add_rows(index, carry, at=at, first=first, landing=landing):
+                here = pl.ds(pl.multiple_of(first + index * 16, 16), 16)
+                there = pl.ds(pl.multiple_of(landing + index * 16, 16), 16)
+                pay_ref[at, here] = (
+                    pay_ref[at, here].astype(jnp.float32) + pay_in[there].astype(jnp.float32)
+                ).astype(jnp.bfloat16)
+                return carry
+
+            lax.fori_loop(0, count // 16, add_rows, 0)
+
+    loads = [
+        pltpu.make_async_copy(d_pay_ref.at[index], pay_ref.at[index], load_sem.at[1 + index])
+        for index in range(8)
     ]
-    own_block = pltpu.make_async_copy(blocks_ref.at[ctx], mine_ref, load_sem.at[2])
+    for copy in loads:
+        copy.start()
+    for copy in loads:
+        copy.wait()
+    send_experts((13, 14, 11, 12, 7, 8, 9, 10))
+    own_block = pltpu.make_async_copy(blocks_ref.at[ctx], mine_ref, load_sem.at[0])
     own_block.start()
-    for copy in kept:
-        copy.start()
 
     def load_kv(index, slot):
         return [
@@ -962,7 +1005,7 @@
     gain_two_row = jnp.sum(normed_grad * state * scale_two, axis=0, keepdims=True)
     state_low = state_grad.astype(jnp.bfloat16)
     attended = att_ref[...]
-    dw_ref[3] = dot(attended.astype(jnp.bfloat16), state_low)
+    dw_low[1] = dot(attended.astype(jnp.bfloat16), state_low).astype(jnp.bfloat16)
     att_grad = dot_nt(state_low, w_ref[3])
     blank = jnp.zeros((HDIM, BLK), jnp.bfloat16)
     low_half = lax.broadcasted_iota(jnp.int32, (BLK, 128), 1) < HDIM
@@ -986,8 +1029,7 @@
         qm_ref[pair, :BLK] = jnp.where(low_half, q_ref[pair], none)
         qm_ref[pair, BLK:] = jnp.where(low_half, none, q_ref[pair])
     dqt_ref[...] = jnp.zeros_like(dqt_ref)
-    dw_ref[1] = jnp.zeros((WIDTH, WIDTH), jnp.float32)
-    dw_ref[2] = jnp.zeros((WIDTH, WIDTH), jnp.float32)
+    dw_ref[...] = jnp.zeros_like(dw_ref)
     gain_ref[...] = jnp.zeros_like(gain_ref)
 
     own_block.wait()
@@ -1028,8 +1070,8 @@
             dk = dot(jnp.concatenate(score_grads, axis=1), qm_ref[pair])
             dk_ref[:, lanes] = (dk * cosine - swapped(dk) * sine).astype(jnp.bfloat16)
         scaled, normed_across = normed_block(tok_ref.at[slot])
-        dw_ref[1] += dot(normed_across, dk_ref[...])
-        dw_ref[2] += dot(normed_across, dv_ref[...])
+        dw_ref[0] += dot(normed_across, dk_ref[...])
+        dw_ref[1] += dot(normed_across, dv_ref[...])
         first = dot_nt(dk_ref[...], w_ref[1]) + dot_nt(dv_ref[...], w_ref[2])
         gain_ref[...] += jnp.sum(first * scaled, axis=0, keepdims=True)
 
@@ -1042,8 +1084,21 @@
         def _():
             own_ref[...] = first
 
+        for when, came, then in (
+            (0, (13, 14), (5, 6)),
+            (1, (3, 4), (2,)),
+            (3, (7, 8, 9, 10, 5, 6), (0, 1)),
+        ):
+
+            @pl.when(index == jnp.minimum(ctx, when))
+            def _(came=came, then=then):
+                add_experts(came)
+                send_experts(then)
+
         return carry
 
+    add_experts((11, 12))
+    send_experts((3, 4))
     lax.fori_loop(0, ctx + 1, block, 0)
     cosine, sine = turning(ctx, tables)
     for pair in range(PAIRS):
@@ -1051,7 +1106,7 @@
         dq = dqt_ref[lanes, :].T * (HDIM**-0.5)
         dk_ref[:, lanes] = (dq * cosine - swapped(dq) * sine).astype(jnp.bfloat16)
     scaled, normed_across = normed_block(mine_ref)
-    dw_ref[0] = dot(normed_across, dk_ref[...])
+    dw_low[0] = dot(normed_across, dk_ref[...]).astype(jnp.bfloat16)
     first = dot_nt(dk_ref[...], w_ref[0])
     own_ref[...] += first
     gain_one_row = gain_ref[...] + jnp.sum(first * scaled, axis=0, keepdims=True)
@@ -1075,9 +1130,10 @@
         rows = pl.ds(pl.multiple_of(group * 48, 16), 48)
 
         def lane_half(start):
-            return jnp.concatenate(
-                [dw_ref[w, rows, start : start + 384] for w in range(4)], axis=0
-            ).astype(jnp.bfloat16)
+            lanes = slice(start, start + 384)
+            query, output = dw_low[0, rows, lanes], dw_low[1, rows, lanes]
+            key, value = (dw_ref[w, rows, lanes].astype(jnp.bfloat16) for w in (0, 1))
+            return jnp.concatenate([query, key, value, output], axis=0)
 
         from_left = dot(left_ref[...], lane_half(0))
         from_right = dot(right_ref[...], lane_half(384))
@@ -1125,7 +1181,7 @@
 
         def add_pair(index, carry, x=x):
             z, y = index // 4, index % 4
-            held[x, z, y] = (
+            grads_ref[x, z, y, core] = (
                 grads_ref[x, z, y, core].astype(jnp.float32) + twin_in[x, z, y].astype(jnp.float32)
             ).astype(jnp.bfloat16)
             return carry
@@ -1141,7 +1197,7 @@
             at = shifted(spot, axis, by)[axis]
             index = tuple(at if a == axis else slice(None) for a in range(3))
             copy = net(
-                part, 0, by, held.at[(*index, slice(None), lanes_of(part))], in_one[part].at[by - 1]
+                part, 0, by, grads_ref.at[(*index, core, slice(None), lanes_of(part))], in_one[part].at[by - 1]
             )
             copy.start()
             started.append(copy)
@@ -1177,7 +1233,7 @@
 
         def add_four(index, carry, part=part, third=third, rest=rest, lanes=lanes):
             at = {rest[0]: index // 4, rest[1]: index % 4, third: spot[third]}
-            total = held[at[0], at[1], at[2], :, lanes].astype(jnp.float32)
+            total = grads_ref[at[0], at[1], at[2], core, :, lanes].astype(jnp.float32)
             for by in range(3):
                 total = total + in_one[part][by, index // 4, index % 4].astype(jnp.float32)
             sum_one[part][index // 4, index % 4] = total.astype(jnp.bfloat16)
@@ -1192,32 +1248,31 @@
             started.append(copy)
     small_step(0)
 
-    for copy in kept:
-        copy.wait()
-    for kind in (0, 1):
-        for by in range(1, 8):
-            expert(kind, by).wait_recv()
-
-    def sum_eight(source, rows):
-        total = source[0, rows].astype(jnp.float32)
-        for by in range(1, 8):
-            total = total + source[by, rows].astype(jnp.float32)
+    for number in (0, 1, 2):
+        expert(number).wait_recv()
+    count = PAY_CUTS[-1]
+
+    def total_rows(start):
+        rows = pl.ds(pl.multiple_of(start, 16), 16)
+        total = pay_ref[ctx, rows].astype(jnp.float32)
+        for number in range(3):
+            there = pl.ds(pl.multiple_of(number * count + start, 16), 16)
+            total = total + pay_in[there].astype(jnp.float32)
         return total
 
-    def expert_rows(index, carry):
+    def gate_rows(index, carry):
         rows = pl.ds(pl.multiple_of(index * 16, 16), 16)
-        gate_out[rows] = sum_eight(gate_up_in, rows)
-        up_out[rows] = sum_eight(gate_up_in, pl.ds(pl.multiple_of(96 + index * 16, 16), 16))
+        gate_out[rows] = total_rows(index * 16)
+        up_out[rows] = total_rows(96 + index * 16)
         return carry
 
-    lax.fori_loop(0, 6, expert_rows, 0)
-
-    def down_rows(index, carry):
-        rows = pl.ds(pl.multiple_of(index * 16, 16), 16)
-        down_out[rows] = sum_eight(down_in, rows)
-        return carry
-
-    lax.fori_loop(0, 8, down_rows, 0)
+    lax.fori_loop(0, 6, gate_rows, 0)
+    for index in range(6):
+        total = total_rows(192 + 16 * index)
+        down_out[16 * index : 16 * index + 16] = total[:, :WIDTH]
+        start = 96 + 16 * (index % 2)
+        lanes = slice(256 * (index // 2), 256 * (index // 2) + 256)
+        down_out[start : start + 16, lanes] = total[:, WIDTH:]
 
     for part in range(3):
         first, second, third = PART_ORDER[part]
@@ -1272,11 +1327,13 @@
     sums_ref[16:] = jnp.concatenate([final[:8, 768:1152], final[8:, 768:1152]], axis=1)
     few_ref[...] = final[:8, 1152:]
     small_step(2)
+    for number in range(len(MESSAGES)):
+        expert(number).wait_send()
     for copy in started:
         copy.wait_send()
 
 
-def run_back(blocks, weights, smalls, prev, wres, routes, cot, kept, back_rows, back_grads, d_gate_up, d_down):
+def run_back(blocks, weights, smalls, prev, wres, routes, cot, kept, back_rows, back_grads, d_pay):
     vmem, anywhere = pl.BlockSpec(memory_space=pltpu.VMEM), pl.BlockSpec(memory_space=pl.ANY)
     shape = jax.ShapeDtypeStruct
     low, wide = jnp.bfloat16, jnp.float32
@@ -1296,7 +1353,7 @@
             shape((96, 1024), wide),
             shape((128, WIDTH), wide),
         ],
-        in_specs=[anywhere] + [vmem] * 18 + [anywhere] * 2 + [vmem] * 4 + [anywhere] * 2,
+        in_specs=[anywhere] + [vmem] * 18 + [anywhere] * 2 + [vmem] * 4 + [anywhere],
         out_specs=[vmem] * 9,
         scratch_shapes=[
             pltpu.VMEM((HEADS, 128, BLK), low),
@@ -1311,7 +1368,8 @@
             pltpu.VMEM((BLK, WIDTH), low),
             pltpu.VMEM((128, BLK), wide),
             pltpu.VMEM((128, 128), wide),
-            pltpu.VMEM((4, WIDTH, WIDTH), wide),
+            pltpu.VMEM((2, WIDTH, WIDTH), wide),
+            pltpu.VMEM((2, WIDTH, WIDTH), low),
             pltpu.VMEM((WIDTH, 128), wide),
             pltpu.VMEM((2, 2, PAIRS, BLK, 128), low),
             pltpu.VMEM((2, BLK + 16, WIDTH), low),
@@ -1319,25 +1377,24 @@
             dma((2, 3)),
             pltpu.VMEM((BLK, WIDTH), wide),
             pltpu.VMEM((BLK, WIDTH), wide),
-            pltpu.VMEM((8, BLK, WIDTH), low),
+            pltpu.VMEM((7, BLK, WIDTH), low),
             pltpu.VMEM((4, 4, 4, 2, 16, 1280), low),
             pltpu.VMEM((7, BLK, WIDTH), low),
-            pltpu.VMEM((8, 192, 1024), low),
-            pltpu.VMEM((8, 128, WIDTH), low),
+            pltpu.VMEM((8, 288, 1024), low),
+            pltpu.VMEM((2016, 1024), low),
             pltpu.VMEM((4, 4, 16, 128), wide),
             pltpu.VMEM((4, 16, 128), wide),
             dma((7,)),
             dma((7,)),
-            dma((2, 7)),
-            dma((2, 7)),
-            dma((3,)),
+            dma((15,)),
+            dma((15,)),
+            dma((9,)),
             dma((3, 3, 3)),
             dma((3, 3, 3)),
             dma((4,)),
             dma((4,)),
             dma((4, 3)),
             dma((4, 3)),
-            pltpu.VMEM((4, 4, 4, 16, 1280), low),
             pltpu.VMEM((4, 4, 4, 16, 1280), low),
             *by_part(3, 4, 4),
             *by_part(3, 4),
@@ -1351,7 +1408,7 @@
         ),
     )(
         blocks, weights, smalls, *rope_tables(), left, right, small, prev, wres, routes, cot,
-        *kept, back_rows, back_grads, d_gate_up, d_down,
+        *kept, back_rows, back_grads, d_pay,
     )
 
 
@@ -1418,7 +1475,7 @@
     prev = jnp.transpose(prev_logits, (2, 0, 1))
     (
         state, normed, att, lse, q, keys, values, info, proj, blocks, weights, smalls, _,
-        back_rows, back_grads, d_gate_up, d_down,
+        back_rows, back_grads, d_pay,
     ) = run_forward(
         [w_query, w_key, w_value, w_output], few, tokens[0], segments, (w_gate[0], w_up[0], w_down[0]),
         prev, w_residual, routes[0].T, rank_order[0], cotangent[0],
@@ -1427,8 +1484,7 @@
         out, prev_grad, residual, tokens_grad, sums, small, d_gate, d_up, d_down,
     ) = run_back(
         blocks, weights, smalls, prev, w_residual, routes[0].T, cotangent[0],
-        (state, normed, att, lse, q, keys, values, info, proj), back_rows, back_grads,
-        d_gate_up, d_down,
+        (state, normed, att, lse, q, keys, values, info, proj), back_rows, back_grads, d_pay,
     )
     (
         out, tokens_grad, d_gate, d_up, d_down, prev_grad, residual, sum_q, sum_k, sum_v, sum_o,

time: 277 us -> 244 us (0.88)
  Pallas kernels: 275 us -> 240 us
    pallas_call x1, Pallas kernels: 131 us -> 102 us  [run_back(): pl.pallas_call(back_kernel, out_shape=[shape((BLK, WIDTH), low), shape((1...]
    pallas_call x1, Pallas kernels: 141 us -> 135 us  [run_forward(): pl.pallas_call(forward_kernel, out_shape=[shape((BLK, WIDTH), wide), shap...]
where the time goes in v5:
time: 244 us; the launch traced here: 241 us
  Pallas kernels  240 us (98%)
    pallas_call x1, Pallas kernels, run_forward(): pl.pallas_call(forward_kernel, out_shape=[shape((BLK, WIDTH), wide), shap...  135 us
    pallas_call x1, Pallas kernels, run_back(): pl.pallas_call(back_kernel, out_shape=[shape((BLK, WIDTH), low), shape((1...  102 us

profile of v5, /device:TPU:4, one launch (start us, length us, event | category | flops | bytes accessed | tf_op | source)
XLA Modules:
  0.0 241.0 jit_solution(13430844187808977228)
XLA Ops:
  0.7 134.9 %forward.1 = (f32[256,768]{1,0:T(8,128)}, bf16[256,768]{1,0:T(8,128)(2,1)}, f32[768,256]{1,0:T(8,128)}, f32[16,256]{1,0:T(8,128)}, bf16[6,256,128]{2,1,0:T(8,128...) custom-call(bf16[6,768]{1,0:T(8,128)(2,1)} %wq_ref.1, ...), custom_call_target="tpu_custom_call" | custom-call | tf_op jit(solution)/shard_map/forward/pallas_call | solution.py:731
  135.6 102.1 %back.1 = (bf16[256,768]{1,0:T(8,128)(2,1)}, f32[16,256]{1,0:T(8,128)}, f32[16,128]{1,0:T(8,128)}, f32[256,768]{1,0:T(8,128)}, f32[24,768]{1,0:T(8,128)}, /*inde...) custom-call(bf16[8,272,768]{2,1,0:T(8,128)(2,1)} %get-tuple-element.56.blocks_ref, ...), custom_call_target="tpu_custom_call" | custom-call | tf_op jit(solution)/shard_map/back/pallas_call | solution.py:1343
  237.6 3.2 %finish.1 = (bf16[256,768]{1,0:T(8,128)(2,1)}, f32[256,768]{1,0:T(8,128)}, f32[96,1024]{1,0:T(8,128)}, f32[96,1024]{1,0:T(8,128)}, f32[128,768]{1,0:T(8,128)}, /...) custom-call(bf16[256,768]{1,0:T(8,128)(2,1)} %get-tuple-element.71.o, ...), custom_call_target="tpu_custom_call" | custom-call | tf_op jit(solution)/shard_map/finish/pallas_call | solution.py:1453

commit v6 on v5

--- a/solution.py
+++ b/solution.py
@@ -29,6 +29,7 @@
 
 BLOCK_CUTS = (0, 64, 144, 224, 272)
 PAY_CUTS = (0, 64, 144, 224, 288)
+GRAD_CUTS = (0, 80, 144, 208, 288)
 SPANS = {"all": (0, 4), "p": (1, 3), "h1": (0, 2), "h2": (2, 4), "q1": (0, 1), "p1": (1, 2), "p2": (2, 3), "q2": (3, 4)}
 MESSAGES = (
     (1, (0, 0), "all"), (-1, (0, 0), "all"), (0, (0, 0), "all"),
@@ -397,9 +398,10 @@
             kv_ref[slot, 1, pair] = value[:, lanes].astype(jnp.bfloat16)
             vt_ref[lanes, :] = value[:, lanes].T.astype(jnp.bfloat16)
         mask_bias(blocks_ref.at[index], blocks_ref.at[ctx], bias_ref, ctx, index)
-        for head in range(HEADS):
-            rows = slice(head * HDIM, head * HDIM + HDIM)
-            scores = dot(kv_ref[slot, 0, head // 2], qt_ref[head]) + bias_ref[...]
+        def score(head):
+            return dot(kv_ref[slot, 0, head // 2], qt_ref[head]) + bias_ref[...]
+
+        def soften(head, scores):
             before = max_ref[head : head + 1]
             top = jnp.maximum(before, jnp.max(scores, axis=0, keepdims=True))
             weights = jnp.exp(scores - top)
@@ -408,15 +410,32 @@
                 weights, axis=0, keepdims=True
             )
             max_ref[head : head + 1] = top
-            acc_ref[rows] = acc_ref[rows] * shrink + dot(vt_ref[rows, :], weights.astype(jnp.bfloat16))
+            return shrink, weights.astype(jnp.bfloat16)
+
+        def gather(head, shrink, weights):
+            rows = slice(head * HDIM, head * HDIM + HDIM)
+            acc_ref[rows] = acc_ref[rows] * shrink + dot(vt_ref[rows, :], weights)
+
+        ahead = [score(0), score(1)]
+        done = None
+        for head in range(0, HEADS, 2):
+            now = ahead
+            if head + 2 < HEADS:
+                ahead = [score(head + 2), score(head + 3)]
+            if done is not None:
+                gather(head - 2, *done[0])
+                gather(head - 1, *done[1])
+            done = [soften(head, now[0]), soften(head + 1, now[1])]
+        gather(HEADS - 2, *done[0])
+        gather(HEADS - 1, *done[1])
 
         for copy in keep_block(index, slot):
             copy.start()
         for when, todo in (
-            (0, ((0, 3),)),
-            (1, ((0, 4), (1, 0))),
-            (4, ((1, 1), (1, 2))),
-            (6, ((1, 3),)),
+            (0, ((0, 3), (1, 0))),
+            (1, ((0, 4),)),
+            (5, ((1, 1), (1, 2))),
+            (7, ((1, 3),)),
         ):
 
             @pl.when(step == jnp.minimum(ctx, when))
@@ -826,6 +845,7 @@
     (
         qt_ref, ot_ref, o_ref, qm_ref, bias_ref, inner_ref, dqt_ref, gain_ref, dk_ref, dv_ref,
         prev_pad, wres_pad, dw_ref, dw_low, few_sum, kv_ref, tok_ref, mine_ref, kv_sem, own_ref, state_grad_ref, others_ref, grads_ref, block_in,
+        far_in, far_land, far_sum, far_out, far_back, mark_ref, far_send, far_recv,
         pay_ref, pay_in, small_in, small_sum,
         block_send, block_recv, exp_send, exp_recv, load_sem,
         net_send, net_recv, twin_send, twin_recv, small_send, small_recv,
@@ -845,7 +865,7 @@
     along, side = ctx // 2, ctx % 2
 
     def rows_of(number):
-        first, last = (PAY_CUTS[i] for i in SPANS[MESSAGES[number][2]])
+        first, last = (GRAD_CUTS[i] for i in SPANS[MESSAGES[number][2]])
         return first, last - first
 
     def owner(steps, across_it):
@@ -908,6 +928,42 @@
 
     for copy in load_kv(0, 0):
         copy.start()
+
+    mine_half, twin_half = (
+        pl.ds(pl.multiple_of(on * 128, 128), 128) for on in (core, 1 - core)
+    )
+    end_mark = pltpu.make_async_copy(blocks_ref.at[7, pl.ds(BLK, 16)], mark_ref, load_sem.at[9])
+    end_mark.start()
+
+    def far_share(index):
+        return pltpu.make_async_remote_copy(
+            src_ref=others_ref.at[index, twin_half],
+            dst_ref=far_in.at[index],
+            send_sem=far_send.at[index],
+            recv_sem=far_recv.at[index],
+            device_id=twin,
+            device_id_type=MESH,
+        )
+
+    def far_copy(by, target):
+        return pltpu.make_async_remote_copy(
+            src_ref=others_ref.at[target, mine_half],
+            dst_ref=far_land.at[by - 3],
+            send_sem=block_send.at[by - 1],
+            recv_sem=block_recv.at[by - 1],
+            device_id={"ctx": target, "fsdp": fsdp},
+            device_id_type=MESH,
+        )
+
+    def far_halves():
+        return pltpu.make_async_remote_copy(
+            src_ref=far_out,
+            dst_ref=far_back,
+            send_sem=far_send.at[5],
+            recv_sem=far_recv.at[5],
+            device_id=twin,
+            device_id_type=MESH,
+        )
 
     def block_copy(by, target):
         return pltpu.make_async_remote_copy(
@@ -1051,15 +1107,24 @@
 
         mask_bias(tok_ref.at[slot], mine_ref, bias_ref, ctx, index)
         cosine, sine = turning(index, tables)
+        def products(pair):
+            key, value = kv_ref[slot, 0, pair], kv_ref[slot, 1, pair]
+            return [
+                (dot(key, qt_ref[2 * pair + half]) + bias_ref[...], dot(value, ot_ref[2 * pair + half]))
+                for half in (0, 1)
+            ]
+
+        ahead = products(0)
         for pair in range(PAIRS):
-            key, value = kv_ref[slot, 0, pair], kv_ref[slot, 1, pair]
-            key_across = key.astype(jnp.float32).T.astype(jnp.bfloat16)
+            now = ahead
+            if pair + 1 < PAIRS:
+                ahead = products(pair + 1)
+            key_across = kv_ref[slot, 0, pair].T
             weights, score_grads = [], []
             for half in (0, 1):
                 head = 2 * pair + half
-                scores = dot(key, qt_ref[head]) + bias_ref[...]
+                scores, weight_grad = now[half]
                 weight = jnp.exp(scores - lse_ref[head : head + 1])
-                weight_grad = dot(value, ot_ref[head])
                 score_grad = (weight * (weight_grad - inner_ref[head : head + 1])).astype(jnp.bfloat16)
                 weights.append(weight.astype(jnp.bfloat16))
                 score_grads.append(score_grad)
@@ -1078,7 +1143,23 @@
         @pl.when(index < ctx)
         def _():
             others_ref[index] = first.astype(jnp.bfloat16)
+
+        @pl.when((index < ctx) & (index >= ctx - 2))
+        def _():
             block_copy(ctx - index, index).start()
+
+        @pl.when(index < ctx - 2)
+        def _():
+            far_share(index).start()
+
+        @pl.when((index >= 1) & (index - 1 < ctx - 2))
+        def _():
+            far_share(index - 1).wait_recv()
+            others_ref[index - 1, mine_half] = (
+                others_ref[index - 1, mine_half].astype(jnp.float32)
+                + far_in[index - 1].astype(jnp.float32)
+            ).astype(jnp.bfloat16)
+            far_copy(ctx - (index - 1), index - 1).start()
 
         @pl.when(index == ctx)
         def _():
@@ -1087,7 +1168,7 @@
         for when, came, then in (
             (0, (13, 14), (5, 6)),
             (1, (3, 4), (2,)),
-            (3, (7, 8, 9, 10, 5, 6), (0, 1)),
+            (2, (7, 8, 9, 10, 5, 6), (0, 1)),
         ):
 
             @pl.when(index == jnp.minimum(ctx, when))
@@ -1294,7 +1375,7 @@
             started.append(copy)
     small_step(1)
 
-    for by in range(1, 8):
+    for by in (1, 2):
 
         @pl.when(ctx + by < 8)
         def _(by=by):
@@ -1304,6 +1385,28 @@
         @pl.when(ctx - by >= 0)
         def _(by=by):
             block_copy(by, ctx - by).wait_send()
+
+    far_sum[...] = jnp.zeros_like(far_sum)
+    for by in range(3, 8):
+
+        @pl.when(ctx + by < 8)
+        def _(by=by):
+            far_copy(by, ctx).wait_recv()
+            far_sum[...] += far_land[by - 3].astype(jnp.float32)
+
+        @pl.when(ctx - by >= 0)
+        def _(by=by):
+            far_copy(by, ctx - by).wait_send()
+            far_share(ctx - by).wait_send()
+
+    far_out[...] = far_sum[...].astype(jnp.bfloat16)
+    far_halves().start()
+    end_mark.wait()
+    single = mark_ref[...].astype(jnp.float32)[0:1, BLK - 1 : BLK] == 0.0
+    far_halves().wait_recv()
+    own_ref[mine_half] += jnp.where(single, far_sum[...], 0.0)
+    own_ref[twin_half] += jnp.where(single, far_back[...].astype(jnp.float32), 0.0)
+    far_halves().wait_send()
 
     wide = mine_ref[:BLK].astype(jnp.float32)
     scale = rms_rows(wide)
@@ -1379,7 +1482,15 @@
             pltpu.VMEM((BLK, WIDTH), wide),
             pltpu.VMEM((7, BLK, WIDTH), low),
             pltpu.VMEM((4, 4, 4, 2, 16, 1280), low),
-            pltpu.VMEM((7, BLK, WIDTH), low),
+            pltpu.VMEM((2, BLK, WIDTH), low),
+            pltpu.VMEM((5, 128, WIDTH), low),
+            pltpu.VMEM((5, 128, WIDTH), low),
+            pltpu.VMEM((128, WIDTH), wide),
+            pltpu.VMEM((128, WIDTH), low),
+            pltpu.VMEM((128, WIDTH), low),
+            pltpu.VMEM((16, WIDTH), low),
+            dma((6,)),
+            dma((6,)),
             pltpu.VMEM((8, 288, 1024), low),
             pltpu.VMEM((2016, 1024), low),
             pltpu.VMEM((4, 4, 16, 128), wide),
@@ -1388,7 +1499,7 @@
             dma((7,)),
             dma((15,)),
             dma((15,)),
-            dma((9,)),
+            dma((10,)),
             dma((3, 3, 3)),
             dma((3, 3, 3)),
             dma((4,)),

time: 244 us -> 231 us (0.947)
  Pallas kernels: 240 us -> 229 us
    pallas_call x1, Pallas kernels: 102 us -> 91.6 us  [run_back(): pl.pallas_call(back_kernel, out_shape=[shape((BLK, WIDTH), low), shape((1...]
where the time goes in v6:
time: 231 us; the launch traced here: 230 us
  Pallas kernels  229 us (99%)
    pallas_call x1, Pallas kernels, run_forward(): pl.pallas_call(forward_kernel, out_shape=[shape((BLK, WIDTH), wide), shap...  134 us
    pallas_call x1, Pallas kernels, run_back(): pl.pallas_call(back_kernel, out_shape=[shape((BLK, WIDTH), low), shape((1...  91.6 us

profile of v6, /device:TPU:4, one launch (start us, length us, event | category | flops | bytes accessed | tf_op | source)
XLA Modules:
  0.0 229.6 jit_solution(16835278196875336158)
XLA Ops:
  0.7 133.9 %forward.1 = (f32[256,768]{1,0:T(8,128)}, bf16[256,768]{1,0:T(8,128)(2,1)}, f32[768,256]{1,0:T(8,128)}, f32[16,256]{1,0:T(8,128)}, bf16[6,256,128]{2,1,0:T(8,128...) custom-call(bf16[6,768]{1,0:T(8,128)(2,1)} %wq_ref.1, ...), custom_call_target="tpu_custom_call" | custom-call | tf_op jit(solution)/shard_map/forward/pallas_call | solution.py:750
  134.6 91.6 %back.1 = (bf16[256,768]{1,0:T(8,128)(2,1)}, f32[16,256]{1,0:T(8,128)}, f32[16,128]{1,0:T(8,128)}, f32[256,768]{1,0:T(8,128)}, f32[24,768]{1,0:T(8,128)}, /*inde...) custom-call(bf16[8,272,768]{2,1,0:T(8,128)(2,1)} %get-tuple-element.56.blocks_ref, ...), custom_call_target="tpu_custom_call" | custom-call | tf_op jit(solution)/shard_map/back/pallas_call | solution.py:1446
  226.2 3.2 %finish.1 = (bf16[256,768]{1,0:T(8,128)(2,1)}, f32[256,768]{1,0:T(8,128)}, f32[96,1024]{1,0:T(8,128)}, f32[96,1024]{1,0:T(8,128)}, f32[128,768]{1,0:T(8,128)}, /...) custom-call(bf16[256,768]{1,0:T(8,128)(2,1)} %get-tuple-element.71.o, ...), custom_call_target="tpu_custom_call" | custom-call | tf_op jit(solution)/shard_map/finish/pallas_call | solution.py:1564

commit v7 on v6

--- a/solution.py
+++ b/solution.py
@@ -29,7 +29,7 @@
 
 BLOCK_CUTS = (0, 64, 144, 224, 272)
 PAY_CUTS = (0, 64, 144, 224, 288)
-GRAD_CUTS = (0, 80, 144, 208, 288)
+GRAD_CUTS = (0, 64, 144, 224, 288)
 SPANS = {"all": (0, 4), "p": (1, 3), "h1": (0, 2), "h2": (2, 4), "q1": (0, 1), "p1": (1, 2), "p2": (2, 3), "q2": (3, 4)}
 MESSAGES = (
     (1, (0, 0), "all"), (-1, (0, 0), "all"), (0, (0, 0), "all"),
@@ -169,11 +169,12 @@
     tokens_ref, segments_in, gate_in, up_in, down_in,
     left_ref, right_ref, place_ref, cos_in, sin_in, cos_out, sin_out,
     prev_ref, wres_ref, routes_ref, rank_ref, cot_ref,
-    state_ref, normed_ref, att_ref, lse_ref, q_ref, keys_ref, values_ref,
-    info_ref, proj_ref, blocks_ref, w_ref, small_ref, pay_ref,
-    back_rows_ref, back_grads_ref, d_pay_ref,
+    state_out, normed_out, att_out, lse_ref, q_out, keys_ref, values_ref,
+    info_ref, proj_ref, blocks_out, w_out, small_ref, pay_ref,
+    back_rows_ref, back_grads_ref, d_pay_out,
     part_a, part_b, part_c, own_ref, qt_ref, vt_ref, bias_ref, max_ref, sum_ref, acc_ref,
-    prev_pad, wres_pad, few_wide, few_tall, kv_ref, rows_ref, grads_ref,
+    prev_pad, wres_pad, few_wide, few_tall, kv_ref, rows_ref, grads_ref, blocks_ref, w_ref,
+    state_ref, normed_ref, att_ref, q_ref, d_pay_ref,
     gate_w, up_w, down_w, x_ref, g_ref, gate_ref, up_ref, hidden_ref, d_gate, d_up,
     mine_ref, twin_out, twin_in,
     net_send, net_recv, twin_send, twin_recv, own_sem, ring_send, ring_recv, kv_sem,
@@ -346,6 +347,8 @@
     pass_on(0, 1)
     lax.fori_loop(0, 16, unpack, 0)
     pass_on(0, 2)
+    weights_kept = pltpu.make_async_copy(w_ref, w_out, own_sem.at[9])
+    weights_kept.start()
     across = small_ref[...].astype(jnp.float32).T
     gain_one, gain_two = across[18:19], across[19:20]
 
@@ -446,6 +449,8 @@
         return carry
 
     lax.fori_loop(0, ctx + 1, block, 0)
+    blocks_kept = pltpu.make_async_copy(blocks_ref, blocks_out, own_sem.at[10])
+    blocks_kept.start()
     for head in range(HEADS):
         rows = slice(head * HDIM, head * HDIM + HDIM)
         att_ref[rows] = acc_ref[rows] / sum_ref[head : head + 1]
@@ -503,6 +508,12 @@
 
     other = 1 - core
     half = EXPERTS * SLOTS
+    leaving = [
+        pltpu.make_async_copy(source, target, own_sem.at[11 + number])
+        for number, (source, target) in enumerate(
+            ((state_ref, state_out), (normed_ref, normed_out), (att_ref, att_out), (q_ref, q_out))
+        )
+    ]
 
     def slots(index, on):
         return pl.ds(pl.multiple_of((on * EXPERTS + index) * SLOTS, SLOTS), SLOTS)
@@ -680,6 +691,8 @@
     for owner in range(8):
         for copy in load(owner):
             copy.start()
+    for copy in leaving:
+        copy.start()
     arrive(0)
     for owner in range(8):
         for copy in load(owner):
@@ -723,9 +736,13 @@
         return carry
 
     lax.fori_loop(0, 4, gate_tile, 0)
+    leaving.append(pltpu.make_async_copy(d_pay_ref, d_pay_out, own_sem.at[15]))
+    leaving[-1].start()
     for kind in (0, 1):
         for by in range(1, EXPERTS):
             give_back(kind, by).wait_recv()
+    for copy in [weights_kept, blocks_kept, *leaving]:
+        copy.wait()
     for kind in (0, 1):
         for number in range(len(MESSAGES)):
             ring(kind, number).wait_send()
@@ -768,7 +785,7 @@
             shape((8, 288, 1024), low),
         ],
         in_specs=[vmem] * 26,
-        out_specs=[vmem] * 5 + [anywhere] * 2 + [vmem] * 5 + [anywhere] + [vmem] * 3,
+        out_specs=[anywhere] * 3 + [vmem] + [anywhere] * 3 + [vmem] * 2 + [anywhere] * 2 + [vmem] + [anywhere] + [vmem] * 2 + [anywhere],
         scratch_shapes=[
             *(pltpu.VMEM((4, 4, 4, 2, 16, lanes), low) for lanes in PART_LANES),
             pltpu.VMEM((16, 1280), low),
@@ -785,6 +802,13 @@
             pltpu.VMEM((2, 2, PAIRS, BLK, 128), low),
             pltpu.VMEM((half, WIDTH), low),
             pltpu.VMEM((half, WIDTH), low),
+            pltpu.VMEM((8, BLK + 16, WIDTH), low),
+            pltpu.VMEM((4, WIDTH, WIDTH), low),
+            pltpu.VMEM((BLK, WIDTH), wide),
+            pltpu.VMEM((BLK, WIDTH), low),
+            pltpu.VMEM((WIDTH, BLK), wide),
+            pltpu.VMEM((PAIRS, BLK, 128), low),
+            pltpu.VMEM((8, 288, 1024), low),
             pltpu.VMEM((WIDTH, 1024), low),
             pltpu.VMEM((WIDTH, 1024), low),
             pltpu.VMEM((1024, WIDTH), low),
@@ -802,7 +826,7 @@
             dma((3, 3, 3)),
             dma((3, 10)),
             dma((3, 10)),
-            dma((9,)),
+            dma((16,)),
             dma((2, 15)),
             dma((2, 15)),
             dma((2, 2)),
@@ -834,7 +858,7 @@
 
 
 def back_kernel(
-    blocks_ref, w_ref, small_ref, cos_in, sin_in, cos_out, sin_out, left_ref, right_ref, place_ref,
+    blocks_ref, w_in, small_ref, cos_in, sin_in, cos_out, sin_out, left_ref, right_ref, place_ref,
     prev_ref, wres_ref, routes_ref, cot_ref,
     state_ref, normed_ref, att_ref, lse_ref, q_ref, keys_ref, values_ref, info_ref, proj_ref,
     back_rows_ref, back_grads_ref, d_pay_ref,
@@ -846,7 +870,7 @@
         qt_ref, ot_ref, o_ref, qm_ref, bias_ref, inner_ref, dqt_ref, gain_ref, dk_ref, dv_ref,
         prev_pad, wres_pad, dw_ref, dw_low, few_sum, kv_ref, tok_ref, mine_ref, kv_sem, own_ref, state_grad_ref, others_ref, grads_ref, block_in,
         far_in, far_land, far_sum, far_out, far_back, mark_ref, far_send, far_recv,
-        pay_ref, pay_in, small_in, small_sum,
+        w_ref, pay_ref, pay_in, small_in, small_sum,
         block_send, block_recv, exp_send, exp_recv, load_sem,
         net_send, net_recv, twin_send, twin_recv, small_send, small_recv,
         *more,
@@ -876,7 +900,7 @@
         first, count = rows_of(number)
         landing = sum(rows_of(before)[1] for before in range(number))
         return pltpu.make_async_remote_copy(
-            src_ref=pay_ref.at[
+            src_ref=(d_pay_ref if number >= 7 else pay_ref).at[
                 owner(steps - to, across_it if to else 1 - across_it), pl.ds(first, count)
             ],
             dst_ref=pay_in.at[pl.ds(landing, count)],
@@ -912,11 +936,11 @@
         pltpu.make_async_copy(d_pay_ref.at[index], pay_ref.at[index], load_sem.at[1 + index])
         for index in range(8)
     ]
+    send_experts((13, 14, 11, 12, 7, 8, 9, 10))
     for copy in loads:
         copy.start()
-    for copy in loads:
-        copy.wait()
-    send_experts((13, 14, 11, 12, 7, 8, 9, 10))
+    weights_in = pltpu.make_async_copy(w_in, w_ref, load_sem.at[10])
+    weights_in.start()
     own_block = pltpu.make_async_copy(blocks_ref.at[ctx], mine_ref, load_sem.at[0])
     own_block.start()
 
@@ -1062,6 +1086,7 @@
     state_low = state_grad.astype(jnp.bfloat16)
     attended = att_ref[...]
     dw_low[1] = dot(attended.astype(jnp.bfloat16), state_low).astype(jnp.bfloat16)
+    weights_in.wait()
     att_grad = dot_nt(state_low, w_ref[3])
     blank = jnp.zeros((HDIM, BLK), jnp.bfloat16)
     low_half = lax.broadcasted_iota(jnp.int32, (BLK, 128), 1) < HDIM
@@ -1167,8 +1192,8 @@
 
         for when, came, then in (
             (0, (13, 14), (5, 6)),
-            (1, (3, 4), (2,)),
-            (2, (7, 8, 9, 10, 5, 6), (0, 1)),
+            (2, (3, 4), (2,)),
+            (4, (7, 8, 9, 10, 5, 6), (0, 1)),
         ):
 
             @pl.when(index == jnp.minimum(ctx, when))
@@ -1178,6 +1203,8 @@
 
         return carry
 
+    for copy in loads:
+        copy.wait()
     add_experts((11, 12))
     send_experts((3, 4))
     lax.fori_loop(0, ctx + 1, block, 0)
@@ -1456,7 +1483,7 @@
             shape((96, 1024), wide),
             shape((128, WIDTH), wide),
         ],
-        in_specs=[anywhere] + [vmem] * 18 + [anywhere] * 2 + [vmem] * 4 + [anywhere],
+        in_specs=[anywhere] * 2 + [vmem] * 17 + [anywhere] * 2 + [vmem] * 4 + [anywhere],
         out_specs=[vmem] * 9,
         scratch_shapes=[
             pltpu.VMEM((HEADS, 128, BLK), low),
@@ -1491,6 +1518,7 @@
             pltpu.VMEM((16, WIDTH), low),
             dma((6,)),
             dma((6,)),
+            pltpu.VMEM((4, WIDTH, WIDTH), low),
             pltpu.VMEM((8, 288, 1024), low),
             pltpu.VMEM((2016, 1024), low),
             pltpu.VMEM((4, 4, 16, 128), wide),
@@ -1499,7 +1527,7 @@
             dma((7,)),
             dma((15,)),
             dma((15,)),
-            dma((10,)),
+            dma((11,)),
             dma((3, 3, 3)),
             dma((3, 3, 3)),
             dma((4,)),

time: 231 us -> 225 us (0.974)
  Pallas kernels: 229 us -> 223 us
    pallas_call x1, Pallas kernels: 134 us -> 129 us  [run_forward(): pl.pallas_call(forward_kernel, out_shape=[shape((BLK, WIDTH), wide), shap...]
where the time goes in v7:
time: 225 us; the launch traced here: 224 us
  Pallas kernels  223 us (99%)
    pallas_call x1, Pallas kernels, run_forward(): pl.pallas_call(forward_kernel, out_shape=[shape((BLK, WIDTH), wide), shap...  129 us
    pallas_call x1, Pallas kernels, run_back(): pl.pallas_call(back_kernel, out_shape=[shape((BLK, WIDTH), low), shape((1...  90.2 us

profile of v7, /device:TPU:4, one launch (start us, length us, event | category | flops | bytes accessed | tf_op | source)
XLA Modules:
  0.0 223.5 jit_solution(11478164038475127409)
XLA Ops:
  0.7 129.3 %forward.1 = (f32[256,768]{1,0:T(8,128)}, bf16[256,768]{1,0:T(8,128)(2,1)}, f32[768,256]{1,0:T(8,128)}, f32[16,256]{1,0:T(8,128)}, bf16[6,256,128]{2,1,0:T(8,128...) custom-call(bf16[6,768]{1,0:T(8,128)(2,1)} %wq_ref.1, ...), custom_call_target="tpu_custom_call" | custom-call | tf_op jit(solution)/shard_map/forward/pallas_call | solution.py:767
  129.9 90.2 %back.1 = (bf16[256,768]{1,0:T(8,128)(2,1)}, f32[16,256]{1,0:T(8,128)}, f32[16,128]{1,0:T(8,128)}, f32[256,768]{1,0:T(8,128)}, f32[24,768]{1,0:T(8,128)}, /*inde...) custom-call(bf16[8,272,768]{2,1,0:T(8,128)(2,1)} %get-tuple-element.56.blocks_ref, ...), custom_call_target="tpu_custom_call" | custom-call | tf_op jit(solution)/shard_map/back/pallas_call | solution.py:1473
  220.1 3.2 %finish.1 = (bf16[256,768]{1,0:T(8,128)(2,1)}, f32[256,768]{1,0:T(8,128)}, f32[96,1024]{1,0:T(8,128)}, f32[96,1024]{1,0:T(8,128)}, f32[128,768]{1,0:T(8,128)}, /...) custom-call(bf16[256,768]{1,0:T(8,128)(2,1)} %get-tuple-element.71.o, ...), custom_call_target="tpu_custom_call" | custom-call | tf_op jit(solution)/shard_map/finish/pallas_call | solution.py:1592

commit v8 on v7

--- a/solution.py
+++ b/solution.py
@@ -687,9 +687,15 @@
             for number, (source, target) in enumerate(parts)
         ]
 
+    def owner_at(steps, on):
+        return ((along + steps + 4) % 4) * 2 + on
+
+    for steps, on in ((0, side), (0, 1 - side), (-1, side), (1, side)):
+        for copy in load(owner_at(steps, on)):
+            copy.start()
     pass_on(1, 4)
-    for owner in range(8):
-        for copy in load(owner):
+    for steps, on in ((-1, 1 - side), (1, 1 - side), (2, side), (2, 1 - side)):
+        for copy in load(owner_at(steps, on)):
             copy.start()
     for copy in leaving:
         copy.start()
@@ -1284,6 +1290,9 @@
     copy.start()
     started.append(copy)
 
+    def lanes_of(part):
+        return pl.ds(PART_START[part], PART_LANES[part])
+
     for x in range(4):
         share(x).wait_recv()
 
@@ -1296,8 +1305,10 @@
 
         lax.fori_loop(0, 16, add_pair, 0, unroll=2)
 
-    def lanes_of(part):
-        return pl.ds(PART_START[part], PART_LANES[part])
+        @pl.when(spot[0] != x)
+        def _(x=x):
+            by = (x - spot[0] + 4) % 4
+            net(1, 0, by, grads_ref.at[x, :, :, core, :, lanes_of(1)], in_one[1].at[by - 1]).start()
 
     for part in range(3):
         axis = PART_ORDER[part][2]
@@ -1307,7 +1318,8 @@
             copy = net(
                 part, 0, by, grads_ref.at[(*index, core, slice(None), lanes_of(part))], in_one[part].at[by - 1]
             )
-            copy.start()
+            if part != 1:
+                copy.start()
             started.append(copy)
 
     small(3, 1, small_sum.at[3], 1 - core).wait_recv()

time: 225 us -> 225 us (level)
  no operation moved by 1% of the time
where the time goes in v8:
time: 225 us; the launch traced here: 224 us
  Pallas kernels  223 us (99%)
    pallas_call x1, Pallas kernels, run_forward(): pl.pallas_call(forward_kernel, out_shape=[shape((BLK, WIDTH), wide), shap...  129 us
    pallas_call x1, Pallas kernels, run_back(): pl.pallas_call(back_kernel, out_shape=[shape((BLK, WIDTH), low), shape((1...  90.2 us

profile of v8, /device:TPU:4, one launch (start us, length us, event | category | flops | bytes accessed | tf_op | source)
XLA Modules:
  0.0 223.5 jit_solution(14082172306938117033)
XLA Ops:
  0.7 129.3 %forward.1 = (f32[256,768]{1,0:T(8,128)}, bf16[256,768]{1,0:T(8,128)(2,1)}, f32[768,256]{1,0:T(8,128)}, f32[16,256]{1,0:T(8,128)}, bf16[6,256,128]{2,1,0:T(8,128...) custom-call(bf16[6,768]{1,0:T(8,128)(2,1)} %wq_ref.1, ...), custom_call_target="tpu_custom_call" | custom-call | tf_op jit(solution)/shard_map/forward/pallas_call | solution.py:773
  129.9 90.2 %back.1 = (bf16[256,768]{1,0:T(8,128)(2,1)}, f32[16,256]{1,0:T(8,128)}, f32[16,128]{1,0:T(8,128)}, f32[256,768]{1,0:T(8,128)}, f32[24,768]{1,0:T(8,128)}, /*inde...) custom-call(bf16[8,272,768]{2,1,0:T(8,128)(2,1)} %get-tuple-element.56.blocks_ref, ...), custom_call_target="tpu_custom_call" | custom-call | tf_op jit(solution)/shard_map/back/pallas_call | solution.py:1485
  220.1 3.2 %finish.1 = (bf16[256,768]{1,0:T(8,128)(2,1)}, f32[256,768]{1,0:T(8,128)}, f32[96,1024]{1,0:T(8,128)}, f32[96,1024]{1,0:T(8,128)}, f32[128,768]{1,0:T(8,128)}, /...) custom-call(bf16[256,768]{1,0:T(8,128)(2,1)} %get-tuple-element.71.o, ...), custom_call_target="tpu_custom_call" | custom-call | tf_op jit(solution)/shard_map/finish/pallas_call | solution.py:1604
